TPU v7x, 32 devices: a whole 2x2x4 slice. The times are simulated.
32 devices in a mesh: grp: 2 (over y), head: 4 (over z), tm: 4 (over x, core).
Axes of the slice: x: 2, y: 2, z: 4, core: 2. Of those that a mesh axis runs over, the one named last changes fastest.
Arguments:
- query_rows: bfloat16 [32, 64, 3072], P(('grp', 'tm'), 'head'), parts along dimension 0, may hold values from -180 to 180
- key_rows: bfloat16 [32, 64, 3072], P(('grp', 'tm'), 'head'), parts along dimension 0, may hold values from -6 to 6
- value_rows: bfloat16 [32, 64, 3072], P(('grp', 'tm'), 'head'), parts along dimension 0, may hold values from -6 to 6
- pair_list: int32 [32, 32], P('grp'), parts along dimension 0, may hold values from 0 to 15, as said below
- block_tokens: int32 [32], P('grp'), parts along dimension 0, may hold values from 1 to 64, 768 in all
Outputs:
- attended: bfloat16 [32, 64, 3072], P(('grp', 'tm'), 'head'), parts along dimension 0
There are 2 independent parts, one for each index of `grp`. A program takes and returns all parts, laid end to end along the dimension named above; each array names one. Nothing has to cross between parts.
Inputs may be any that keep to these rules, and one draw needn't show every extreme that they name: `pair_list`: row q names q in column 0 and q xor 1 in column 1; a block may be named twice in a row. The query blocks of one time shard name at most 2 different blocks of a time shard beside it and at most 1 of a time shard two or more away; both bounds are reached.
All inputs are finite; a program needn't handle non-finite values.
Results may differ from a plain program's by a relative error of at most 0.0012.
The roundings to bfloat16 on the way count: a program that leaves them out, or rounds other values in their place, can miss the bound.
Values may be sent and summed in bfloat16 or wider, within the bound.
No kernel may reach another device: no remote copies, remote signals or barrier semaphores. Data moves between devices by JAX's collectives and lax.ppermute only.
A program may use at most 128 MiB of HBM per device.

v0:
```python
import functools
import math

import jax
import jax.numpy as jnp
from jax import lax
from jax.experimental import pallas as pl
from jax.experimental.pallas import tpu as pltpu
from jax.sharding import PartitionSpec as P

HD = 128
BLK = 64
NEAR_CAP = 2
FAR_CAP = 1
NEG = -1e30
ROTATE_SCALE = 1.0 / math.sqrt(HD)
SCORE_SCALE = 1.0 / math.sqrt(HD)
VMEM = 24 * 1024 * 1024
WIDE_VMEM = 60 * 1024 * 1024
TOKEN = jax.ShapeDtypeStruct((8, 128), jnp.float32)
NO_COST = pl.CostEstimate(flops=0, bytes_accessed=0, transcendentals=0)
HIGH_COST = pl.CostEstimate(flops=10**11, bytes_accessed=0, transcendentals=0)
LOG2E = math.log2(math.e)


def sign_matrix():
    common = lax.broadcasted_iota(jnp.int32, (HD, HD), 0) & lax.broadcasted_iota(
        jnp.int32, (HD, HD), 1
    )
    bits = HD.bit_length() - 1
    parity = common
    for bit in range(1, bits):
        parity = parity ^ (common >> bit)
    return jnp.where((parity & 1) == 0, 1.0, -1.0).astype(jnp.bfloat16)


def rows_of(block):
    rows, width = math.prod(block.shape[:-1]), block.shape[-1]
    if block.shape[-2] % 16 == 0:
        return block.reshape(rows, width)
    return block.astype(jnp.float32).reshape(rows, width).astype(block.dtype)


def fields_of(message):
    at, fields = 0, []
    for source, start, size in message:
        fields.append((source, start, size, at))
        at += size
    return fields, at


def by_distance(refs, count, direction):
    if len(refs[0].shape) == 3:
        return list(refs)
    me = lax.axis_index("head")
    return [refs[0].at[lax.rem(me + direction * s + count, count)] for s in range(count)]


def rotated(block, sign):
    blocks, tokens, size = block.shape
    flat = rows_of(block)
    heads = [flat[:, at : at + HD] for at in range(0, size, HD)]
    turned = jnp.dot(jnp.concatenate(heads, axis=0), sign, preferred_element_type=jnp.float32)
    return (turned * ROTATE_SCALE).reshape(size // HD, blocks, tokens, HD).astype(jnp.bfloat16)


def store_heads(out, start, turned):
    for h in range(turned.shape[0]):
        at = start + h * HD
        out[:, :, at : at + HD] = turned[h]


def rotate_kernel(message, sources, count_head, *refs):
    fields, total = fields_of(message)
    ins = dict(zip(sources, refs))
    outs, (token, buffer, sems) = refs[len(sources) : -3], refs[-3:]
    token[...] = jnp.zeros_like(token)
    width_here = refs[0].shape[2] // count_head
    me = lax.axis_index("head")
    order = list(range(1, count_head)) + [0]
    copies = {}
    for s in order:
        goal = lax.rem(me + s, count_head)
        for f, (source, start, size, at) in enumerate(fields):
            column = pl.multiple_of(goal * width_here + start, HD)
            copies[s, f] = pltpu.make_async_copy(
                ins[source].at[:, :, pl.ds(column, size)],
                buffer.at[s, :, :, pl.ds(at, size)],
                sems.at[s, f],
            )
            copies[s, f].start()
    sign = sign_matrix()
    for s in order:
        for f, (_, _, size, start) in enumerate(fields):
            copies[s, f].wait()
            store_heads(outs[s], start, rotated(buffer[s, :, :, start : start + size], sign))


def rotate_here(fields, ins, outs, distances, count_head, sign):
    width_here = next(iter(ins.values())).shape[2] // count_head
    me = lax.axis_index("head")
    for s in distances:
        goal = lax.rem(me + s, count_head)
        for source, start, size, at in fields:
            column = pl.multiple_of(goal * width_here + start, HD)
            store_heads(outs[s], at, rotated(ins[source][:, :, pl.ds(column, size)], sign))


def rotate_pieces(arrays, message, count_head):
    blocks, tokens, _ = arrays[0].shape
    fields, total = fields_of(message)
    sources = sorted({source for source, _, _ in message})
    one = (blocks, tokens, total)
    *pieces, token = pl.pallas_call(
        functools.partial(rotate_kernel, message, sources, count_head),
        in_specs=[pl.BlockSpec(memory_space=pltpu.HBM)] * len(sources),
        out_specs=[pl.BlockSpec(memory_space=pltpu.VMEM)] * (count_head + 1),
        out_shape=[jax.ShapeDtypeStruct(one, jnp.bfloat16)] * count_head + [TOKEN],
        scratch_shapes=[
            pltpu.VMEM((count_head,) + one, jnp.bfloat16),
            pltpu.SemaphoreType.DMA((count_head, len(fields))),
        ],
        cost_estimate=NO_COST,
        compiler_params=pltpu.CompilerParams(vmem_limit_bytes=WIDE_VMEM),
    )(*[arrays[source] for source in sources])
    return pieces, token


def slots_at(distance, count_tm):
    return NEAR_CAP if distance in (1, count_tm - 1) else FAR_CAP


def pick_kernel(count_head, count_tm, lanes, picks_ref, *refs):
    pieces, outs = refs[:count_head], refs[count_head + 1 : count_head + count_tm]
    shard = lax.axis_index("tm")
    for distance, out in enumerate(outs, 1):
        goal = lax.rem(shard + distance, count_tm)
        for k in range(slots_at(distance, count_tm)):
            pick = picks_ref[NEAR_CAP * goal + k]
            for s in range(count_head):
                out[k, s] = pieces[s][pick, :, lanes[0] : lanes[1]]


def pick_blocks(picks, pieces, lanes, count_tm, held, passes):
    count_head = len(pieces)
    one = (count_head, pieces[0].shape[1], lanes[1] - lanes[0])
    vmem, anywhere = pl.BlockSpec(memory_space=pltpu.VMEM), pl.BlockSpec(memory_space=pl.ANY)
    shapes = [
        jax.ShapeDtypeStruct((slots_at(distance, count_tm),) + one, jnp.bfloat16)
        for distance in range(1, count_tm)
    ]
    passed = [jax.ShapeDtypeStruct(held.shape, held.dtype)] if passes else []
    return pl.pallas_call(
        functools.partial(pick_kernel, count_head, count_tm, lanes),
        in_specs=[pl.BlockSpec(memory_space=pltpu.SMEM)] + [vmem] * count_head + [anywhere],
        out_specs=[vmem] * len(shapes) + [anywhere] * len(passed),
        out_shape=shapes + passed,
        input_output_aliases={1 + count_head: len(shapes)} if passes else {},
        cost_estimate=HIGH_COST,
        compiler_params=pltpu.CompilerParams(vmem_limit_bytes=VMEM),
    )(picks, *pieces, held)


def remote_rows(count_tm):
    return [
        (distance, k)
        for distance in range(1, count_tm)
        for k in range(slots_at(distance, count_tm))
    ]


def split(value, by):
    if by & (by - 1) == 0:
        return value >> (by.bit_length() - 1), value & (by - 1)
    return lax.div(value, by), lax.rem(value, by)


def plan_kernel(messages, count_head, count_tm, blocks, *refs):
    *sources, pair_hbm, tokens_ref, _ = refs[:6]
    picks_ref, bias_ref, query_out = refs[6:9]
    pair_ref, named_ref, table_ref, pair_sem, table_sem = refs[-5:]
    outs = refs[9:-5]
    ins = dict(enumerate(sources))
    pair_copy = pltpu.make_async_copy(pair_hbm, pair_ref, pair_sem)
    pair_copy.start()
    sign = sign_matrix()
    places = list(range(1, count_head)) + [0]
    jobs = [
        (fields_of(message)[0], outs[m * count_head : (m + 1) * count_head], s)
        for m, message in enumerate(messages)
        for s in places
    ]
    query_fields = [(0, 0, query_out.shape[-1], 0)]
    jobs += [(query_fields, by_distance([query_out], count_head, 1), s) for s in places]
    half = len(jobs) // 2
    for fields, pieces, s in jobs[:half]:
        rotate_here(fields, ins, pieces, [s], count_head, sign)
    pair_copy.wait()
    total_blocks, columns = pair_ref.shape
    pairs = pair_ref[...]
    lane = lax.broadcasted_iota(jnp.int32, named_ref.shape, 1)
    named = jnp.zeros(named_ref.shape, jnp.int32)
    for c in range(columns):
        named = jnp.where(pairs[:, c : c + 1] == lane, 1, named)
    named_ref[...] = named
    copy = pltpu.make_async_copy(named_ref, table_ref, table_sem)
    copy.start()
    for fields, pieces, s in jobs[half:]:
        rotate_here(fields, ins, pieces, [s], count_head, sign)
    copy.wait()
    shard = lax.axis_index("tm")
    place = lax.axis_index("head")
    mine = shard * blocks

    def two_picks(wanted):
        picks = [jnp.int32(0)] * NEAR_CAP
        count = jnp.int32(0)
        for j in range(blocks):
            for k in range(NEAR_CAP):
                picks[k] = jnp.where((wanted[j] > 0) & (count == k), j, picks[k])
            count = count + wanted[j]
        return picks, count

    def named_by(rows, column):
        found = table_ref[rows, column]
        for i in range(1, blocks):
            found = found | table_ref[rows + i, column]
        return found

    for d in range(count_tm):
        picks, _ = two_picks([named_by(d * blocks, mine + j) for j in range(blocks)])
        for k in range(NEAR_CAP):
            picks_ref[NEAR_CAP * d + k] = picks[k]

    kept = [[table_ref[mine + i, mine + j] * tokens_ref[mine + j] for j in range(blocks)] for i in range(blocks)]
    arrivals = {}
    for distance, k in remote_rows(count_tm):
        first = lax.rem(shard - distance + count_tm, count_tm) * blocks
        if k == 0:
            arrivals[distance] = two_picks([named_by(mine, first + j) for j in range(blocks)])
        picks, count = arrivals[distance]
        there = first + picks[k]
        live = jnp.where(count > k, tokens_ref[there], 0)
        for i in range(blocks):
            kept[i].append(table_ref[mine + i, there] * live)

    total = bias_ref.shape[1]
    piece_rows = BLK // count_head
    at = lax.broadcasted_iota(jnp.int32, (blocks, total), 1)
    query = lax.broadcasted_iota(jnp.int32, (blocks, total), 0)
    own = at < blocks * BLK
    group, token = split(at, piece_rows)
    own_piece, own_block = split(group, blocks)
    far_row, far_group = split(group, count_head)
    row = jnp.where(own, own_block, far_row)
    piece = jnp.where(own, own_piece, far_group)
    source = jnp.where(piece > place, place - piece + count_head, place - piece)
    position = source * piece_rows + token
    limit = jnp.zeros((blocks, total), jnp.int32)
    for r in range(len(kept[0])):
        value = jnp.zeros((blocks, total), jnp.int32)
        for i in range(blocks):
            value = jnp.where(query == i, kept[i][r], value)
        limit = jnp.where(row == r, value, limit)
    bias_ref[...] = jnp.where(position < limit, 0.0, NEG)


def plan(arrays, messages, pair_list, block_tokens, after, count_head, count_tm):
    blocks, tokens, _ = arrays[0].shape
    total_blocks, columns = pair_list.shape
    lanes = -(-total_blocks // 128) * 128
    total = (blocks + len(remote_rows(count_tm))) * BLK
    vmem = pl.BlockSpec(memory_space=pltpu.VMEM)
    smem = pl.BlockSpec(memory_space=pltpu.SMEM)
    stacked = (count_head, blocks, tokens, arrays[0].shape[2] // count_head)
    shapes = [jax.ShapeDtypeStruct(stacked, jnp.bfloat16)] + [
        jax.ShapeDtypeStruct((blocks, tokens, fields_of(message)[1]), jnp.bfloat16)
        for message in messages
        for _ in range(count_head)
    ]
    picks, bias, query, *pieces = pl.pallas_call(
        functools.partial(plan_kernel, messages, count_head, count_tm, blocks),
        in_specs=[vmem] * 3
        + [pl.BlockSpec(memory_space=pl.ANY), smem, pl.BlockSpec(memory_space=pl.ANY)],
        out_specs=[smem, vmem] + [vmem] * len(shapes),
        out_shape=[
            jax.ShapeDtypeStruct((NEAR_CAP * count_tm,), jnp.int32),
            jax.ShapeDtypeStruct((blocks, total), jnp.float32),
        ]
        + shapes,
        scratch_shapes=[
            pltpu.VMEM((total_blocks, columns), jnp.int32),
            pltpu.VMEM((total_blocks, lanes), jnp.int32),
            pltpu.SMEM((total_blocks, lanes), jnp.int32),
            pltpu.SemaphoreType.DMA,
            pltpu.SemaphoreType.DMA,
        ],
        cost_estimate=NO_COST,
        compiler_params=pltpu.CompilerParams(vmem_limit_bytes=VMEM),
    )(*arrays, pair_list, block_tokens, after)
    return picks, bias, query, [pieces[at : at + count_head] for at in range(0, len(pieces), count_head)]


def attend_kernel(counts, heads_of, distances, tokens_ref, bias_ref, query_ref, *refs):
    count_head, count_tm = counts
    queries = by_distance([query_ref], count_head, -1)
    per_part = count_head + count_tm - 1
    parts = [refs[p * per_part : (p + 1) * per_part] for p in range(len(heads_of))]
    outs = refs[len(heads_of) * per_part :][-len(distances) :]
    blocks, tokens, _ = outs[0].shape
    rows = len(distances) * tokens
    shard = lax.axis_index("tm")
    me = lax.axis_index("head")
    bias = bias_ref[...][:, None, :]
    place_of = [(p, h) for p, (_, size) in enumerate(heads_of) for h in range(size // HD)]

    def gathered(kind, head):
        p, h = place_of[head]
        first = kind * heads_of[p][1] + h * HD
        lanes = slice(first, first + HD)
        pieces = [rows_of(own[:, :, lanes]) for own in parts[p][:count_head]]
        pieces += [
            rows_of(parts[p][count_head + distance - 1][k, :, :, lanes])
            for distance, k in remote_rows(count_tm)
        ]
        return jnp.concatenate(pieces, axis=0)

    def products(head):
        first = heads_of[0][0] + head * HD
        lanes = slice(first, first + HD)
        query = jnp.concatenate(
            [rows_of(queries[s][i, :, lanes]) for i in range(blocks) for s in distances], axis=0
        )
        return lax.dot_general(
            query, gathered(0, head), (((1,), (1,)), ((), ())), preferred_element_type=jnp.float32
        )

    heads = len(place_of)
    dots, mixed = products(0), []
    for h in range(heads):
        ahead = products(h + 1) if h + 1 < heads else None
        dots = dots.reshape(blocks, rows, -1) + bias
        peak = jnp.max(dots, axis=-1, keepdims=True)
        weights = jnp.exp2((dots - peak) * (SCORE_SCALE * LOG2E))
        inverse = 1.0 / jnp.sum(weights, axis=-1, keepdims=True)
        weights_half = weights.astype(jnp.bfloat16).reshape(blocks * rows, -1)
        part = jnp.dot(weights_half, gathered(1, h), preferred_element_type=jnp.float32)
        mixed.append(part * inverse.reshape(blocks * rows, 1))
        dots = ahead
    mixed = jnp.concatenate(mixed, axis=0)
    sign = sign_matrix()
    high = mixed.astype(jnp.bfloat16)
    low = (mixed - high.astype(jnp.float32)).astype(jnp.bfloat16)
    turned = jnp.dot(high, sign, preferred_element_type=jnp.float32)
    turned = turned + jnp.dot(low, sign, preferred_element_type=jnp.float32)
    turned = (turned * ROTATE_SCALE).reshape(heads, blocks, len(distances), tokens, HD)
    token = lax.broadcasted_iota(jnp.int32, (tokens, HD), 0)
    for at, s in enumerate(distances):
        position = lax.rem(me - s + count_head, count_head) * tokens + token
        for i in range(blocks):
            live = position < tokens_ref[shard * blocks + i]
            for h in range(heads):
                outs[at][i, :, h * HD : (h + 1) * HD] = jnp.where(
                    live, turned[h, i, at], 0.0
                ).astype(jnp.bfloat16)


def attend(block_tokens, bias, query, parts, heads_of, distances, after=(), cost=NO_COST):
    count_head, count_tm = query.shape[0], len(parts[0][1]) + 1
    operands = [ref for owns, slots in parts for ref in owns + slots]
    shape = query.shape[1:3] + (sum(size for _, size in heads_of),)
    vmem = pl.BlockSpec(memory_space=pltpu.VMEM)
    return pl.pallas_call(
        functools.partial(attend_kernel, (count_head, count_tm), heads_of, distances),
        in_specs=[pl.BlockSpec(memory_space=pltpu.SMEM)]
        + [vmem] * (2 + len(operands))
        + [pl.BlockSpec(memory_space=pl.ANY)] * len(after),
        out_specs=[vmem] * len(distances),
        out_shape=[jax.ShapeDtypeStruct(shape, jnp.bfloat16)] * len(distances),
        cost_estimate=cost,
        compiler_params=pltpu.CompilerParams(vmem_limit_bytes=VMEM),
    )(block_tokens, bias, query, *operands, *after)


def place_kernel(places, width_here, *refs):
    pieces, out_ref, sems = refs[:-2], refs[-2], refs[-1]
    me, count = lax.axis_index("head"), lax.axis_size("head")
    copies = []
    for at, (piece, (s, start)) in enumerate(zip(pieces, places)):
        column = pl.multiple_of(lax.rem(me + s, count) * width_here + start, HD)
        copies.append(
            pltpu.make_async_copy(
                piece, out_ref.at[:, :, pl.ds(column, piece.shape[-1])], sems.at[at]
            )
        )
        copies[-1].start()
    for copy in copies:
        copy.wait()


def place_pieces(pieces, places, width_here):
    blocks, tokens, _ = pieces[0].shape
    width = width_here * lax.axis_size("head")
    return pl.pallas_call(
        functools.partial(place_kernel, places, width_here),
        in_specs=[pl.BlockSpec(memory_space=pl.ANY)] * len(pieces),
        out_specs=pl.BlockSpec(memory_space=pltpu.HBM),
        out_shape=jax.ShapeDtypeStruct((blocks, tokens, width), jnp.bfloat16),
        scratch_shapes=[pltpu.SemaphoreType.DMA((len(pieces),))],
        compiler_params=pltpu.CompilerParams(vmem_limit_bytes=VMEM),
    )(*pieces)


def shifted(array, axis, distance):
    count = lax.axis_size(axis)
    return lax.ppermute(array, axis, [(i, (i + distance) % count) for i in range(count)])


def exchange(pieces, direction):
    return [shifted(piece, "head", direction * s) for s, piece in enumerate(pieces, 1)]


def forward(sent):
    return [shifted(block, "tm", distance) for distance, block in enumerate(sent, 1)]


def shards(query_rows, key_rows, value_rows, pair_list, block_tokens):
    count_head = lax.axis_size("head")
    count_tm = lax.axis_size("tm")
    blocks, tokens, width = query_rows.shape
    width_here = width // count_head
    heads = width_here // HD
    cut = (heads + 1) // 2 * HD
    parts = [(0, cut), (cut, width_here - cut)] if heads > 1 else [(0, width_here)]
    arrays = [query_rows, key_rows, value_rows]
    messages = [[(1,) + part, (2,) + part] for part in parts]
    pieces, token = rotate_pieces(arrays, messages[0], count_head)
    picks, bias, query, later = plan(
        arrays, messages[1:], pair_list, block_tokens, token, count_head, count_tm
    )
    received = [piece[:1] + exchange(piece[1:], 1) for piece in [pieces] + later]
    sent = []
    for owns, (_, size) in zip(received, parts):
        held = sent[-1][0] if sent else query
        picked = pick_blocks(picks, owns, (0, 2 * size), count_tm, held, not sent)
        if not sent:
            *picked, query = picked
        sent.append(list(picked))
    query = lax.all_to_all(query, "head", split_axis=0, concat_axis=0, tiled=True)
    inputs = [(owns, forward(picked)) for owns, picked in zip(received, sent)]
    distances, after = list(range(1, count_head)), ()
    pieces, places = [], []
    for at, part in enumerate(parts):
        cost = NO_COST if at == len(parts) - 1 else HIGH_COST
        leaving = attend(
            block_tokens, bias, query, [inputs[at]], [part], distances, after, cost
        )
        after = (leaving[0],)
        pieces += exchange(leaving, -1)
        places += [(s, part[0]) for s in distances]
    pieces += attend(block_tokens, bias, query, inputs, parts, [0], after)
    return place_pieces(pieces, places + [(0, 0)], width_here)


def solution(mesh):
    placed = (
        P(("grp", "tm"), "head", None),
        P(("grp", "tm"), "head", None),
        P(("grp", "tm"), "head", None),
        P("grp", None),
        P("grp"),
    )
    return jax.shard_map(
        shards,
        mesh=mesh,
        in_specs=placed,
        out_specs=P(("grp", "tm"), "head", None),
        check_vma=False,
    )
```

profile of v0, /device:TPU:0, one launch (start us, length us, event | category | flops | bytes accessed | tf_op | source)
XLA Modules:
  0.0 50.0 jit_solution(16895061474182599552)
XLA Ops:
  0.0 0.0 copy-start.1
  0.0 0.0 copy-start
  0.0 2.9 %shard_map.55 = (bf16[4,16,768]{2,1,0:T(8,128)(2,1)}, bf16[4,16,768]{2,1,0:T(8,128)(2,1)}, bf16[4,16,768]{2,1,0:T(8,128)(2,1)}, bf16[4,16,768]{2,1,0:T(8,128)(2,1)}, f32[8,128]{1,0:T(8,128)}) custom-call(bf16[4,16,3072]{2,1,0:T(8,128)(2,1)} %refs_1_.3, bf16[4,16,3072]{2,1,0:T(8,128)(2,1)} %refs_2_.1), custom_call_target="tpu_custom_call" | custom-call | tf_op jit(solution)/shard_map/pallas_call | solution.py:114
  2.9 0.0 copy-start.7
  2.9 3.1 %collective-permute-start = (bf16[4,16,768]{2,1,0:T(8,128)(2,1)}, bf16[4,16,768]{2,1,0:T(8,128)(2,1)S(1)}, u32[]{:S(2)}, u32[]{:S(2)}) collective-permute-start(bf16[4,16,768]{2,1,0:T(8,128)(2,1)} %get-tuple-element.34), channel_id=1, source_target_pairs={{0,4},{4,8},{8,12},{12,0},{1,5},{5,9},{9,13},{13,1},{2,6},{6,10},{... | collective-permute-start | bytes 294920 | tf_op jit(solution)/shard_map/ppermute | solution.py:416
  6.0 2.6 %collective-permute-start.1 = (bf16[4,16,768]{2,1,0:T(8,128)(2,1)}, bf16[4,16,768]{2,1,0:T(8,128)(2,1)S(1)}, u32[]{:S(2)}, u32[]{:S(2)}) collective-permute-start(bf16[4,16,768]{2,1,0:T(8,128)(2,1)} %get-tuple-element.35), channel_id=1, source_target_pairs={{0,8},{4,12},{8,0},{12,4},{1,9},{5,13},{9,1},{13,5},{2,10},{6,14},... | collective-permute-start | bytes 294920 | tf_op jit(solution)/shard_map/ppermute | solution.py:416
  8.5 0.0 copy-start.5
  8.5 1.3 %collective-permute-start.2 = (bf16[4,16,768]{2,1,0:T(8,128)(2,1)}, bf16[4,16,768]{2,1,0:T(8,128)(2,1)S(1)}, u32[]{:S(2)}, u32[]{:S(2)}) collective-permute-start(bf16[4,16,768]{2,1,0:T(8,128)(2,1)} %get-tuple-element.36), channel_id=1, source_target_pairs={{0,12},{4,0},{8,4},{12,8},{1,13},{5,1},{9,5},{13,9},{2,14},{6,2},{... | collective-permute-start | bytes 294920 | tf_op jit(solution)/shard_map/ppermute | solution.py:416
  9.9 0.0 copy-done.1
  9.9 0.0 copy-done
  9.9 0.0 copy-done.7
  9.9 0.0 copy-done.5
  9.9 0.0 copy-start.2
  9.9 1.0 %copy-done.2 = bf16[4,16,3072]{2,1,0:T(8,128)(2,1)S(1)} copy-done((bf16[4,16,3072]{2,1,0:T(8,128)(2,1)S(1)}, bf16[4,16,3072]{2,1,0:T(8,128)(2,1)}, u32[]{:S(2)}) %copy-start.2) | copy-done | bytes 393240
  10.9 0.0 copy-start.4
  10.9 0.7 %copy-done.4 = s32[16,32]{1,0:T(8,128)S(1)} copy-done((s32[16,32]{1,0:T(8,128)S(1)}, s32[16,32]{1,0:T(8,128)}, u32[]{:S(2)}) %copy-start.4) | copy-done | bytes 2072
  11.6 0.0 copy-start.3
  11.6 2.8 %shard_map.56 = (s32[8]{0:T(128)S(1)}, f32[4,576]{1,0:T(4,128)S(1)}, bf16[4,4,16,768]{3,2,1,0:T(8,128)(2,1)}, bf16[4,16,768]{2,1,0:T(8,128)(2,1)S(1)}, bf16[4,16...) custom-call(bf16[4,16,3072]{2,1,0:T(8,128)(2,1)S(1)} %copy-done.2, ...), custom_call_target="tpu_custom_call" | custom-call | tf_op jit(solution)/shard_map/pallas_call | solution.py:281
  14.4 0.7 %collective-permute-start.9 = (bf16[4,16,768]{2,1,0:T(8,128)(2,1)S(1)}, bf16[4,16,768]{2,1,0:T(8,128)(2,1)S(1)}, u32[]{:S(2)}, u32[]{:S(2)}) collective-permute-start(bf16[4,16,768]{2,1,0:T(8,128)(2,1)S(1)} %get-tuple-element.46), channel_id=1, source_target_pairs={{0,4},{4,8},{8,12},{12,0},{1,5},{5,9},{9,13},{13,1},{2,6},{6,10},{... | collective-permute-start | bytes 294920 | tf_op jit(solution)/shard_map/ppermute | solution.py:416
  15.1 0.5 %collective-permute-start.10 = (bf16[4,16,768]{2,1,0:T(8,128)(2,1)S(1)}, bf16[4,16,768]{2,1,0:T(8,128)(2,1)S(1)}, u32[]{:S(2)}, u32[]{:S(2)}) collective-permute-start(bf16[4,16,768]{2,1,0:T(8,128)(2,1)S(1)} %get-tuple-element.47), channel_id=1, source_target_pairs={{0,8},{4,12},{8,0},{12,4},{1,9},{5,13},{9,1},{13,5},{2,10},{6,14},... | collective-permute-start | bytes 294920 | tf_op jit(solution)/shard_map/ppermute | solution.py:416
  15.6 0.0 collective-permute-done.refs_1_
  15.6 2.6 %collective-permute-start.11 = (bf16[4,16,768]{2,1,0:T(8,128)(2,1)S(1)}, bf16[4,16,768]{2,1,0:T(8,128)(2,1)S(1)}, u32[]{:S(2)}, u32[]{:S(2)}) collective-permute-start(bf16[4,16,768]{2,1,0:T(8,128)(2,1)S(1)} %get-tuple-element.48), channel_id=1, source_target_pairs={{0,12},{4,0},{8,4},{12,8},{1,13},{5,1},{9,5},{13,9},{2,14},{6,2},{... | collective-permute-start | bytes 294920 | tf_op jit(solution)/shard_map/ppermute | solution.py:416
  18.3 0.0 collective-permute-done.1.refs_2_
  18.3 0.0 collective-permute-done.2.refs_3_
  18.3 0.0 copy-done.3
  18.3 0.6 %shard_map.57 = (bf16[2,4,16,768]{3,2,1,0:T(8,128)(2,1)S(1)}, bf16[1,4,16,768]{3,2,1,0:T(8,128)(2,1)S(1)}, bf16[2,4,16,768]{3,2,1,0:T(8,128)(2,1)S(1)}, bf16[4,4,16,768]{3,2,1,0:T(8,128)(2,1)}) custom-call(s32[8]{0:T(128)S(1)} %get-tuple-element.32.picks_ref, bf16[4,16,768]{2,1,0:T(8,128)(2,1)S(1)} %copy-done.3, ...), custom_call_target="tpu_custom_call", output_to_operand_aliasing={{3}: (5, {})} | custom-call | flops 99999997952 | tf_op jit(solution)/shard_map/pallas_call | solution.py:153
  18.9 4.1 %all-to-all-start = ((bf16[4,4,16,768]{3,2,1,0:T(8,128)(2,1)}), bf16[4,4,16,768]{3,2,1,0:T(8,128)(2,1)S(1)}, u32[]{:S(2)}, u32[]{:S(2)}) async-start(bf16[4,4,16,768]{3,2,1,0:T(8,128)(2,1)} %get-tuple-element.38), calls=%async_computation | async-start | bytes 786432 | tf_op jit(solution)/shard_map/all_to_all | solution.py:449
  23.0 1.5 %collective-permute-start.4 = (bf16[1,4,16,768]{3,2,1,0:T(8,128)(2,1)S(1)}, bf16[1,4,16,768]{3,2,1,0:T(8,128)(2,1)S(1)}, u32[]{:S(2)}, u32[]{:S(2)}) collective-permute-start(bf16[1,4,16,768]{3,2,1,0:T(8,128)(2,1)S(1)} %get-tuple-element.40), channel_id=1, source_target_pairs={{0,2},{1,3},{2,0},{3,1},{4,6},{5,7},{6,4},{7,5},{8,10},{9,11},{10,... | collective-permute-start | bytes 294920 | tf_op jit(solution)/shard_map/ppermute | solution.py:416
  24.5 0.0 collective-permute-start.5
  24.5 0.0 collective-permute-done.9.refs_1_.refs_8_
  24.5 0.5 %collective-permute-start.3 = (bf16[2,4,16,768]{3,2,1,0:T(8,128)(2,1)S(1)}, bf16[2,4,16,768]{3,2,1,0:T(8,128)(2,1)S(1)}, u32[]{:S(2)}, u32[]{:S(2)}) collective-permute-start(bf16[2,4,16,768]{3,2,1,0:T(8,128)(2,1)S(1)} %get-tuple-element.39.refs_4_), channel_id=1, source_target_pairs={{0,1},{1,2},{2,3},{3,0},{4,5},{5,6},{6,7},{7,4},{8,9},{9,10},{10,1... | collective-permute-start | bytes 589832 | tf_op jit(solution)/shard_map/ppermute | solution.py:416
  25.0 0.0 collective-permute-done.10.refs_2_.refs_9_
  25.0 0.0 collective-permute-done.11.refs_3_.refs_10_
  25.0 0.6 %shard_map.59 = (bf16[2,4,16,768]{3,2,1,0:T(8,128)(2,1)S(1)}, bf16[1,4,16,768]{3,2,1,0:T(8,128)(2,1)S(1)}, bf16[2,4,16,768]{3,2,1,0:T(8,128)(2,1)S(1)}) custom-call(s32[8]{0:T(128)S(1)} %get-tuple-element.32.picks_ref, bf16[4,16,768]{2,1,0:T(8,128)(2,1)S(1)} %get-tuple-element.45.refs_0_.refs_7_, ...), custom_call_target="tpu_custom_call" | custom-call | flops 99999997952 | tf_op jit(solution)/shard_map/pallas_call | solution.py:153
  25.6 0.8 %collective-permute-start.13 = (bf16[1,4,16,768]{3,2,1,0:T(8,128)(2,1)S(1)}, bf16[1,4,16,768]{3,2,1,0:T(8,128)(2,1)S(1)}, u32[]{:S(2)}, u32[]{:S(2)}) collective-permute-start(bf16[1,4,16,768]{3,2,1,0:T(8,128)(2,1)S(1)} %get-tuple-element.50), channel_id=1, source_target_pairs={{0,2},{1,3},{2,0},{3,1},{4,6},{5,7},{6,4},{7,5},{8,10},{9,11},{10,... | collective-permute-start | bytes 294920 | tf_op jit(solution)/shard_map/ppermute | solution.py:416
  26.5 0.6 %collective-permute-start.12 = (bf16[2,4,16,768]{3,2,1,0:T(8,128)(2,1)S(1)}, bf16[2,4,16,768]{3,2,1,0:T(8,128)(2,1)S(1)}, u32[]{:S(2)}, u32[]{:S(2)}) collective-permute-start(bf16[2,4,16,768]{3,2,1,0:T(8,128)(2,1)S(1)} %get-tuple-element.49), channel_id=1, source_target_pairs={{0,1},{1,2},{2,3},{3,0},{4,5},{5,6},{6,7},{7,4},{8,9},{9,10},{10,1... | collective-permute-start | bytes 589832 | tf_op jit(solution)/shard_map/ppermute | solution.py:416
  27.0 0.7 %collective-permute-done.4.refs_5_ = bf16[1,4,16,768]{3,2,1,0:T(8,128)(2,1)S(1)} collective-permute-done((bf16[1,4,16,768]{3,2,1,0:T(8,128)(2,1)S(1)}, bf16[1,4,16,768]{3,2,1,0:T(8,128)(2,1)S(1)}, u32[]{:S(2)}, u32[]{:S(2)}) %collective-permute-start.4) | collective-permute-done | bytes 98336 | tf_op jit(solution)/shard_map/ppermute | solution.py:416
  27.8 0.0 copy-start.6
  27.8 0.5 collective-permute-start.14
  28.2 3.7 %collective-permute-done.5.refs_6_ = bf16[2,4,16,768]{3,2,1,0:T(8,128)(2,1)S(1)} collective-permute-done((bf16[2,4,16,768]{3,2,1,0:T(8,128)(2,1)S(1)}, bf16[2,4,16,768]{3,2,1,0:T(8,128)(2,1)S(1)}, u32[]{:S(2)}, u32[]{:S(2)}) %collective-permute-start.5) | collective-permute-done | bytes 196640 | tf_op jit(solution)/shard_map/ppermute | solution.py:416
  31.9 0.0 collective-permute-done.3.refs_4_
  31.9 2.3 %all-to-all-done.query_ref = bf16[4,4,16,768]{3,2,1,0:T(8,128)(2,1)S(1)} async-done(((bf16[4,4,16,768]{3,2,1,0:T(8,128)(2,1)}), bf16[4,4,16,768]{3,2,1,0:T(8,128)(2,1)S(1)}, u32[]{:S(2)}, u32[]{:S(2)}) %all-to-all-start) | async-done | bytes 393248 | tf_op jit(solution)/shard_map/all_to_all | solution.py:449
  34.2 0.0 copy-done.6
  34.2 1.6 %shard_map.58 = (bf16[4,16,384]{2,1,0:T(8,128)(2,1)S(1)}, bf16[4,16,384]{2,1,0:T(8,128)(2,1)S(1)}, bf16[4,16,384]{2,1,0:T(8,128)(2,1)S(1)}) custom-call(s32[16]{0:T(128)S(1)} %copy-done.6, f32[4,576]{1,0:T(4,128)S(1)} %get-tuple-element.31.bias_ref, bf16[4,4,16,768]{3,2,1,0:T(8,128)(2,1)S(1)} %all-to-all-done.query_ref, bf16[4,16,768]{2,1,0:T(8,128)(2,1)S(1)} %copy-done.3, ...), custom_call_target="tpu_custom_call" | custom-call | flops 99999997952 | tf_op jit(solution)/shard_map/pallas_call | solution.py:373
  35.8 0.7 %collective-permute-start.7 = (bf16[4,16,384]{2,1,0:T(8,128)(2,1)S(1)}, bf16[4,16,384]{2,1,0:T(8,128)(2,1)S(1)}, u32[]{:S(2)}, u32[]{:S(2)}) collective-permute-start(bf16[4,16,384]{2,1,0:T(8,128)(2,1)S(1)} %get-tuple-element.43), channel_id=1, source_target_pairs={{0,8},{4,12},{8,0},{12,4},{1,9},{5,13},{9,1},{13,5},{2,10},{6,14},... | collective-permute-start | bytes 147464 | tf_op jit(solution)/shard_map/ppermute | solution.py:416
  36.5 2.4 %collective-permute-start.8 = (bf16[4,16,384]{2,1,0:T(8,128)(2,1)S(1)}, bf16[4,16,384]{2,1,0:T(8,128)(2,1)S(1)}, u32[]{:S(2)}, u32[]{:S(2)}) collective-permute-start(bf16[4,16,384]{2,1,0:T(8,128)(2,1)S(1)} %get-tuple-element.44), channel_id=1, source_target_pairs={{0,4},{4,8},{8,12},{12,0},{1,5},{5,9},{9,13},{13,1},{2,6},{6,10},{... | collective-permute-start | bytes 147464 | tf_op jit(solution)/shard_map/ppermute | solution.py:416
  38.9 0.0 collective-permute-done.13.refs_5_.refs_12_
  38.9 1.4 %collective-permute-start.6 = (bf16[4,16,384]{2,1,0:T(8,128)(2,1)S(1)}, bf16[4,16,384]{2,1,0:T(8,128)(2,1)S(1)}, u32[]{:S(2)}, u32[]{:S(2)}) collective-permute-start(bf16[4,16,384]{2,1,0:T(8,128)(2,1)S(1)} %get-tuple-element.42.refs_7_), channel_id=1, source_target_pairs={{0,12},{4,0},{8,4},{12,8},{1,13},{5,1},{9,5},{13,9},{2,14},{6,2},{... | collective-permute-start | bytes 147464 | tf_op jit(solution)/shard_map/ppermute | solution.py:416
  40.3 0.0 collective-permute-done.12.refs_4_.refs_11_
  40.3 0.0 collective-permute-done.14.refs_6_.refs_13_
  40.3 1.6 %shard_map.60 = (bf16[4,16,384]{2,1,0:T(8,128)(2,1)S(1)}, bf16[4,16,384]{2,1,0:T(8,128)(2,1)S(1)}, bf16[4,16,384]{2,1,0:T(8,128)(2,1)S(1)}) custom-call(s32[16]{0:T(128)S(1)} %copy-done.6, f32[4,576]{1,0:T(4,128)S(1)} %get-tuple-element.31.bias_ref, bf16[4,4,16,768]{3,2,1,0:T(8,128)(2,1)S(1)} %all-to-all-done.query_ref, ...), custom_call_target="tpu_custom_call" | custom-call | tf_op jit(solution)/shard_map/pallas_call | solution.py:373
  41.9 0.7 %collective-permute-start.16 = (bf16[4,16,384]{2,1,0:T(8,128)(2,1)S(1)}, bf16[4,16,384]{2,1,0:T(8,128)(2,1)S(1)}, u32[]{:S(2)}, u32[]{:S(2)}) collective-permute-start(bf16[4,16,384]{2,1,0:T(8,128)(2,1)S(1)} %get-tuple-element.53), channel_id=1, source_target_pairs={{0,8},{4,12},{8,0},{12,4},{1,9},{5,13},{9,1},{13,5},{2,10},{6,14},... | collective-permute-start | bytes 147464 | tf_op jit(solution)/shard_map/ppermute | solution.py:416
  42.6 1.2 %collective-permute-start.17 = (bf16[4,16,384]{2,1,0:T(8,128)(2,1)S(1)}, bf16[4,16,384]{2,1,0:T(8,128)(2,1)S(1)}, u32[]{:S(2)}, u32[]{:S(2)}) collective-permute-start(bf16[4,16,384]{2,1,0:T(8,128)(2,1)S(1)} %get-tuple-element.54), channel_id=1, source_target_pairs={{0,4},{4,8},{8,12},{12,0},{1,5},{5,9},{9,13},{13,1},{2,6},{6,10},{... | collective-permute-start | bytes 147464 | tf_op jit(solution)/shard_map/ppermute | solution.py:416
  43.8 0.0 collective-permute-done.7.refs_1_
  43.8 2.7 %collective-permute-start.15 = (bf16[4,16,384]{2,1,0:T(8,128)(2,1)S(1)}, bf16[4,16,384]{2,1,0:T(8,128)(2,1)S(1)}, u32[]{:S(2)}, u32[]{:S(2)}) collective-permute-start(bf16[4,16,384]{2,1,0:T(8,128)(2,1)S(1)} %get-tuple-element.52.refs_14_), channel_id=1, source_target_pairs={{0,12},{4,0},{8,4},{12,8},{1,13},{5,1},{9,5},{13,9},{2,14},{6,2},{... | collective-permute-start | bytes 147464 | tf_op jit(solution)/shard_map/ppermute | solution.py:416
  46.4 1.7 %shard_map.61.refs_6_ = bf16[4,16,768]{2,1,0:T(8,128)(2,1)S(1)} custom-call(s32[16]{0:T(128)S(1)} %copy-done.6, f32[4,576]{1,0:T(4,128)S(1)} %get-tuple-element.31.bias_ref, bf16[4,4,16,768]{3,2,1,0:T(8,128)(2,1)S(1)} %all-to-all-done.query_ref, bf16[4,16,768]{2,1,0:T(8,128)(2,1)S(1)} %copy-done.3, bf16[4,16,768]{2,1,0:T(8,128)(2,1)S(1)} %collective-permute-done.refs_1_, ...), custom_call_target="tpu_custom_call" | custom-call | tf_op jit(solution)/shard_map/pallas_call | solution.py:373
  48.2 0.0 collective-permute-done.8.refs_2_
  48.2 0.0 collective-permute-done.6.refs_0_
  48.2 0.8 %collective-permute-done.16.refs_4_ = bf16[4,16,384]{2,1,0:T(8,128)(2,1)S(1)} collective-permute-done((bf16[4,16,384]{2,1,0:T(8,128)(2,1)S(1)}, bf16[4,16,384]{2,1,0:T(8,128)(2,1)S(1)}, u32[]{:S(2)}, u32[]{:S(2)}) %collective-permute-start.16) | collective-permute-done | bytes 49184 | tf_op jit(solution)/shard_map/ppermute | solution.py:416
  49.0 0.0 collective-permute-done.17.refs_5_
  49.0 0.2 collective-permute-done.15.refs_3_
  49.2 0.8 %shard_map.62 = bf16[4,16,3072]{2,1,0:T(8,128)(2,1)} custom-call(bf16[4,16,384]{2,1,0:T(8,128)(2,1)S(1)} %collective-permute-done.6.refs_0_, bf16[4,16,384]{2,1,0:T(8,128)(2,1)S(1)} %collective-permute-done.7.refs_1_, bf16[4,16,384]{2,1,0:T(8,128)(2,1)S(1)} %collective-permute-done.8.refs_2_, bf16[4,16,384]{2,1,0:T(8,128)(2,1)S(1)} %collective-permute-done.15.refs_3_, ...), custom_call_target="tpu_custom_call" | custom-call | tf_op jit(solution)/shard_map/pallas_call | solution.py:404
Async XLA Ops:
  0.0 9.9 %copy-start.1 = (bf16[4,16,3072]{2,1,0:T(8,128)(2,1)S(1)}, bf16[4,16,3072]{2,1,0:T(8,128)(2,1)}, u32[]{:S(2)}) copy-start(bf16[4,16,3072]{2,1,0:T(8,128)(2,1)} %refs_2_.1) | copy-start | bytes 1179652
  0.0 9.9 %copy-start = (bf16[4,16,3072]{2,1,0:T(8,128)(2,1)S(1)}, bf16[4,16,3072]{2,1,0:T(8,128)(2,1)}, u32[]{:S(2)}) copy-start(bf16[4,16,3072]{2,1,0:T(8,128)(2,1)} %refs_1_.3) | copy-start | bytes 1179652
  2.9 7.0 %copy-start.7 = (f32[8,128]{1,0:T(8,128)S(1)}, f32[8,128]{1,0:T(8,128)}, u32[]{:S(2)}) copy-start(f32[8,128]{1,0:T(8,128)} %get-tuple-element.30.refs_5_) | copy-start | bytes 12292
  2.9 12.7 %collective-permute-start = (bf16[4,16,768]{2,1,0:T(8,128)(2,1)}, bf16[4,16,768]{2,1,0:T(8,128)(2,1)S(1)}, u32[]{:S(2)}, u32[]{:S(2)}) collective-permute-start(bf16[4,16,768]{2,1,0:T(8,128)(2,1)} %get-tuple-element.34), channel_id=1, source_target_pairs={{0,4},{4,8},{8,12},{12,0},{1,5},{5,9},{9,13},{13,1},{2,6},{6,10},{... | collective-permute-start | bytes 294920 | tf_op jit(solution)/shard_map/ppermute | solution.py:416
  6.0 12.3 %collective-permute-start.1 = (bf16[4,16,768]{2,1,0:T(8,128)(2,1)}, bf16[4,16,768]{2,1,0:T(8,128)(2,1)S(1)}, u32[]{:S(2)}, u32[]{:S(2)}) collective-permute-start(bf16[4,16,768]{2,1,0:T(8,128)(2,1)} %get-tuple-element.35), channel_id=1, source_target_pairs={{0,8},{4,12},{8,0},{12,4},{1,9},{5,13},{9,1},{13,5},{2,10},{6,14},... | collective-permute-start | bytes 294920 | tf_op jit(solution)/shard_map/ppermute | solution.py:416
  8.5 1.4 %copy-start.5 = (s32[16]{0:T(128)S(1)}, s32[16]{0:T(128)}, u32[]{:S(2)}) copy-start(s32[16]{0:T(128)} %tokens_ref.5) | copy-start | bytes 196
  8.5 9.7 %collective-permute-start.2 = (bf16[4,16,768]{2,1,0:T(8,128)(2,1)}, bf16[4,16,768]{2,1,0:T(8,128)(2,1)S(1)}, u32[]{:S(2)}, u32[]{:S(2)}) collective-permute-start(bf16[4,16,768]{2,1,0:T(8,128)(2,1)} %get-tuple-element.36), channel_id=1, source_target_pairs={{0,12},{4,0},{8,4},{12,8},{1,13},{5,1},{9,5},{13,9},{2,14},{6,2},{... | collective-permute-start | bytes 294920 | tf_op jit(solution)/shard_map/ppermute | solution.py:416
  9.9 1.0 %copy-start.2 = (bf16[4,16,3072]{2,1,0:T(8,128)(2,1)S(1)}, bf16[4,16,3072]{2,1,0:T(8,128)(2,1)}, u32[]{:S(2)}) copy-start(bf16[4,16,3072]{2,1,0:T(8,128)(2,1)} %refs_0_.3) | copy-start | bytes 1179652
  10.9 0.7 %copy-start.4 = (s32[16,32]{1,0:T(8,128)S(1)}, s32[16,32]{1,0:T(8,128)}, u32[]{:S(2)}) copy-start(s32[16,32]{1,0:T(8,128)} %refs_3_.1) | copy-start | bytes 6148
  11.6 6.7 %copy-start.3 = (bf16[4,16,768]{2,1,0:T(8,128)(2,1)S(1)}, bf16[4,16,768]{2,1,0:T(8,128)(2,1)}, u32[]{:S(2)}) copy-start(bf16[4,16,768]{2,1,0:T(8,128)(2,1)} %get-tuple-element.33.refs_0_) | copy-start | bytes 294916
  14.4 10.1 %collective-permute-start.9 = (bf16[4,16,768]{2,1,0:T(8,128)(2,1)S(1)}, bf16[4,16,768]{2,1,0:T(8,128)(2,1)S(1)}, u32[]{:S(2)}, u32[]{:S(2)}) collective-permute-start(bf16[4,16,768]{2,1,0:T(8,128)(2,1)S(1)} %get-tuple-element.46), channel_id=1, source_target_pairs={{0,4},{4,8},{8,12},{12,0},{1,5},{5,9},{9,13},{13,1},{2,6},{6,10},{... | collective-permute-start | bytes 294920 | tf_op jit(solution)/shard_map/ppermute | solution.py:416
  15.1 9.9 %collective-permute-start.10 = (bf16[4,16,768]{2,1,0:T(8,128)(2,1)S(1)}, bf16[4,16,768]{2,1,0:T(8,128)(2,1)S(1)}, u32[]{:S(2)}, u32[]{:S(2)}) collective-permute-start(bf16[4,16,768]{2,1,0:T(8,128)(2,1)S(1)} %get-tuple-element.47), channel_id=1, source_target_pairs={{0,8},{4,12},{8,0},{12,4},{1,9},{5,13},{9,1},{13,5},{2,10},{6,14},... | collective-permute-start | bytes 294920 | tf_op jit(solution)/shard_map/ppermute | solution.py:416
  15.6 9.4 %collective-permute-start.11 = (bf16[4,16,768]{2,1,0:T(8,128)(2,1)S(1)}, bf16[4,16,768]{2,1,0:T(8,128)(2,1)S(1)}, u32[]{:S(2)}, u32[]{:S(2)}) collective-permute-start(bf16[4,16,768]{2,1,0:T(8,128)(2,1)S(1)} %get-tuple-element.48), channel_id=1, source_target_pairs={{0,12},{4,0},{8,4},{12,8},{1,13},{5,1},{9,5},{13,9},{2,14},{6,2},{... | collective-permute-start | bytes 294920 | tf_op jit(solution)/shard_map/ppermute | solution.py:416
  18.9 15.3 %all-to-all-start = ((bf16[4,4,16,768]{3,2,1,0:T(8,128)(2,1)}), bf16[4,4,16,768]{3,2,1,0:T(8,128)(2,1)S(1)}, u32[]{:S(2)}, u32[]{:S(2)}) async-start(bf16[4,4,16,768]{3,2,1,0:T(8,128)(2,1)} %get-tuple-element.38), calls=%async_computation | async-start | bytes 786432 | tf_op jit(solution)/shard_map/all_to_all | solution.py:449
  23.0 4.8 %collective-permute-start.4 = (bf16[1,4,16,768]{3,2,1,0:T(8,128)(2,1)S(1)}, bf16[1,4,16,768]{3,2,1,0:T(8,128)(2,1)S(1)}, u32[]{:S(2)}, u32[]{:S(2)}) collective-permute-start(bf16[1,4,16,768]{3,2,1,0:T(8,128)(2,1)S(1)} %get-tuple-element.40), channel_id=1, source_target_pairs={{0,2},{1,3},{2,0},{3,1},{4,6},{5,7},{6,4},{7,5},{8,10},{9,11},{10,... | collective-permute-start | bytes 294920 | tf_op jit(solution)/shard_map/ppermute | solution.py:416
  24.5 7.4 %collective-permute-start.5 = (bf16[2,4,16,768]{3,2,1,0:T(8,128)(2,1)S(1)}, bf16[2,4,16,768]{3,2,1,0:T(8,128)(2,1)S(1)}, u32[]{:S(2)}, u32[]{:S(2)}) collective-permute-start(bf16[2,4,16,768]{3,2,1,0:T(8,128)(2,1)S(1)} %get-tuple-element.41), channel_id=1, source_target_pairs={{0,3},{1,0},{2,1},{3,2},{4,7},{5,4},{6,5},{7,6},{8,11},{9,8},{10,9... | collective-permute-start | bytes 589832 | tf_op jit(solution)/shard_map/ppermute | solution.py:416
  24.5 7.4 %collective-permute-start.3 = (bf16[2,4,16,768]{3,2,1,0:T(8,128)(2,1)S(1)}, bf16[2,4,16,768]{3,2,1,0:T(8,128)(2,1)S(1)}, u32[]{:S(2)}, u32[]{:S(2)}) collective-permute-start(bf16[2,4,16,768]{3,2,1,0:T(8,128)(2,1)S(1)} %get-tuple-element.39.refs_4_), channel_id=1, source_target_pairs={{0,1},{1,2},{2,3},{3,0},{4,5},{5,6},{6,7},{7,4},{8,9},{9,10},{10,1... | collective-permute-start | bytes 589832 | tf_op jit(solution)/shard_map/ppermute | solution.py:416
  25.6 13.3 %collective-permute-start.13 = (bf16[1,4,16,768]{3,2,1,0:T(8,128)(2,1)S(1)}, bf16[1,4,16,768]{3,2,1,0:T(8,128)(2,1)S(1)}, u32[]{:S(2)}, u32[]{:S(2)}) collective-permute-start(bf16[1,4,16,768]{3,2,1,0:T(8,128)(2,1)S(1)} %get-tuple-element.50), channel_id=1, source_target_pairs={{0,2},{1,3},{2,0},{3,1},{4,6},{5,7},{6,4},{7,5},{8,10},{9,11},{10,... | collective-permute-start | bytes 294920 | tf_op jit(solution)/shard_map/ppermute | solution.py:416
  26.5 13.9 %collective-permute-start.12 = (bf16[2,4,16,768]{3,2,1,0:T(8,128)(2,1)S(1)}, bf16[2,4,16,768]{3,2,1,0:T(8,128)(2,1)S(1)}, u32[]{:S(2)}, u32[]{:S(2)}) collective-permute-start(bf16[2,4,16,768]{3,2,1,0:T(8,128)(2,1)S(1)} %get-tuple-element.49), channel_id=1, source_target_pairs={{0,1},{1,2},{2,3},{3,0},{4,5},{5,6},{6,7},{7,4},{8,9},{9,10},{10,1... | collective-permute-start | bytes 589832 | tf_op jit(solution)/shard_map/ppermute | solution.py:416
  27.8 6.5 %copy-start.6 = (s32[16]{0:T(128)S(1)}, s32[16]{0:T(128)}, u32[]{:S(2)}) copy-start(s32[16]{0:T(128)} %tokens_ref.5) | copy-start | bytes 196
  27.8 12.6 %collective-permute-start.14 = (bf16[2,4,16,768]{3,2,1,0:T(8,128)(2,1)S(1)}, bf16[2,4,16,768]{3,2,1,0:T(8,128)(2,1)S(1)}, u32[]{:S(2)}, u32[]{:S(2)}) collective-permute-start(bf16[2,4,16,768]{3,2,1,0:T(8,128)(2,1)S(1)} %get-tuple-element.51), channel_id=1, source_target_pairs={{0,3},{1,0},{2,1},{3,2},{4,7},{5,4},{6,5},{7,6},{8,11},{9,8},{10,9... | collective-permute-start | bytes 589832 | tf_op jit(solution)/shard_map/ppermute | solution.py:416
  35.8 7.9 %collective-permute-start.7 = (bf16[4,16,384]{2,1,0:T(8,128)(2,1)S(1)}, bf16[4,16,384]{2,1,0:T(8,128)(2,1)S(1)}, u32[]{:S(2)}, u32[]{:S(2)}) collective-permute-start(bf16[4,16,384]{2,1,0:T(8,128)(2,1)S(1)} %get-tuple-element.43), channel_id=1, source_target_pairs={{0,8},{4,12},{8,0},{12,4},{1,9},{5,13},{9,1},{13,5},{2,10},{6,14},... | collective-permute-start | bytes 147464 | tf_op jit(solution)/shard_map/ppermute | solution.py:416
  36.5 11.7 %collective-permute-start.8 = (bf16[4,16,384]{2,1,0:T(8,128)(2,1)S(1)}, bf16[4,16,384]{2,1,0:T(8,128)(2,1)S(1)}, u32[]{:S(2)}, u32[]{:S(2)}) collective-permute-start(bf16[4,16,384]{2,1,0:T(8,128)(2,1)S(1)} %get-tuple-element.44), channel_id=1, source_target_pairs={{0,4},{4,8},{8,12},{12,0},{1,5},{5,9},{9,13},{13,1},{2,6},{6,10},{... | collective-permute-start | bytes 147464 | tf_op jit(solution)/shard_map/ppermute | solution.py:416
  38.9 9.3 %collective-permute-start.6 = (bf16[4,16,384]{2,1,0:T(8,128)(2,1)S(1)}, bf16[4,16,384]{2,1,0:T(8,128)(2,1)S(1)}, u32[]{:S(2)}, u32[]{:S(2)}) collective-permute-start(bf16[4,16,384]{2,1,0:T(8,128)(2,1)S(1)} %get-tuple-element.42.refs_7_), channel_id=1, source_target_pairs={{0,12},{4,0},{8,4},{12,8},{1,13},{5,1},{9,5},{13,9},{2,14},{6,2},{... | collective-permute-start | bytes 147464 | tf_op jit(solution)/shard_map/ppermute | solution.py:416
  41.9 7.0 %collective-permute-start.16 = (bf16[4,16,384]{2,1,0:T(8,128)(2,1)S(1)}, bf16[4,16,384]{2,1,0:T(8,128)(2,1)S(1)}, u32[]{:S(2)}, u32[]{:S(2)}) collective-permute-start(bf16[4,16,384]{2,1,0:T(8,128)(2,1)S(1)} %get-tuple-element.53), channel_id=1, source_target_pairs={{0,8},{4,12},{8,0},{12,4},{1,9},{5,13},{9,1},{13,5},{2,10},{6,14},... | collective-permute-start | bytes 147464 | tf_op jit(solution)/shard_map/ppermute | solution.py:416
  42.6 6.4 %collective-permute-start.17 = (bf16[4,16,384]{2,1,0:T(8,128)(2,1)S(1)}, bf16[4,16,384]{2,1,0:T(8,128)(2,1)S(1)}, u32[]{:S(2)}, u32[]{:S(2)}) collective-permute-start(bf16[4,16,384]{2,1,0:T(8,128)(2,1)S(1)} %get-tuple-element.54), channel_id=1, source_target_pairs={{0,4},{4,8},{8,12},{12,0},{1,5},{5,9},{9,13},{13,1},{2,6},{6,10},{... | collective-permute-start | bytes 147464 | tf_op jit(solution)/shard_map/ppermute | solution.py:416
  43.8 5.4 %collective-permute-start.15 = (bf16[4,16,384]{2,1,0:T(8,128)(2,1)S(1)}, bf16[4,16,384]{2,1,0:T(8,128)(2,1)S(1)}, u32[]{:S(2)}, u32[]{:S(2)}) collective-permute-start(bf16[4,16,384]{2,1,0:T(8,128)(2,1)S(1)} %get-tuple-element.52.refs_14_), channel_id=1, source_target_pairs={{0,12},{4,0},{8,4},{12,8},{1,13},{5,1},{9,5},{13,9},{2,14},{6,2},{... | collective-permute-start | bytes 147464 | tf_op jit(solution)/shard_map/ppermute | solution.py:416
where the time goes:
time: 50.2 us; the launch traced here: 50 us
  starting transfers between devices  27.9 us (56%)
  Pallas kernels  12.5 us (25%)
  waiting for transfers between devices  7.74 us (15%)
  local copies, waits for them, and re-layouts  1.71 us (3%)
    ppermute x18, starting transfers between devices, shifted(): lax.ppermute(array, axis, [(i, (i + distance) % count) for i in range(cou...  23.7 us
    ppermute x18, waiting for transfers between devices, shifted(): lax.ppermute(array, axis, [(i, (i + distance) % count) for i in range(cou...  5.43 us
    pallas_call x3, Pallas kernels, attend(): pl.pallas_call(functools.partial(attend_kernel, (count_head, count_tm), h...  4.93 us
    all_to_all x1, starting transfers between devices, shards(): lax.all_to_all(query, 'head', split_axis=0, concat_axis=0, tiled=True)  4.13 us
    pallas_call x1, Pallas kernels, rotate_pieces(): pl.pallas_call(functools.partial(rotate_kernel, message, sources, count_h...  2.86 us
    pallas_call x1, Pallas kernels, plan(): pl.pallas_call(functools.partial(plan_kernel, messages, count_head, count...  2.76 us
    all_to_all x1, waiting for transfers between devices, shards(): lax.all_to_all(query, 'head', split_axis=0, concat_axis=0, tiled=True)  2.32 us
    unnamed x16, local copies, waits for them, and re-layouts  1.71 us
  transfers between devices with their start and end apart: 19, of which 5 were waited for; matrix products, arithmetic and copies ran while one was open for 0% of the time, Pallas kernels for 18%

commit v1 on v0

--- a/solution.py
+++ b/solution.py
@@ -446,8 +446,8 @@
         if not sent:
             *picked, query = picked
         sent.append(list(picked))
+    inputs = [(owns, forward(picked)) for owns, picked in zip(received, sent)]
     query = lax.all_to_all(query, "head", split_axis=0, concat_axis=0, tiled=True)
-    inputs = [(owns, forward(picked)) for owns, picked in zip(received, sent)]
     distances, after = list(range(1, count_head)), ()
     pieces, places = [], []
     for at, part in enumerate(parts):

time: 50.2 us -> 50.2 us (level)
  no operation moved by 1% of the time
where the time goes in v1:
time: 50.2 us; the launch traced here: 50 us
  starting transfers between devices  27.9 us (56%)
  Pallas kernels  12.5 us (25%)
  waiting for transfers between devices  7.74 us (15%)
  local copies, waits for them, and re-layouts  1.71 us (3%)
    ppermute x18, starting transfers between devices, shifted(): lax.ppermute(array, axis, [(i, (i + distance) % count) for i in range(cou...  23.7 us
    ppermute x18, waiting for transfers between devices, shifted(): lax.ppermute(array, axis, [(i, (i + distance) % count) for i in range(cou...  5.43 us
    pallas_call x3, Pallas kernels, attend(): pl.pallas_call(functools.partial(attend_kernel, (count_head, count_tm), h...  4.93 us
    all_to_all x1, starting transfers between devices, shards(): lax.all_to_all(query, 'head', split_axis=0, concat_axis=0, tiled=True)  4.13 us
    pallas_call x1, Pallas kernels, rotate_pieces(): pl.pallas_call(functools.partial(rotate_kernel, message, sources, count_h...  2.86 us
    pallas_call x1, Pallas kernels, plan(): pl.pallas_call(functools.partial(plan_kernel, messages, count_head, count...  2.76 us
    all_to_all x1, waiting for transfers between devices, shards(): lax.all_to_all(query, 'head', split_axis=0, concat_axis=0, tiled=True)  2.32 us
    unnamed x16, local copies, waits for them, and re-layouts  1.71 us
  transfers between devices with their start and end apart: 19, of which 5 were waited for; matrix products, arithmetic and copies ran while one was open for 0% of the time, Pallas kernels for 18%

profile of v1, /device:TPU:0, one launch (start us, length us, event | category | flops | bytes accessed | tf_op | source)
XLA Modules:
  0.0 50.0 jit_solution(16895061474182599552)
XLA Ops:
  0.0 0.0 copy-start.1
  0.0 0.0 copy-start
  0.0 2.9 %shard_map.55 = (bf16[4,16,768]{2,1,0:T(8,128)(2,1)}, bf16[4,16,768]{2,1,0:T(8,128)(2,1)}, bf16[4,16,768]{2,1,0:T(8,128)(2,1)}, bf16[4,16,768]{2,1,0:T(8,128)(2,1)}, f32[8,128]{1,0:T(8,128)}) custom-call(bf16[4,16,3072]{2,1,0:T(8,128)(2,1)} %refs_1_.3, bf16[4,16,3072]{2,1,0:T(8,128)(2,1)} %refs_2_.1), custom_call_target="tpu_custom_call" | custom-call | tf_op jit(solution)/shard_map/pallas_call | solution.py:114
  2.9 0.0 copy-start.7
  2.9 3.1 %collective-permute-start = (bf16[4,16,768]{2,1,0:T(8,128)(2,1)}, bf16[4,16,768]{2,1,0:T(8,128)(2,1)S(1)}, u32[]{:S(2)}, u32[]{:S(2)}) collective-permute-start(bf16[4,16,768]{2,1,0:T(8,128)(2,1)} %get-tuple-element.34), channel_id=1, source_target_pairs={{0,4},{4,8},{8,12},{12,0},{1,5},{5,9},{9,13},{13,1},{2,6},{6,10},{... | collective-permute-start | bytes 294920 | tf_op jit(solution)/shard_map/ppermute | solution.py:416
  6.0 2.6 %collective-permute-start.1 = (bf16[4,16,768]{2,1,0:T(8,128)(2,1)}, bf16[4,16,768]{2,1,0:T(8,128)(2,1)S(1)}, u32[]{:S(2)}, u32[]{:S(2)}) collective-permute-start(bf16[4,16,768]{2,1,0:T(8,128)(2,1)} %get-tuple-element.35), channel_id=1, source_target_pairs={{0,8},{4,12},{8,0},{12,4},{1,9},{5,13},{9,1},{13,5},{2,10},{6,14},... | collective-permute-start | bytes 294920 | tf_op jit(solution)/shard_map/ppermute | solution.py:416
  8.5 0.0 copy-start.5
  8.5 1.3 %collective-permute-start.2 = (bf16[4,16,768]{2,1,0:T(8,128)(2,1)}, bf16[4,16,768]{2,1,0:T(8,128)(2,1)S(1)}, u32[]{:S(2)}, u32[]{:S(2)}) collective-permute-start(bf16[4,16,768]{2,1,0:T(8,128)(2,1)} %get-tuple-element.36), channel_id=1, source_target_pairs={{0,12},{4,0},{8,4},{12,8},{1,13},{5,1},{9,5},{13,9},{2,14},{6,2},{... | collective-permute-start | bytes 294920 | tf_op jit(solution)/shard_map/ppermute | solution.py:416
  9.9 0.0 copy-done.1
  9.9 0.0 copy-done
  9.9 0.0 copy-done.7
  9.9 0.0 copy-done.5
  9.9 0.0 copy-start.2
  9.9 1.0 %copy-done.2 = bf16[4,16,3072]{2,1,0:T(8,128)(2,1)S(1)} copy-done((bf16[4,16,3072]{2,1,0:T(8,128)(2,1)S(1)}, bf16[4,16,3072]{2,1,0:T(8,128)(2,1)}, u32[]{:S(2)}) %copy-start.2) | copy-done | bytes 393240
  10.9 0.0 copy-start.4
  10.9 0.7 %copy-done.4 = s32[16,32]{1,0:T(8,128)S(1)} copy-done((s32[16,32]{1,0:T(8,128)S(1)}, s32[16,32]{1,0:T(8,128)}, u32[]{:S(2)}) %copy-start.4) | copy-done | bytes 2072
  11.6 0.0 copy-start.3
  11.6 2.8 %shard_map.56 = (s32[8]{0:T(128)S(1)}, f32[4,576]{1,0:T(4,128)S(1)}, bf16[4,4,16,768]{3,2,1,0:T(8,128)(2,1)}, bf16[4,16,768]{2,1,0:T(8,128)(2,1)S(1)}, bf16[4,16...) custom-call(bf16[4,16,3072]{2,1,0:T(8,128)(2,1)S(1)} %copy-done.2, ...), custom_call_target="tpu_custom_call" | custom-call | tf_op jit(solution)/shard_map/pallas_call | solution.py:281
  14.4 0.7 %collective-permute-start.9 = (bf16[4,16,768]{2,1,0:T(8,128)(2,1)S(1)}, bf16[4,16,768]{2,1,0:T(8,128)(2,1)S(1)}, u32[]{:S(2)}, u32[]{:S(2)}) collective-permute-start(bf16[4,16,768]{2,1,0:T(8,128)(2,1)S(1)} %get-tuple-element.46), channel_id=1, source_target_pairs={{0,4},{4,8},{8,12},{12,0},{1,5},{5,9},{9,13},{13,1},{2,6},{6,10},{... | collective-permute-start | bytes 294920 | tf_op jit(solution)/shard_map/ppermute | solution.py:416
  15.1 0.5 %collective-permute-start.10 = (bf16[4,16,768]{2,1,0:T(8,128)(2,1)S(1)}, bf16[4,16,768]{2,1,0:T(8,128)(2,1)S(1)}, u32[]{:S(2)}, u32[]{:S(2)}) collective-permute-start(bf16[4,16,768]{2,1,0:T(8,128)(2,1)S(1)} %get-tuple-element.47), channel_id=1, source_target_pairs={{0,8},{4,12},{8,0},{12,4},{1,9},{5,13},{9,1},{13,5},{2,10},{6,14},... | collective-permute-start | bytes 294920 | tf_op jit(solution)/shard_map/ppermute | solution.py:416
  15.6 0.0 collective-permute-done.refs_1_
  15.6 2.6 %collective-permute-start.11 = (bf16[4,16,768]{2,1,0:T(8,128)(2,1)S(1)}, bf16[4,16,768]{2,1,0:T(8,128)(2,1)S(1)}, u32[]{:S(2)}, u32[]{:S(2)}) collective-permute-start(bf16[4,16,768]{2,1,0:T(8,128)(2,1)S(1)} %get-tuple-element.48), channel_id=1, source_target_pairs={{0,12},{4,0},{8,4},{12,8},{1,13},{5,1},{9,5},{13,9},{2,14},{6,2},{... | collective-permute-start | bytes 294920 | tf_op jit(solution)/shard_map/ppermute | solution.py:416
  18.3 0.0 collective-permute-done.1.refs_2_
  18.3 0.0 collective-permute-done.2.refs_3_
  18.3 0.0 copy-done.3
  18.3 0.6 %shard_map.57 = (bf16[2,4,16,768]{3,2,1,0:T(8,128)(2,1)S(1)}, bf16[1,4,16,768]{3,2,1,0:T(8,128)(2,1)S(1)}, bf16[2,4,16,768]{3,2,1,0:T(8,128)(2,1)S(1)}, bf16[4,4,16,768]{3,2,1,0:T(8,128)(2,1)}) custom-call(s32[8]{0:T(128)S(1)} %get-tuple-element.32.picks_ref, bf16[4,16,768]{2,1,0:T(8,128)(2,1)S(1)} %copy-done.3, ...), custom_call_target="tpu_custom_call", output_to_operand_aliasing={{3}: (5, {})} | custom-call | flops 99999997952 | tf_op jit(solution)/shard_map/pallas_call | solution.py:153
  18.9 4.1 %all-to-all-start = ((bf16[4,4,16,768]{3,2,1,0:T(8,128)(2,1)}), bf16[4,4,16,768]{3,2,1,0:T(8,128)(2,1)S(1)}, u32[]{:S(2)}, u32[]{:S(2)}) async-start(bf16[4,4,16,768]{3,2,1,0:T(8,128)(2,1)} %get-tuple-element.38), calls=%async_computation | async-start | bytes 786432 | tf_op jit(solution)/shard_map/all_to_all | solution.py:450
  23.0 1.5 %collective-permute-start.4 = (bf16[1,4,16,768]{3,2,1,0:T(8,128)(2,1)S(1)}, bf16[1,4,16,768]{3,2,1,0:T(8,128)(2,1)S(1)}, u32[]{:S(2)}, u32[]{:S(2)}) collective-permute-start(bf16[1,4,16,768]{3,2,1,0:T(8,128)(2,1)S(1)} %get-tuple-element.40), channel_id=1, source_target_pairs={{0,2},{1,3},{2,0},{3,1},{4,6},{5,7},{6,4},{7,5},{8,10},{9,11},{10,... | collective-permute-start | bytes 294920 | tf_op jit(solution)/shard_map/ppermute | solution.py:416
  24.5 0.0 collective-permute-start.5
  24.5 0.0 collective-permute-done.9.refs_1_.refs_8_
  24.5 0.5 %collective-permute-start.3 = (bf16[2,4,16,768]{3,2,1,0:T(8,128)(2,1)S(1)}, bf16[2,4,16,768]{3,2,1,0:T(8,128)(2,1)S(1)}, u32[]{:S(2)}, u32[]{:S(2)}) collective-permute-start(bf16[2,4,16,768]{3,2,1,0:T(8,128)(2,1)S(1)} %get-tuple-element.39.refs_4_), channel_id=1, source_target_pairs={{0,1},{1,2},{2,3},{3,0},{4,5},{5,6},{6,7},{7,4},{8,9},{9,10},{10,1... | collective-permute-start | bytes 589832 | tf_op jit(solution)/shard_map/ppermute | solution.py:416
  25.0 0.0 collective-permute-done.10.refs_2_.refs_9_
  25.0 0.0 collective-permute-done.11.refs_3_.refs_10_
  25.0 0.6 %shard_map.59 = (bf16[2,4,16,768]{3,2,1,0:T(8,128)(2,1)S(1)}, bf16[1,4,16,768]{3,2,1,0:T(8,128)(2,1)S(1)}, bf16[2,4,16,768]{3,2,1,0:T(8,128)(2,1)S(1)}) custom-call(s32[8]{0:T(128)S(1)} %get-tuple-element.32.picks_ref, bf16[4,16,768]{2,1,0:T(8,128)(2,1)S(1)} %get-tuple-element.45.refs_0_.refs_7_, ...), custom_call_target="tpu_custom_call" | custom-call | flops 99999997952 | tf_op jit(solution)/shard_map/pallas_call | solution.py:153
  25.6 0.8 %collective-permute-start.13 = (bf16[1,4,16,768]{3,2,1,0:T(8,128)(2,1)S(1)}, bf16[1,4,16,768]{3,2,1,0:T(8,128)(2,1)S(1)}, u32[]{:S(2)}, u32[]{:S(2)}) collective-permute-start(bf16[1,4,16,768]{3,2,1,0:T(8,128)(2,1)S(1)} %get-tuple-element.50), channel_id=1, source_target_pairs={{0,2},{1,3},{2,0},{3,1},{4,6},{5,7},{6,4},{7,5},{8,10},{9,11},{10,... | collective-permute-start | bytes 294920 | tf_op jit(solution)/shard_map/ppermute | solution.py:416
  26.5 0.6 %collective-permute-start.12 = (bf16[2,4,16,768]{3,2,1,0:T(8,128)(2,1)S(1)}, bf16[2,4,16,768]{3,2,1,0:T(8,128)(2,1)S(1)}, u32[]{:S(2)}, u32[]{:S(2)}) collective-permute-start(bf16[2,4,16,768]{3,2,1,0:T(8,128)(2,1)S(1)} %get-tuple-element.49), channel_id=1, source_target_pairs={{0,1},{1,2},{2,3},{3,0},{4,5},{5,6},{6,7},{7,4},{8,9},{9,10},{10,1... | collective-permute-start | bytes 589832 | tf_op jit(solution)/shard_map/ppermute | solution.py:416
  27.0 0.7 %collective-permute-done.4.refs_5_ = bf16[1,4,16,768]{3,2,1,0:T(8,128)(2,1)S(1)} collective-permute-done((bf16[1,4,16,768]{3,2,1,0:T(8,128)(2,1)S(1)}, bf16[1,4,16,768]{3,2,1,0:T(8,128)(2,1)S(1)}, u32[]{:S(2)}, u32[]{:S(2)}) %collective-permute-start.4) | collective-permute-done | bytes 98336 | tf_op jit(solution)/shard_map/ppermute | solution.py:416
  27.8 0.0 copy-start.6
  27.8 0.5 collective-permute-start.14
  28.2 3.7 %collective-permute-done.5.refs_6_ = bf16[2,4,16,768]{3,2,1,0:T(8,128)(2,1)S(1)} collective-permute-done((bf16[2,4,16,768]{3,2,1,0:T(8,128)(2,1)S(1)}, bf16[2,4,16,768]{3,2,1,0:T(8,128)(2,1)S(1)}, u32[]{:S(2)}, u32[]{:S(2)}) %collective-permute-start.5) | collective-permute-done | bytes 196640 | tf_op jit(solution)/shard_map/ppermute | solution.py:416
  31.9 0.0 collective-permute-done.3.refs_4_
  31.9 2.3 %all-to-all-done.query_ref = bf16[4,4,16,768]{3,2,1,0:T(8,128)(2,1)S(1)} async-done(((bf16[4,4,16,768]{3,2,1,0:T(8,128)(2,1)}), bf16[4,4,16,768]{3,2,1,0:T(8,128)(2,1)S(1)}, u32[]{:S(2)}, u32[]{:S(2)}) %all-to-all-start) | async-done | bytes 393248 | tf_op jit(solution)/shard_map/all_to_all | solution.py:450
  34.2 0.0 copy-done.6
  34.2 1.6 %shard_map.58 = (bf16[4,16,384]{2,1,0:T(8,128)(2,1)S(1)}, bf16[4,16,384]{2,1,0:T(8,128)(2,1)S(1)}, bf16[4,16,384]{2,1,0:T(8,128)(2,1)S(1)}) custom-call(s32[16]{0:T(128)S(1)} %copy-done.6, f32[4,576]{1,0:T(4,128)S(1)} %get-tuple-element.31.bias_ref, bf16[4,4,16,768]{3,2,1,0:T(8,128)(2,1)S(1)} %all-to-all-done.query_ref, bf16[4,16,768]{2,1,0:T(8,128)(2,1)S(1)} %copy-done.3, ...), custom_call_target="tpu_custom_call" | custom-call | flops 99999997952 | tf_op jit(solution)/shard_map/pallas_call | solution.py:373
  35.8 0.7 %collective-permute-start.7 = (bf16[4,16,384]{2,1,0:T(8,128)(2,1)S(1)}, bf16[4,16,384]{2,1,0:T(8,128)(2,1)S(1)}, u32[]{:S(2)}, u32[]{:S(2)}) collective-permute-start(bf16[4,16,384]{2,1,0:T(8,128)(2,1)S(1)} %get-tuple-element.43), channel_id=1, source_target_pairs={{0,8},{4,12},{8,0},{12,4},{1,9},{5,13},{9,1},{13,5},{2,10},{6,14},... | collective-permute-start | bytes 147464 | tf_op jit(solution)/shard_map/ppermute | solution.py:416
  36.5 2.4 %collective-permute-start.8 = (bf16[4,16,384]{2,1,0:T(8,128)(2,1)S(1)}, bf16[4,16,384]{2,1,0:T(8,128)(2,1)S(1)}, u32[]{:S(2)}, u32[]{:S(2)}) collective-permute-start(bf16[4,16,384]{2,1,0:T(8,128)(2,1)S(1)} %get-tuple-element.44), channel_id=1, source_target_pairs={{0,4},{4,8},{8,12},{12,0},{1,5},{5,9},{9,13},{13,1},{2,6},{6,10},{... | collective-permute-start | bytes 147464 | tf_op jit(solution)/shard_map/ppermute | solution.py:416
  38.9 0.0 collective-permute-done.13.refs_5_.refs_12_
  38.9 1.4 %collective-permute-start.6 = (bf16[4,16,384]{2,1,0:T(8,128)(2,1)S(1)}, bf16[4,16,384]{2,1,0:T(8,128)(2,1)S(1)}, u32[]{:S(2)}, u32[]{:S(2)}) collective-permute-start(bf16[4,16,384]{2,1,0:T(8,128)(2,1)S(1)} %get-tuple-element.42.refs_7_), channel_id=1, source_target_pairs={{0,12},{4,0},{8,4},{12,8},{1,13},{5,1},{9,5},{13,9},{2,14},{6,2},{... | collective-permute-start | bytes 147464 | tf_op jit(solution)/shard_map/ppermute | solution.py:416
  40.3 0.0 collective-permute-done.12.refs_4_.refs_11_
  40.3 0.0 collective-permute-done.14.refs_6_.refs_13_
  40.3 1.6 %shard_map.60 = (bf16[4,16,384]{2,1,0:T(8,128)(2,1)S(1)}, bf16[4,16,384]{2,1,0:T(8,128)(2,1)S(1)}, bf16[4,16,384]{2,1,0:T(8,128)(2,1)S(1)}) custom-call(s32[16]{0:T(128)S(1)} %copy-done.6, f32[4,576]{1,0:T(4,128)S(1)} %get-tuple-element.31.bias_ref, bf16[4,4,16,768]{3,2,1,0:T(8,128)(2,1)S(1)} %all-to-all-done.query_ref, ...), custom_call_target="tpu_custom_call" | custom-call | tf_op jit(solution)/shard_map/pallas_call | solution.py:373
  41.9 0.7 %collective-permute-start.16 = (bf16[4,16,384]{2,1,0:T(8,128)(2,1)S(1)}, bf16[4,16,384]{2,1,0:T(8,128)(2,1)S(1)}, u32[]{:S(2)}, u32[]{:S(2)}) collective-permute-start(bf16[4,16,384]{2,1,0:T(8,128)(2,1)S(1)} %get-tuple-element.53), channel_id=1, source_target_pairs={{0,8},{4,12},{8,0},{12,4},{1,9},{5,13},{9,1},{13,5},{2,10},{6,14},... | collective-permute-start | bytes 147464 | tf_op jit(solution)/shard_map/ppermute | solution.py:416
  42.6 1.2 %collective-permute-start.17 = (bf16[4,16,384]{2,1,0:T(8,128)(2,1)S(1)}, bf16[4,16,384]{2,1,0:T(8,128)(2,1)S(1)}, u32[]{:S(2)}, u32[]{:S(2)}) collective-permute-start(bf16[4,16,384]{2,1,0:T(8,128)(2,1)S(1)} %get-tuple-element.54), channel_id=1, source_target_pairs={{0,4},{4,8},{8,12},{12,0},{1,5},{5,9},{9,13},{13,1},{2,6},{6,10},{... | collective-permute-start | bytes 147464 | tf_op jit(solution)/shard_map/ppermute | solution.py:416
  43.8 0.0 collective-permute-done.7.refs_1_
  43.8 2.7 %collective-permute-start.15 = (bf16[4,16,384]{2,1,0:T(8,128)(2,1)S(1)}, bf16[4,16,384]{2,1,0:T(8,128)(2,1)S(1)}, u32[]{:S(2)}, u32[]{:S(2)}) collective-permute-start(bf16[4,16,384]{2,1,0:T(8,128)(2,1)S(1)} %get-tuple-element.52.refs_14_), channel_id=1, source_target_pairs={{0,12},{4,0},{8,4},{12,8},{1,13},{5,1},{9,5},{13,9},{2,14},{6,2},{... | collective-permute-start | bytes 147464 | tf_op jit(solution)/shard_map/ppermute | solution.py:416
  46.4 1.7 %shard_map.61.refs_6_ = bf16[4,16,768]{2,1,0:T(8,128)(2,1)S(1)} custom-call(s32[16]{0:T(128)S(1)} %copy-done.6, f32[4,576]{1,0:T(4,128)S(1)} %get-tuple-element.31.bias_ref, bf16[4,4,16,768]{3,2,1,0:T(8,128)(2,1)S(1)} %all-to-all-done.query_ref, bf16[4,16,768]{2,1,0:T(8,128)(2,1)S(1)} %copy-done.3, bf16[4,16,768]{2,1,0:T(8,128)(2,1)S(1)} %collective-permute-done.refs_1_, ...), custom_call_target="tpu_custom_call" | custom-call | tf_op jit(solution)/shard_map/pallas_call | solution.py:373
  48.2 0.0 collective-permute-done.8.refs_2_
  48.2 0.0 collective-permute-done.6.refs_0_
  48.2 0.8 %collective-permute-done.16.refs_4_ = bf16[4,16,384]{2,1,0:T(8,128)(2,1)S(1)} collective-permute-done((bf16[4,16,384]{2,1,0:T(8,128)(2,1)S(1)}, bf16[4,16,384]{2,1,0:T(8,128)(2,1)S(1)}, u32[]{:S(2)}, u32[]{:S(2)}) %collective-permute-start.16) | collective-permute-done | bytes 49184 | tf_op jit(solution)/shard_map/ppermute | solution.py:416
  49.0 0.0 collective-permute-done.17.refs_5_
  49.0 0.2 collective-permute-done.15.refs_3_
  49.2 0.8 %shard_map.62 = bf16[4,16,3072]{2,1,0:T(8,128)(2,1)} custom-call(bf16[4,16,384]{2,1,0:T(8,128)(2,1)S(1)} %collective-permute-done.6.refs_0_, bf16[4,16,384]{2,1,0:T(8,128)(2,1)S(1)} %collective-permute-done.7.refs_1_, bf16[4,16,384]{2,1,0:T(8,128)(2,1)S(1)} %collective-permute-done.8.refs_2_, bf16[4,16,384]{2,1,0:T(8,128)(2,1)S(1)} %collective-permute-done.15.refs_3_, ...), custom_call_target="tpu_custom_call" | custom-call | tf_op jit(solution)/shard_map/pallas_call | solution.py:404
Async XLA Ops:
  0.0 9.9 %copy-start.1 = (bf16[4,16,3072]{2,1,0:T(8,128)(2,1)S(1)}, bf16[4,16,3072]{2,1,0:T(8,128)(2,1)}, u32[]{:S(2)}) copy-start(bf16[4,16,3072]{2,1,0:T(8,128)(2,1)} %refs_2_.1) | copy-start | bytes 1179652
  0.0 9.9 %copy-start = (bf16[4,16,3072]{2,1,0:T(8,128)(2,1)S(1)}, bf16[4,16,3072]{2,1,0:T(8,128)(2,1)}, u32[]{:S(2)}) copy-start(bf16[4,16,3072]{2,1,0:T(8,128)(2,1)} %refs_1_.3) | copy-start | bytes 1179652
  2.9 7.0 %copy-start.7 = (f32[8,128]{1,0:T(8,128)S(1)}, f32[8,128]{1,0:T(8,128)}, u32[]{:S(2)}) copy-start(f32[8,128]{1,0:T(8,128)} %get-tuple-element.30.refs_5_) | copy-start | bytes 12292
  2.9 12.7 %collective-permute-start = (bf16[4,16,768]{2,1,0:T(8,128)(2,1)}, bf16[4,16,768]{2,1,0:T(8,128)(2,1)S(1)}, u32[]{:S(2)}, u32[]{:S(2)}) collective-permute-start(bf16[4,16,768]{2,1,0:T(8,128)(2,1)} %get-tuple-element.34), channel_id=1, source_target_pairs={{0,4},{4,8},{8,12},{12,0},{1,5},{5,9},{9,13},{13,1},{2,6},{6,10},{... | collective-permute-start | bytes 294920 | tf_op jit(solution)/shard_map/ppermute | solution.py:416
  6.0 12.3 %collective-permute-start.1 = (bf16[4,16,768]{2,1,0:T(8,128)(2,1)}, bf16[4,16,768]{2,1,0:T(8,128)(2,1)S(1)}, u32[]{:S(2)}, u32[]{:S(2)}) collective-permute-start(bf16[4,16,768]{2,1,0:T(8,128)(2,1)} %get-tuple-element.35), channel_id=1, source_target_pairs={{0,8},{4,12},{8,0},{12,4},{1,9},{5,13},{9,1},{13,5},{2,10},{6,14},... | collective-permute-start | bytes 294920 | tf_op jit(solution)/shard_map/ppermute | solution.py:416
  8.5 1.4 %copy-start.5 = (s32[16]{0:T(128)S(1)}, s32[16]{0:T(128)}, u32[]{:S(2)}) copy-start(s32[16]{0:T(128)} %tokens_ref.5) | copy-start | bytes 196
  8.5 9.7 %collective-permute-start.2 = (bf16[4,16,768]{2,1,0:T(8,128)(2,1)}, bf16[4,16,768]{2,1,0:T(8,128)(2,1)S(1)}, u32[]{:S(2)}, u32[]{:S(2)}) collective-permute-start(bf16[4,16,768]{2,1,0:T(8,128)(2,1)} %get-tuple-element.36), channel_id=1, source_target_pairs={{0,12},{4,0},{8,4},{12,8},{1,13},{5,1},{9,5},{13,9},{2,14},{6,2},{... | collective-permute-start | bytes 294920 | tf_op jit(solution)/shard_map/ppermute | solution.py:416
  9.9 1.0 %copy-start.2 = (bf16[4,16,3072]{2,1,0:T(8,128)(2,1)S(1)}, bf16[4,16,3072]{2,1,0:T(8,128)(2,1)}, u32[]{:S(2)}) copy-start(bf16[4,16,3072]{2,1,0:T(8,128)(2,1)} %refs_0_.3) | copy-start | bytes 1179652
  10.9 0.7 %copy-start.4 = (s32[16,32]{1,0:T(8,128)S(1)}, s32[16,32]{1,0:T(8,128)}, u32[]{:S(2)}) copy-start(s32[16,32]{1,0:T(8,128)} %refs_3_.1) | copy-start | bytes 6148
  11.6 6.7 %copy-start.3 = (bf16[4,16,768]{2,1,0:T(8,128)(2,1)S(1)}, bf16[4,16,768]{2,1,0:T(8,128)(2,1)}, u32[]{:S(2)}) copy-start(bf16[4,16,768]{2,1,0:T(8,128)(2,1)} %get-tuple-element.33.refs_0_) | copy-start | bytes 294916
  14.4 10.1 %collective-permute-start.9 = (bf16[4,16,768]{2,1,0:T(8,128)(2,1)S(1)}, bf16[4,16,768]{2,1,0:T(8,128)(2,1)S(1)}, u32[]{:S(2)}, u32[]{:S(2)}) collective-permute-start(bf16[4,16,768]{2,1,0:T(8,128)(2,1)S(1)} %get-tuple-element.46), channel_id=1, source_target_pairs={{0,4},{4,8},{8,12},{12,0},{1,5},{5,9},{9,13},{13,1},{2,6},{6,10},{... | collective-permute-start | bytes 294920 | tf_op jit(solution)/shard_map/ppermute | solution.py:416
  15.1 9.9 %collective-permute-start.10 = (bf16[4,16,768]{2,1,0:T(8,128)(2,1)S(1)}, bf16[4,16,768]{2,1,0:T(8,128)(2,1)S(1)}, u32[]{:S(2)}, u32[]{:S(2)}) collective-permute-start(bf16[4,16,768]{2,1,0:T(8,128)(2,1)S(1)} %get-tuple-element.47), channel_id=1, source_target_pairs={{0,8},{4,12},{8,0},{12,4},{1,9},{5,13},{9,1},{13,5},{2,10},{6,14},... | collective-permute-start | bytes 294920 | tf_op jit(solution)/shard_map/ppermute | solution.py:416
  15.6 9.4 %collective-permute-start.11 = (bf16[4,16,768]{2,1,0:T(8,128)(2,1)S(1)}, bf16[4,16,768]{2,1,0:T(8,128)(2,1)S(1)}, u32[]{:S(2)}, u32[]{:S(2)}) collective-permute-start(bf16[4,16,768]{2,1,0:T(8,128)(2,1)S(1)} %get-tuple-element.48), channel_id=1, source_target_pairs={{0,12},{4,0},{8,4},{12,8},{1,13},{5,1},{9,5},{13,9},{2,14},{6,2},{... | collective-permute-start | bytes 294920 | tf_op jit(solution)/shard_map/ppermute | solution.py:416
  18.9 15.3 %all-to-all-start = ((bf16[4,4,16,768]{3,2,1,0:T(8,128)(2,1)}), bf16[4,4,16,768]{3,2,1,0:T(8,128)(2,1)S(1)}, u32[]{:S(2)}, u32[]{:S(2)}) async-start(bf16[4,4,16,768]{3,2,1,0:T(8,128)(2,1)} %get-tuple-element.38), calls=%async_computation | async-start | bytes 786432 | tf_op jit(solution)/shard_map/all_to_all | solution.py:450
  23.0 4.8 %collective-permute-start.4 = (bf16[1,4,16,768]{3,2,1,0:T(8,128)(2,1)S(1)}, bf16[1,4,16,768]{3,2,1,0:T(8,128)(2,1)S(1)}, u32[]{:S(2)}, u32[]{:S(2)}) collective-permute-start(bf16[1,4,16,768]{3,2,1,0:T(8,128)(2,1)S(1)} %get-tuple-element.40), channel_id=1, source_target_pairs={{0,2},{1,3},{2,0},{3,1},{4,6},{5,7},{6,4},{7,5},{8,10},{9,11},{10,... | collective-permute-start | bytes 294920 | tf_op jit(solution)/shard_map/ppermute | solution.py:416
  24.5 7.4 %collective-permute-start.5 = (bf16[2,4,16,768]{3,2,1,0:T(8,128)(2,1)S(1)}, bf16[2,4,16,768]{3,2,1,0:T(8,128)(2,1)S(1)}, u32[]{:S(2)}, u32[]{:S(2)}) collective-permute-start(bf16[2,4,16,768]{3,2,1,0:T(8,128)(2,1)S(1)} %get-tuple-element.41), channel_id=1, source_target_pairs={{0,3},{1,0},{2,1},{3,2},{4,7},{5,4},{6,5},{7,6},{8,11},{9,8},{10,9... | collective-permute-start | bytes 589832 | tf_op jit(solution)/shard_map/ppermute | solution.py:416
  24.5 7.4 %collective-permute-start.3 = (bf16[2,4,16,768]{3,2,1,0:T(8,128)(2,1)S(1)}, bf16[2,4,16,768]{3,2,1,0:T(8,128)(2,1)S(1)}, u32[]{:S(2)}, u32[]{:S(2)}) collective-permute-start(bf16[2,4,16,768]{3,2,1,0:T(8,128)(2,1)S(1)} %get-tuple-element.39.refs_4_), channel_id=1, source_target_pairs={{0,1},{1,2},{2,3},{3,0},{4,5},{5,6},{6,7},{7,4},{8,9},{9,10},{10,1... | collective-permute-start | bytes 589832 | tf_op jit(solution)/shard_map/ppermute | solution.py:416
  25.6 13.3 %collective-permute-start.13 = (bf16[1,4,16,768]{3,2,1,0:T(8,128)(2,1)S(1)}, bf16[1,4,16,768]{3,2,1,0:T(8,128)(2,1)S(1)}, u32[]{:S(2)}, u32[]{:S(2)}) collective-permute-start(bf16[1,4,16,768]{3,2,1,0:T(8,128)(2,1)S(1)} %get-tuple-element.50), channel_id=1, source_target_pairs={{0,2},{1,3},{2,0},{3,1},{4,6},{5,7},{6,4},{7,5},{8,10},{9,11},{10,... | collective-permute-start | bytes 294920 | tf_op jit(solution)/shard_map/ppermute | solution.py:416
  26.5 13.9 %collective-permute-start.12 = (bf16[2,4,16,768]{3,2,1,0:T(8,128)(2,1)S(1)}, bf16[2,4,16,768]{3,2,1,0:T(8,128)(2,1)S(1)}, u32[]{:S(2)}, u32[]{:S(2)}) collective-permute-start(bf16[2,4,16,768]{3,2,1,0:T(8,128)(2,1)S(1)} %get-tuple-element.49), channel_id=1, source_target_pairs={{0,1},{1,2},{2,3},{3,0},{4,5},{5,6},{6,7},{7,4},{8,9},{9,10},{10,1... | collective-permute-start | bytes 589832 | tf_op jit(solution)/shard_map/ppermute | solution.py:416
  27.8 6.5 %copy-start.6 = (s32[16]{0:T(128)S(1)}, s32[16]{0:T(128)}, u32[]{:S(2)}) copy-start(s32[16]{0:T(128)} %tokens_ref.5) | copy-start | bytes 196
  27.8 12.6 %collective-permute-start.14 = (bf16[2,4,16,768]{3,2,1,0:T(8,128)(2,1)S(1)}, bf16[2,4,16,768]{3,2,1,0:T(8,128)(2,1)S(1)}, u32[]{:S(2)}, u32[]{:S(2)}) collective-permute-start(bf16[2,4,16,768]{3,2,1,0:T(8,128)(2,1)S(1)} %get-tuple-element.51), channel_id=1, source_target_pairs={{0,3},{1,0},{2,1},{3,2},{4,7},{5,4},{6,5},{7,6},{8,11},{9,8},{10,9... | collective-permute-start | bytes 589832 | tf_op jit(solution)/shard_map/ppermute | solution.py:416
  35.8 7.9 %collective-permute-start.7 = (bf16[4,16,384]{2,1,0:T(8,128)(2,1)S(1)}, bf16[4,16,384]{2,1,0:T(8,128)(2,1)S(1)}, u32[]{:S(2)}, u32[]{:S(2)}) collective-permute-start(bf16[4,16,384]{2,1,0:T(8,128)(2,1)S(1)} %get-tuple-element.43), channel_id=1, source_target_pairs={{0,8},{4,12},{8,0},{12,4},{1,9},{5,13},{9,1},{13,5},{2,10},{6,14},... | collective-permute-start | bytes 147464 | tf_op jit(solution)/shard_map/ppermute | solution.py:416
  36.5 11.7 %collective-permute-start.8 = (bf16[4,16,384]{2,1,0:T(8,128)(2,1)S(1)}, bf16[4,16,384]{2,1,0:T(8,128)(2,1)S(1)}, u32[]{:S(2)}, u32[]{:S(2)}) collective-permute-start(bf16[4,16,384]{2,1,0:T(8,128)(2,1)S(1)} %get-tuple-element.44), channel_id=1, source_target_pairs={{0,4},{4,8},{8,12},{12,0},{1,5},{5,9},{9,13},{13,1},{2,6},{6,10},{... | collective-permute-start | bytes 147464 | tf_op jit(solution)/shard_map/ppermute | solution.py:416
  38.9 9.3 %collective-permute-start.6 = (bf16[4,16,384]{2,1,0:T(8,128)(2,1)S(1)}, bf16[4,16,384]{2,1,0:T(8,128)(2,1)S(1)}, u32[]{:S(2)}, u32[]{:S(2)}) collective-permute-start(bf16[4,16,384]{2,1,0:T(8,128)(2,1)S(1)} %get-tuple-element.42.refs_7_), channel_id=1, source_target_pairs={{0,12},{4,0},{8,4},{12,8},{1,13},{5,1},{9,5},{13,9},{2,14},{6,2},{... | collective-permute-start | bytes 147464 | tf_op jit(solution)/shard_map/ppermute | solution.py:416
  41.9 7.0 %collective-permute-start.16 = (bf16[4,16,384]{2,1,0:T(8,128)(2,1)S(1)}, bf16[4,16,384]{2,1,0:T(8,128)(2,1)S(1)}, u32[]{:S(2)}, u32[]{:S(2)}) collective-permute-start(bf16[4,16,384]{2,1,0:T(8,128)(2,1)S(1)} %get-tuple-element.53), channel_id=1, source_target_pairs={{0,8},{4,12},{8,0},{12,4},{1,9},{5,13},{9,1},{13,5},{2,10},{6,14},... | collective-permute-start | bytes 147464 | tf_op jit(solution)/shard_map/ppermute | solution.py:416
  42.6 6.4 %collective-permute-start.17 = (bf16[4,16,384]{2,1,0:T(8,128)(2,1)S(1)}, bf16[4,16,384]{2,1,0:T(8,128)(2,1)S(1)}, u32[]{:S(2)}, u32[]{:S(2)}) collective-permute-start(bf16[4,16,384]{2,1,0:T(8,128)(2,1)S(1)} %get-tuple-element.54), channel_id=1, source_target_pairs={{0,4},{4,8},{8,12},{12,0},{1,5},{5,9},{9,13},{13,1},{2,6},{6,10},{... | collective-permute-start | bytes 147464 | tf_op jit(solution)/shard_map/ppermute | solution.py:416
  43.8 5.4 %collective-permute-start.15 = (bf16[4,16,384]{2,1,0:T(8,128)(2,1)S(1)}, bf16[4,16,384]{2,1,0:T(8,128)(2,1)S(1)}, u32[]{:S(2)}, u32[]{:S(2)}) collective-permute-start(bf16[4,16,384]{2,1,0:T(8,128)(2,1)S(1)} %get-tuple-element.52.refs_14_), channel_id=1, source_target_pairs={{0,12},{4,0},{8,4},{12,8},{1,13},{5,1},{9,5},{13,9},{2,14},{6,2},{... | collective-permute-start | bytes 147464 | tf_op jit(solution)/shard_map/ppermute | solution.py:416

commit v2 on v1

--- a/solution.py
+++ b/solution.py
@@ -336,18 +336,17 @@
         )
 
     heads = len(place_of)
-    dots, mixed = products(0), []
-    for h in range(heads):
-        ahead = products(h + 1) if h + 1 < heads else None
-        dots = dots.reshape(blocks, rows, -1) + bias
-        peak = jnp.max(dots, axis=-1, keepdims=True)
-        weights = jnp.exp2((dots - peak) * (SCORE_SCALE * LOG2E))
-        inverse = 1.0 / jnp.sum(weights, axis=-1, keepdims=True)
-        weights_half = weights.astype(jnp.bfloat16).reshape(blocks * rows, -1)
-        part = jnp.dot(weights_half, gathered(1, h), preferred_element_type=jnp.float32)
-        mixed.append(part * inverse.reshape(blocks * rows, 1))
-        dots = ahead
-    mixed = jnp.concatenate(mixed, axis=0)
+    dots = jnp.concatenate([products(h) for h in range(heads)], axis=0)
+    dots = dots.reshape(heads, blocks, rows, -1) + bias
+    peak = jnp.max(dots, axis=-1, keepdims=True)
+    weights = jnp.exp2((dots - peak) * (SCORE_SCALE * LOG2E))
+    inverse = 1.0 / jnp.sum(weights, axis=-1, keepdims=True)
+    weights_half = weights.astype(jnp.bfloat16).reshape(heads, blocks * rows, -1)
+    mixed = [
+        jnp.dot(weights_half[h], gathered(1, h), preferred_element_type=jnp.float32)
+        for h in range(heads)
+    ]
+    mixed = jnp.concatenate(mixed, axis=0) * inverse.reshape(heads * blocks * rows, 1)
     sign = sign_matrix()
     high = mixed.astype(jnp.bfloat16)
     low = (mixed - high.astype(jnp.float32)).astype(jnp.bfloat16)

time: 50.2 us -> 50.1 us (level)
  Pallas kernels: 12.5 us -> 11.9 us
    pallas_call x3, Pallas kernels: 4.93 us -> 4.35 us  [attend(): pl.pallas_call(functools.partial(attend_kernel, (count_head, count_tm), h...]
  transfers between devices with their start and end apart: 19 -> 19, of which waited for: 5 -> 5; matrix products, arithmetic and copies ran while one was open for 0% -> 0% of each run, Pallas kernels for 18% -> 17%
where the time goes in v2:
time: 50.1 us; the launch traced here: 49.9 us
  starting transfers between devices  28 us (56%)
  Pallas kernels  11.9 us (24%)
  waiting for transfers between devices  8.07 us (16%)
  local copies, waits for them, and re-layouts  1.71 us (3%)
    ppermute x18, starting transfers between devices, shifted(): lax.ppermute(array, axis, [(i, (i + distance) % count) for i in range(cou...  23.9 us
    ppermute x18, waiting for transfers between devices, shifted(): lax.ppermute(array, axis, [(i, (i + distance) % count) for i in range(cou...  5.76 us
    pallas_call x3, Pallas kernels, attend(): pl.pallas_call(functools.partial(attend_kernel, (count_head, count_tm), h...  4.35 us
    all_to_all x1, starting transfers between devices, shards(): lax.all_to_all(query, 'head', split_axis=0, concat_axis=0, tiled=True)  4.13 us
    pallas_call x1, Pallas kernels, rotate_pieces(): pl.pallas_call(functools.partial(rotate_kernel, message, sources, count_h...  2.86 us
    pallas_call x1, Pallas kernels, plan(): pl.pallas_call(functools.partial(plan_kernel, messages, count_head, count...  2.76 us
    all_to_all x1, waiting for transfers between devices, shards(): lax.all_to_all(query, 'head', split_axis=0, concat_axis=0, tiled=True)  2.32 us
    unnamed x16, local copies, waits for them, and re-layouts  1.71 us
  transfers between devices with their start and end apart: 19, of which 5 were waited for; matrix products, arithmetic and copies ran while one was open for 0% of the time, Pallas kernels for 17%

profile of v2, /device:TPU:0, one launch (start us, length us, event | category | flops | bytes accessed | tf_op | source)
XLA Modules:
  0.0 49.9 jit_solution(7045034898084317138)
XLA Ops:
  0.0 0.0 copy-start.1
  0.0 0.0 copy-start
  0.0 2.9 %shard_map.55 = (bf16[4,16,768]{2,1,0:T(8,128)(2,1)}, bf16[4,16,768]{2,1,0:T(8,128)(2,1)}, bf16[4,16,768]{2,1,0:T(8,128)(2,1)}, bf16[4,16,768]{2,1,0:T(8,128)(2,1)}, f32[8,128]{1,0:T(8,128)}) custom-call(bf16[4,16,3072]{2,1,0:T(8,128)(2,1)} %refs_1_.3, bf16[4,16,3072]{2,1,0:T(8,128)(2,1)} %refs_2_.1), custom_call_target="tpu_custom_call" | custom-call | tf_op jit(solution)/shard_map/pallas_call | solution.py:114
  2.9 0.0 copy-start.7
  2.9 3.1 %collective-permute-start = (bf16[4,16,768]{2,1,0:T(8,128)(2,1)}, bf16[4,16,768]{2,1,0:T(8,128)(2,1)S(1)}, u32[]{:S(2)}, u32[]{:S(2)}) collective-permute-start(bf16[4,16,768]{2,1,0:T(8,128)(2,1)} %get-tuple-element.34), channel_id=1, source_target_pairs={{0,4},{4,8},{8,12},{12,0},{1,5},{5,9},{9,13},{13,1},{2,6},{6,10},{... | collective-permute-start | bytes 294920 | tf_op jit(solution)/shard_map/ppermute | solution.py:415
  6.0 2.6 %collective-permute-start.1 = (bf16[4,16,768]{2,1,0:T(8,128)(2,1)}, bf16[4,16,768]{2,1,0:T(8,128)(2,1)S(1)}, u32[]{:S(2)}, u32[]{:S(2)}) collective-permute-start(bf16[4,16,768]{2,1,0:T(8,128)(2,1)} %get-tuple-element.35), channel_id=1, source_target_pairs={{0,8},{4,12},{8,0},{12,4},{1,9},{5,13},{9,1},{13,5},{2,10},{6,14},... | collective-permute-start | bytes 294920 | tf_op jit(solution)/shard_map/ppermute | solution.py:415
  8.5 0.0 copy-start.5
  8.5 1.3 %collective-permute-start.2 = (bf16[4,16,768]{2,1,0:T(8,128)(2,1)}, bf16[4,16,768]{2,1,0:T(8,128)(2,1)S(1)}, u32[]{:S(2)}, u32[]{:S(2)}) collective-permute-start(bf16[4,16,768]{2,1,0:T(8,128)(2,1)} %get-tuple-element.36), channel_id=1, source_target_pairs={{0,12},{4,0},{8,4},{12,8},{1,13},{5,1},{9,5},{13,9},{2,14},{6,2},{... | collective-permute-start | bytes 294920 | tf_op jit(solution)/shard_map/ppermute | solution.py:415
  9.9 0.0 copy-done.1
  9.9 0.0 copy-done
  9.9 0.0 copy-done.7
  9.9 0.0 copy-done.5
  9.9 0.0 copy-start.2
  9.9 1.0 %copy-done.2 = bf16[4,16,3072]{2,1,0:T(8,128)(2,1)S(1)} copy-done((bf16[4,16,3072]{2,1,0:T(8,128)(2,1)S(1)}, bf16[4,16,3072]{2,1,0:T(8,128)(2,1)}, u32[]{:S(2)}) %copy-start.2) | copy-done | bytes 393240
  10.9 0.0 copy-start.4
  10.9 0.7 %copy-done.4 = s32[16,32]{1,0:T(8,128)S(1)} copy-done((s32[16,32]{1,0:T(8,128)S(1)}, s32[16,32]{1,0:T(8,128)}, u32[]{:S(2)}) %copy-start.4) | copy-done | bytes 2072
  11.6 0.0 copy-start.3
  11.6 2.8 %shard_map.56 = (s32[8]{0:T(128)S(1)}, f32[4,576]{1,0:T(4,128)S(1)}, bf16[4,4,16,768]{3,2,1,0:T(8,128)(2,1)}, bf16[4,16,768]{2,1,0:T(8,128)(2,1)S(1)}, bf16[4,16...) custom-call(bf16[4,16,3072]{2,1,0:T(8,128)(2,1)S(1)} %copy-done.2, ...), custom_call_target="tpu_custom_call" | custom-call | tf_op jit(solution)/shard_map/pallas_call | solution.py:281
  14.4 0.7 %collective-permute-start.9 = (bf16[4,16,768]{2,1,0:T(8,128)(2,1)S(1)}, bf16[4,16,768]{2,1,0:T(8,128)(2,1)S(1)}, u32[]{:S(2)}, u32[]{:S(2)}) collective-permute-start(bf16[4,16,768]{2,1,0:T(8,128)(2,1)S(1)} %get-tuple-element.46), channel_id=1, source_target_pairs={{0,4},{4,8},{8,12},{12,0},{1,5},{5,9},{9,13},{13,1},{2,6},{6,10},{... | collective-permute-start | bytes 294920 | tf_op jit(solution)/shard_map/ppermute | solution.py:415
  15.1 0.5 %collective-permute-start.10 = (bf16[4,16,768]{2,1,0:T(8,128)(2,1)S(1)}, bf16[4,16,768]{2,1,0:T(8,128)(2,1)S(1)}, u32[]{:S(2)}, u32[]{:S(2)}) collective-permute-start(bf16[4,16,768]{2,1,0:T(8,128)(2,1)S(1)} %get-tuple-element.47), channel_id=1, source_target_pairs={{0,8},{4,12},{8,0},{12,4},{1,9},{5,13},{9,1},{13,5},{2,10},{6,14},... | collective-permute-start | bytes 294920 | tf_op jit(solution)/shard_map/ppermute | solution.py:415
  15.6 0.0 collective-permute-done.refs_1_
  15.6 2.6 %collective-permute-start.11 = (bf16[4,16,768]{2,1,0:T(8,128)(2,1)S(1)}, bf16[4,16,768]{2,1,0:T(8,128)(2,1)S(1)}, u32[]{:S(2)}, u32[]{:S(2)}) collective-permute-start(bf16[4,16,768]{2,1,0:T(8,128)(2,1)S(1)} %get-tuple-element.48), channel_id=1, source_target_pairs={{0,12},{4,0},{8,4},{12,8},{1,13},{5,1},{9,5},{13,9},{2,14},{6,2},{... | collective-permute-start | bytes 294920 | tf_op jit(solution)/shard_map/ppermute | solution.py:415
  18.3 0.0 collective-permute-done.1.refs_2_
  18.3 0.0 collective-permute-done.2.refs_3_
  18.3 0.0 copy-done.3
  18.3 0.6 %shard_map.57 = (bf16[2,4,16,768]{3,2,1,0:T(8,128)(2,1)S(1)}, bf16[1,4,16,768]{3,2,1,0:T(8,128)(2,1)S(1)}, bf16[2,4,16,768]{3,2,1,0:T(8,128)(2,1)S(1)}, bf16[4,4,16,768]{3,2,1,0:T(8,128)(2,1)}) custom-call(s32[8]{0:T(128)S(1)} %get-tuple-element.32.picks_ref, bf16[4,16,768]{2,1,0:T(8,128)(2,1)S(1)} %copy-done.3, ...), custom_call_target="tpu_custom_call", output_to_operand_aliasing={{3}: (5, {})} | custom-call | flops 99999997952 | tf_op jit(solution)/shard_map/pallas_call | solution.py:153
  18.9 4.1 %all-to-all-start = ((bf16[4,4,16,768]{3,2,1,0:T(8,128)(2,1)}), bf16[4,4,16,768]{3,2,1,0:T(8,128)(2,1)S(1)}, u32[]{:S(2)}, u32[]{:S(2)}) async-start(bf16[4,4,16,768]{3,2,1,0:T(8,128)(2,1)} %get-tuple-element.38), calls=%async_computation | async-start | bytes 786432 | tf_op jit(solution)/shard_map/all_to_all | solution.py:449
  23.0 1.5 %collective-permute-start.4 = (bf16[1,4,16,768]{3,2,1,0:T(8,128)(2,1)S(1)}, bf16[1,4,16,768]{3,2,1,0:T(8,128)(2,1)S(1)}, u32[]{:S(2)}, u32[]{:S(2)}) collective-permute-start(bf16[1,4,16,768]{3,2,1,0:T(8,128)(2,1)S(1)} %get-tuple-element.40), channel_id=1, source_target_pairs={{0,2},{1,3},{2,0},{3,1},{4,6},{5,7},{6,4},{7,5},{8,10},{9,11},{10,... | collective-permute-start | bytes 294920 | tf_op jit(solution)/shard_map/ppermute | solution.py:415
  24.5 0.0 collective-permute-start.5
  24.5 0.0 collective-permute-done.9.refs_1_.refs_8_
  24.5 0.5 %collective-permute-start.3 = (bf16[2,4,16,768]{3,2,1,0:T(8,128)(2,1)S(1)}, bf16[2,4,16,768]{3,2,1,0:T(8,128)(2,1)S(1)}, u32[]{:S(2)}, u32[]{:S(2)}) collective-permute-start(bf16[2,4,16,768]{3,2,1,0:T(8,128)(2,1)S(1)} %get-tuple-element.39.refs_4_), channel_id=1, source_target_pairs={{0,1},{1,2},{2,3},{3,0},{4,5},{5,6},{6,7},{7,4},{8,9},{9,10},{10,1... | collective-permute-start | bytes 589832 | tf_op jit(solution)/shard_map/ppermute | solution.py:415
  25.0 0.0 collective-permute-done.10.refs_2_.refs_9_
  25.0 0.0 collective-permute-done.11.refs_3_.refs_10_
  25.0 0.6 %shard_map.59 = (bf16[2,4,16,768]{3,2,1,0:T(8,128)(2,1)S(1)}, bf16[1,4,16,768]{3,2,1,0:T(8,128)(2,1)S(1)}, bf16[2,4,16,768]{3,2,1,0:T(8,128)(2,1)S(1)}) custom-call(s32[8]{0:T(128)S(1)} %get-tuple-element.32.picks_ref, bf16[4,16,768]{2,1,0:T(8,128)(2,1)S(1)} %get-tuple-element.45.refs_0_.refs_7_, ...), custom_call_target="tpu_custom_call" | custom-call | flops 99999997952 | tf_op jit(solution)/shard_map/pallas_call | solution.py:153
  25.6 0.8 %collective-permute-start.13 = (bf16[1,4,16,768]{3,2,1,0:T(8,128)(2,1)S(1)}, bf16[1,4,16,768]{3,2,1,0:T(8,128)(2,1)S(1)}, u32[]{:S(2)}, u32[]{:S(2)}) collective-permute-start(bf16[1,4,16,768]{3,2,1,0:T(8,128)(2,1)S(1)} %get-tuple-element.50), channel_id=1, source_target_pairs={{0,2},{1,3},{2,0},{3,1},{4,6},{5,7},{6,4},{7,5},{8,10},{9,11},{10,... | collective-permute-start | bytes 294920 | tf_op jit(solution)/shard_map/ppermute | solution.py:415
  26.5 0.6 %collective-permute-start.12 = (bf16[2,4,16,768]{3,2,1,0:T(8,128)(2,1)S(1)}, bf16[2,4,16,768]{3,2,1,0:T(8,128)(2,1)S(1)}, u32[]{:S(2)}, u32[]{:S(2)}) collective-permute-start(bf16[2,4,16,768]{3,2,1,0:T(8,128)(2,1)S(1)} %get-tuple-element.49), channel_id=1, source_target_pairs={{0,1},{1,2},{2,3},{3,0},{4,5},{5,6},{6,7},{7,4},{8,9},{9,10},{10,1... | collective-permute-start | bytes 589832 | tf_op jit(solution)/shard_map/ppermute | solution.py:415
  27.0 0.7 %collective-permute-done.4.refs_5_ = bf16[1,4,16,768]{3,2,1,0:T(8,128)(2,1)S(1)} collective-permute-done((bf16[1,4,16,768]{3,2,1,0:T(8,128)(2,1)S(1)}, bf16[1,4,16,768]{3,2,1,0:T(8,128)(2,1)S(1)}, u32[]{:S(2)}, u32[]{:S(2)}) %collective-permute-start.4) | collective-permute-done | bytes 98336 | tf_op jit(solution)/shard_map/ppermute | solution.py:415
  27.8 0.0 copy-start.6
  27.8 0.5 collective-permute-start.14
  28.2 3.7 %collective-permute-done.5.refs_6_ = bf16[2,4,16,768]{3,2,1,0:T(8,128)(2,1)S(1)} collective-permute-done((bf16[2,4,16,768]{3,2,1,0:T(8,128)(2,1)S(1)}, bf16[2,4,16,768]{3,2,1,0:T(8,128)(2,1)S(1)}, u32[]{:S(2)}, u32[]{:S(2)}) %collective-permute-start.5) | collective-permute-done | bytes 196640 | tf_op jit(solution)/shard_map/ppermute | solution.py:415
  31.9 0.0 collective-permute-done.3.refs_4_
  31.9 2.3 %all-to-all-done.query_ref = bf16[4,4,16,768]{3,2,1,0:T(8,128)(2,1)S(1)} async-done(((bf16[4,4,16,768]{3,2,1,0:T(8,128)(2,1)}), bf16[4,4,16,768]{3,2,1,0:T(8,128)(2,1)S(1)}, u32[]{:S(2)}, u32[]{:S(2)}) %all-to-all-start) | async-done | bytes 393248 | tf_op jit(solution)/shard_map/all_to_all | solution.py:449
  34.2 0.0 copy-done.6
  34.2 1.5 %shard_map.58 = (bf16[4,16,384]{2,1,0:T(8,128)(2,1)S(1)}, bf16[4,16,384]{2,1,0:T(8,128)(2,1)S(1)}, bf16[4,16,384]{2,1,0:T(8,128)(2,1)S(1)}) custom-call(s32[16]{0:T(128)S(1)} %copy-done.6, f32[4,576]{1,0:T(4,128)S(1)} %get-tuple-element.31.bias_ref, bf16[4,4,16,768]{3,2,1,0:T(8,128)(2,1)S(1)} %all-to-all-done.query_ref, bf16[4,16,768]{2,1,0:T(8,128)(2,1)S(1)} %copy-done.3, ...), custom_call_target="tpu_custom_call" | custom-call | flops 99999997952 | tf_op jit(solution)/shard_map/pallas_call | solution.py:372
  35.7 0.7 %collective-permute-start.7 = (bf16[4,16,384]{2,1,0:T(8,128)(2,1)S(1)}, bf16[4,16,384]{2,1,0:T(8,128)(2,1)S(1)}, u32[]{:S(2)}, u32[]{:S(2)}) collective-permute-start(bf16[4,16,384]{2,1,0:T(8,128)(2,1)S(1)} %get-tuple-element.43), channel_id=1, source_target_pairs={{0,8},{4,12},{8,0},{12,4},{1,9},{5,13},{9,1},{13,5},{2,10},{6,14},... | collective-permute-start | bytes 147464 | tf_op jit(solution)/shard_map/ppermute | solution.py:415
  36.4 2.4 %collective-permute-start.8 = (bf16[4,16,384]{2,1,0:T(8,128)(2,1)S(1)}, bf16[4,16,384]{2,1,0:T(8,128)(2,1)S(1)}, u32[]{:S(2)}, u32[]{:S(2)}) collective-permute-start(bf16[4,16,384]{2,1,0:T(8,128)(2,1)S(1)} %get-tuple-element.44), channel_id=1, source_target_pairs={{0,4},{4,8},{8,12},{12,0},{1,5},{5,9},{9,13},{13,1},{2,6},{6,10},{... | collective-permute-start | bytes 147464 | tf_op jit(solution)/shard_map/ppermute | solution.py:415
  38.8 0.0 collective-permute-done.13.refs_5_.refs_12_
  38.8 1.4 %collective-permute-start.6 = (bf16[4,16,384]{2,1,0:T(8,128)(2,1)S(1)}, bf16[4,16,384]{2,1,0:T(8,128)(2,1)S(1)}, u32[]{:S(2)}, u32[]{:S(2)}) collective-permute-start(bf16[4,16,384]{2,1,0:T(8,128)(2,1)S(1)} %get-tuple-element.42.refs_7_), channel_id=1, source_target_pairs={{0,12},{4,0},{8,4},{12,8},{1,13},{5,1},{9,5},{13,9},{2,14},{6,2},{... | collective-permute-start | bytes 147464 | tf_op jit(solution)/shard_map/ppermute | solution.py:415
  40.2 0.0 collective-permute-done.12.refs_4_.refs_11_
  40.2 0.0 collective-permute-done.14.refs_6_.refs_13_
  40.2 1.5 %shard_map.60 = (bf16[4,16,384]{2,1,0:T(8,128)(2,1)S(1)}, bf16[4,16,384]{2,1,0:T(8,128)(2,1)S(1)}, bf16[4,16,384]{2,1,0:T(8,128)(2,1)S(1)}) custom-call(s32[16]{0:T(128)S(1)} %copy-done.6, f32[4,576]{1,0:T(4,128)S(1)} %get-tuple-element.31.bias_ref, bf16[4,4,16,768]{3,2,1,0:T(8,128)(2,1)S(1)} %all-to-all-done.query_ref, ...), custom_call_target="tpu_custom_call" | custom-call | tf_op jit(solution)/shard_map/pallas_call | solution.py:372
  41.7 0.8 %collective-permute-start.16 = (bf16[4,16,384]{2,1,0:T(8,128)(2,1)S(1)}, bf16[4,16,384]{2,1,0:T(8,128)(2,1)S(1)}, u32[]{:S(2)}, u32[]{:S(2)}) collective-permute-start(bf16[4,16,384]{2,1,0:T(8,128)(2,1)S(1)} %get-tuple-element.53), channel_id=1, source_target_pairs={{0,8},{4,12},{8,0},{12,4},{1,9},{5,13},{9,1},{13,5},{2,10},{6,14},... | collective-permute-start | bytes 147464 | tf_op jit(solution)/shard_map/ppermute | solution.py:415
  42.5 1.2 %collective-permute-start.17 = (bf16[4,16,384]{2,1,0:T(8,128)(2,1)S(1)}, bf16[4,16,384]{2,1,0:T(8,128)(2,1)S(1)}, u32[]{:S(2)}, u32[]{:S(2)}) collective-permute-start(bf16[4,16,384]{2,1,0:T(8,128)(2,1)S(1)} %get-tuple-element.54), channel_id=1, source_target_pairs={{0,4},{4,8},{8,12},{12,0},{1,5},{5,9},{9,13},{13,1},{2,6},{6,10},{... | collective-permute-start | bytes 147464 | tf_op jit(solution)/shard_map/ppermute | solution.py:415
  43.7 0.0 collective-permute-done.7.refs_1_
  43.7 2.7 %collective-permute-start.15 = (bf16[4,16,384]{2,1,0:T(8,128)(2,1)S(1)}, bf16[4,16,384]{2,1,0:T(8,128)(2,1)S(1)}, u32[]{:S(2)}, u32[]{:S(2)}) collective-permute-start(bf16[4,16,384]{2,1,0:T(8,128)(2,1)S(1)} %get-tuple-element.52.refs_14_), channel_id=1, source_target_pairs={{0,12},{4,0},{8,4},{12,8},{1,13},{5,1},{9,5},{13,9},{2,14},{6,2},{... | collective-permute-start | bytes 147464 | tf_op jit(solution)/shard_map/ppermute | solution.py:415
  46.3 1.4 %shard_map.61.refs_6_ = bf16[4,16,768]{2,1,0:T(8,128)(2,1)S(1)} custom-call(s32[16]{0:T(128)S(1)} %copy-done.6, f32[4,576]{1,0:T(4,128)S(1)} %get-tuple-element.31.bias_ref, bf16[4,4,16,768]{3,2,1,0:T(8,128)(2,1)S(1)} %all-to-all-done.query_ref, bf16[4,16,768]{2,1,0:T(8,128)(2,1)S(1)} %copy-done.3, bf16[4,16,768]{2,1,0:T(8,128)(2,1)S(1)} %collective-permute-done.refs_1_, ...), custom_call_target="tpu_custom_call" | custom-call | tf_op jit(solution)/shard_map/pallas_call | solution.py:372
  47.7 0.0 collective-permute-done.8.refs_2_
  47.7 0.0 collective-permute-done.6.refs_0_
  47.7 1.1 %collective-permute-done.16.refs_4_ = bf16[4,16,384]{2,1,0:T(8,128)(2,1)S(1)} collective-permute-done((bf16[4,16,384]{2,1,0:T(8,128)(2,1)S(1)}, bf16[4,16,384]{2,1,0:T(8,128)(2,1)S(1)}, u32[]{:S(2)}, u32[]{:S(2)}) %collective-permute-start.16) | collective-permute-done | bytes 49184 | tf_op jit(solution)/shard_map/ppermute | solution.py:415
  48.8 0.0 collective-permute-done.17.refs_5_
  48.8 0.2 collective-permute-done.15.refs_3_
  49.1 0.8 %shard_map.62 = bf16[4,16,3072]{2,1,0:T(8,128)(2,1)} custom-call(bf16[4,16,384]{2,1,0:T(8,128)(2,1)S(1)} %collective-permute-done.6.refs_0_, bf16[4,16,384]{2,1,0:T(8,128)(2,1)S(1)} %collective-permute-done.7.refs_1_, bf16[4,16,384]{2,1,0:T(8,128)(2,1)S(1)} %collective-permute-done.8.refs_2_, bf16[4,16,384]{2,1,0:T(8,128)(2,1)S(1)} %collective-permute-done.15.refs_3_, ...), custom_call_target="tpu_custom_call" | custom-call | tf_op jit(solution)/shard_map/pallas_call | solution.py:403
Async XLA Ops:
  0.0 9.9 %copy-start.1 = (bf16[4,16,3072]{2,1,0:T(8,128)(2,1)S(1)}, bf16[4,16,3072]{2,1,0:T(8,128)(2,1)}, u32[]{:S(2)}) copy-start(bf16[4,16,3072]{2,1,0:T(8,128)(2,1)} %refs_2_.1) | copy-start | bytes 1179652
  0.0 9.9 %copy-start = (bf16[4,16,3072]{2,1,0:T(8,128)(2,1)S(1)}, bf16[4,16,3072]{2,1,0:T(8,128)(2,1)}, u32[]{:S(2)}) copy-start(bf16[4,16,3072]{2,1,0:T(8,128)(2,1)} %refs_1_.3) | copy-start | bytes 1179652
  2.9 7.0 %copy-start.7 = (f32[8,128]{1,0:T(8,128)S(1)}, f32[8,128]{1,0:T(8,128)}, u32[]{:S(2)}) copy-start(f32[8,128]{1,0:T(8,128)} %get-tuple-element.30.refs_5_) | copy-start | bytes 12292
  2.9 12.7 %collective-permute-start = (bf16[4,16,768]{2,1,0:T(8,128)(2,1)}, bf16[4,16,768]{2,1,0:T(8,128)(2,1)S(1)}, u32[]{:S(2)}, u32[]{:S(2)}) collective-permute-start(bf16[4,16,768]{2,1,0:T(8,128)(2,1)} %get-tuple-element.34), channel_id=1, source_target_pairs={{0,4},{4,8},{8,12},{12,0},{1,5},{5,9},{9,13},{13,1},{2,6},{6,10},{... | collective-permute-start | bytes 294920 | tf_op jit(solution)/shard_map/ppermute | solution.py:415
  6.0 12.3 %collective-permute-start.1 = (bf16[4,16,768]{2,1,0:T(8,128)(2,1)}, bf16[4,16,768]{2,1,0:T(8,128)(2,1)S(1)}, u32[]{:S(2)}, u32[]{:S(2)}) collective-permute-start(bf16[4,16,768]{2,1,0:T(8,128)(2,1)} %get-tuple-element.35), channel_id=1, source_target_pairs={{0,8},{4,12},{8,0},{12,4},{1,9},{5,13},{9,1},{13,5},{2,10},{6,14},... | collective-permute-start | bytes 294920 | tf_op jit(solution)/shard_map/ppermute | solution.py:415
  8.5 1.4 %copy-start.5 = (s32[16]{0:T(128)S(1)}, s32[16]{0:T(128)}, u32[]{:S(2)}) copy-start(s32[16]{0:T(128)} %tokens_ref.5) | copy-start | bytes 196
  8.5 9.7 %collective-permute-start.2 = (bf16[4,16,768]{2,1,0:T(8,128)(2,1)}, bf16[4,16,768]{2,1,0:T(8,128)(2,1)S(1)}, u32[]{:S(2)}, u32[]{:S(2)}) collective-permute-start(bf16[4,16,768]{2,1,0:T(8,128)(2,1)} %get-tuple-element.36), channel_id=1, source_target_pairs={{0,12},{4,0},{8,4},{12,8},{1,13},{5,1},{9,5},{13,9},{2,14},{6,2},{... | collective-permute-start | bytes 294920 | tf_op jit(solution)/shard_map/ppermute | solution.py:415
  9.9 1.0 %copy-start.2 = (bf16[4,16,3072]{2,1,0:T(8,128)(2,1)S(1)}, bf16[4,16,3072]{2,1,0:T(8,128)(2,1)}, u32[]{:S(2)}) copy-start(bf16[4,16,3072]{2,1,0:T(8,128)(2,1)} %refs_0_.3) | copy-start | bytes 1179652
  10.9 0.7 %copy-start.4 = (s32[16,32]{1,0:T(8,128)S(1)}, s32[16,32]{1,0:T(8,128)}, u32[]{:S(2)}) copy-start(s32[16,32]{1,0:T(8,128)} %refs_3_.1) | copy-start | bytes 6148
  11.6 6.7 %copy-start.3 = (bf16[4,16,768]{2,1,0:T(8,128)(2,1)S(1)}, bf16[4,16,768]{2,1,0:T(8,128)(2,1)}, u32[]{:S(2)}) copy-start(bf16[4,16,768]{2,1,0:T(8,128)(2,1)} %get-tuple-element.33.refs_0_) | copy-start | bytes 294916
  14.4 10.1 %collective-permute-start.9 = (bf16[4,16,768]{2,1,0:T(8,128)(2,1)S(1)}, bf16[4,16,768]{2,1,0:T(8,128)(2,1)S(1)}, u32[]{:S(2)}, u32[]{:S(2)}) collective-permute-start(bf16[4,16,768]{2,1,0:T(8,128)(2,1)S(1)} %get-tuple-element.46), channel_id=1, source_target_pairs={{0,4},{4,8},{8,12},{12,0},{1,5},{5,9},{9,13},{13,1},{2,6},{6,10},{... | collective-permute-start | bytes 294920 | tf_op jit(solution)/shard_map/ppermute | solution.py:415
  15.1 9.9 %collective-permute-start.10 = (bf16[4,16,768]{2,1,0:T(8,128)(2,1)S(1)}, bf16[4,16,768]{2,1,0:T(8,128)(2,1)S(1)}, u32[]{:S(2)}, u32[]{:S(2)}) collective-permute-start(bf16[4,16,768]{2,1,0:T(8,128)(2,1)S(1)} %get-tuple-element.47), channel_id=1, source_target_pairs={{0,8},{4,12},{8,0},{12,4},{1,9},{5,13},{9,1},{13,5},{2,10},{6,14},... | collective-permute-start | bytes 294920 | tf_op jit(solution)/shard_map/ppermute | solution.py:415
  15.6 9.4 %collective-permute-start.11 = (bf16[4,16,768]{2,1,0:T(8,128)(2,1)S(1)}, bf16[4,16,768]{2,1,0:T(8,128)(2,1)S(1)}, u32[]{:S(2)}, u32[]{:S(2)}) collective-permute-start(bf16[4,16,768]{2,1,0:T(8,128)(2,1)S(1)} %get-tuple-element.48), channel_id=1, source_target_pairs={{0,12},{4,0},{8,4},{12,8},{1,13},{5,1},{9,5},{13,9},{2,14},{6,2},{... | collective-permute-start | bytes 294920 | tf_op jit(solution)/shard_map/ppermute | solution.py:415
  18.9 15.3 %all-to-all-start = ((bf16[4,4,16,768]{3,2,1,0:T(8,128)(2,1)}), bf16[4,4,16,768]{3,2,1,0:T(8,128)(2,1)S(1)}, u32[]{:S(2)}, u32[]{:S(2)}) async-start(bf16[4,4,16,768]{3,2,1,0:T(8,128)(2,1)} %get-tuple-element.38), calls=%async_computation | async-start | bytes 786432 | tf_op jit(solution)/shard_map/all_to_all | solution.py:449
  23.0 4.8 %collective-permute-start.4 = (bf16[1,4,16,768]{3,2,1,0:T(8,128)(2,1)S(1)}, bf16[1,4,16,768]{3,2,1,0:T(8,128)(2,1)S(1)}, u32[]{:S(2)}, u32[]{:S(2)}) collective-permute-start(bf16[1,4,16,768]{3,2,1,0:T(8,128)(2,1)S(1)} %get-tuple-element.40), channel_id=1, source_target_pairs={{0,2},{1,3},{2,0},{3,1},{4,6},{5,7},{6,4},{7,5},{8,10},{9,11},{10,... | collective-permute-start | bytes 294920 | tf_op jit(solution)/shard_map/ppermute | solution.py:415
  24.5 7.4 %collective-permute-start.5 = (bf16[2,4,16,768]{3,2,1,0:T(8,128)(2,1)S(1)}, bf16[2,4,16,768]{3,2,1,0:T(8,128)(2,1)S(1)}, u32[]{:S(2)}, u32[]{:S(2)}) collective-permute-start(bf16[2,4,16,768]{3,2,1,0:T(8,128)(2,1)S(1)} %get-tuple-element.41), channel_id=1, source_target_pairs={{0,3},{1,0},{2,1},{3,2},{4,7},{5,4},{6,5},{7,6},{8,11},{9,8},{10,9... | collective-permute-start | bytes 589832 | tf_op jit(solution)/shard_map/ppermute | solution.py:415
  24.5 7.4 %collective-permute-start.3 = (bf16[2,4,16,768]{3,2,1,0:T(8,128)(2,1)S(1)}, bf16[2,4,16,768]{3,2,1,0:T(8,128)(2,1)S(1)}, u32[]{:S(2)}, u32[]{:S(2)}) collective-permute-start(bf16[2,4,16,768]{3,2,1,0:T(8,128)(2,1)S(1)} %get-tuple-element.39.refs_4_), channel_id=1, source_target_pairs={{0,1},{1,2},{2,3},{3,0},{4,5},{5,6},{6,7},{7,4},{8,9},{9,10},{10,1... | collective-permute-start | bytes 589832 | tf_op jit(solution)/shard_map/ppermute | solution.py:415
  25.6 13.2 %collective-permute-start.13 = (bf16[1,4,16,768]{3,2,1,0:T(8,128)(2,1)S(1)}, bf16[1,4,16,768]{3,2,1,0:T(8,128)(2,1)S(1)}, u32[]{:S(2)}, u32[]{:S(2)}) collective-permute-start(bf16[1,4,16,768]{3,2,1,0:T(8,128)(2,1)S(1)} %get-tuple-element.50), channel_id=1, source_target_pairs={{0,2},{1,3},{2,0},{3,1},{4,6},{5,7},{6,4},{7,5},{8,10},{9,11},{10,... | collective-permute-start | bytes 294920 | tf_op jit(solution)/shard_map/ppermute | solution.py:415
  26.5 13.8 %collective-permute-start.12 = (bf16[2,4,16,768]{3,2,1,0:T(8,128)(2,1)S(1)}, bf16[2,4,16,768]{3,2,1,0:T(8,128)(2,1)S(1)}, u32[]{:S(2)}, u32[]{:S(2)}) collective-permute-start(bf16[2,4,16,768]{3,2,1,0:T(8,128)(2,1)S(1)} %get-tuple-element.49), channel_id=1, source_target_pairs={{0,1},{1,2},{2,3},{3,0},{4,5},{5,6},{6,7},{7,4},{8,9},{9,10},{10,1... | collective-permute-start | bytes 589832 | tf_op jit(solution)/shard_map/ppermute | solution.py:415
  27.8 6.5 %copy-start.6 = (s32[16]{0:T(128)S(1)}, s32[16]{0:T(128)}, u32[]{:S(2)}) copy-start(s32[16]{0:T(128)} %tokens_ref.5) | copy-start | bytes 196
  27.8 12.5 %collective-permute-start.14 = (bf16[2,4,16,768]{3,2,1,0:T(8,128)(2,1)S(1)}, bf16[2,4,16,768]{3,2,1,0:T(8,128)(2,1)S(1)}, u32[]{:S(2)}, u32[]{:S(2)}) collective-permute-start(bf16[2,4,16,768]{3,2,1,0:T(8,128)(2,1)S(1)} %get-tuple-element.51), channel_id=1, source_target_pairs={{0,3},{1,0},{2,1},{3,2},{4,7},{5,4},{6,5},{7,6},{8,11},{9,8},{10,9... | collective-permute-start | bytes 589832 | tf_op jit(solution)/shard_map/ppermute | solution.py:415
  35.7 7.9 %collective-permute-start.7 = (bf16[4,16,384]{2,1,0:T(8,128)(2,1)S(1)}, bf16[4,16,384]{2,1,0:T(8,128)(2,1)S(1)}, u32[]{:S(2)}, u32[]{:S(2)}) collective-permute-start(bf16[4,16,384]{2,1,0:T(8,128)(2,1)S(1)} %get-tuple-element.43), channel_id=1, source_target_pairs={{0,8},{4,12},{8,0},{12,4},{1,9},{5,13},{9,1},{13,5},{2,10},{6,14},... | collective-permute-start | bytes 147464 | tf_op jit(solution)/shard_map/ppermute | solution.py:415
  36.4 11.3 %collective-permute-start.8 = (bf16[4,16,384]{2,1,0:T(8,128)(2,1)S(1)}, bf16[4,16,384]{2,1,0:T(8,128)(2,1)S(1)}, u32[]{:S(2)}, u32[]{:S(2)}) collective-permute-start(bf16[4,16,384]{2,1,0:T(8,128)(2,1)S(1)} %get-tuple-element.44), channel_id=1, source_target_pairs={{0,4},{4,8},{8,12},{12,0},{1,5},{5,9},{9,13},{13,1},{2,6},{6,10},{... | collective-permute-start | bytes 147464 | tf_op jit(solution)/shard_map/ppermute | solution.py:415
  38.8 9.0 %collective-permute-start.6 = (bf16[4,16,384]{2,1,0:T(8,128)(2,1)S(1)}, bf16[4,16,384]{2,1,0:T(8,128)(2,1)S(1)}, u32[]{:S(2)}, u32[]{:S(2)}) collective-permute-start(bf16[4,16,384]{2,1,0:T(8,128)(2,1)S(1)} %get-tuple-element.42.refs_7_), channel_id=1, source_target_pairs={{0,12},{4,0},{8,4},{12,8},{1,13},{5,1},{9,5},{13,9},{2,14},{6,2},{... | collective-permute-start | bytes 147464 | tf_op jit(solution)/shard_map/ppermute | solution.py:415
  41.7 7.1 %collective-permute-start.16 = (bf16[4,16,384]{2,1,0:T(8,128)(2,1)S(1)}, bf16[4,16,384]{2,1,0:T(8,128)(2,1)S(1)}, u32[]{:S(2)}, u32[]{:S(2)}) collective-permute-start(bf16[4,16,384]{2,1,0:T(8,128)(2,1)S(1)} %get-tuple-element.53), channel_id=1, source_target_pairs={{0,8},{4,12},{8,0},{12,4},{1,9},{5,13},{9,1},{13,5},{2,10},{6,14},... | collective-permute-start | bytes 147464 | tf_op jit(solution)/shard_map/ppermute | solution.py:415
  42.5 6.3 %collective-permute-start.17 = (bf16[4,16,384]{2,1,0:T(8,128)(2,1)S(1)}, bf16[4,16,384]{2,1,0:T(8,128)(2,1)S(1)}, u32[]{:S(2)}, u32[]{:S(2)}) collective-permute-start(bf16[4,16,384]{2,1,0:T(8,128)(2,1)S(1)} %get-tuple-element.54), channel_id=1, source_target_pairs={{0,4},{4,8},{8,12},{12,0},{1,5},{5,9},{9,13},{13,1},{2,6},{6,10},{... | collective-permute-start | bytes 147464 | tf_op jit(solution)/shard_map/ppermute | solution.py:415
  43.7 5.4 %collective-permute-start.15 = (bf16[4,16,384]{2,1,0:T(8,128)(2,1)S(1)}, bf16[4,16,384]{2,1,0:T(8,128)(2,1)S(1)}, u32[]{:S(2)}, u32[]{:S(2)}) collective-permute-start(bf16[4,16,384]{2,1,0:T(8,128)(2,1)S(1)} %get-tuple-element.52.refs_14_), channel_id=1, source_target_pairs={{0,12},{4,0},{8,4},{12,8},{1,13},{5,1},{9,5},{13,9},{2,14},{6,2},{... | collective-permute-start | bytes 147464 | tf_op jit(solution)/shard_map/ppermute | solution.py:415

commit v3 on v2

--- a/solution.py
+++ b/solution.py
@@ -438,14 +438,13 @@
         arrays, messages[1:], pair_list, block_tokens, token, count_head, count_tm
     )
     received = [piece[:1] + exchange(piece[1:], 1) for piece in [pieces] + later]
-    sent = []
+    inputs, held = [], query
     for owns, (_, size) in zip(received, parts):
-        held = sent[-1][0] if sent else query
-        picked = pick_blocks(picks, owns, (0, 2 * size), count_tm, held, not sent)
-        if not sent:
+        picked = pick_blocks(picks, owns, (0, 2 * size), count_tm, held, not inputs)
+        if not inputs:
             *picked, query = picked
-        sent.append(list(picked))
-    inputs = [(owns, forward(picked)) for owns, picked in zip(received, sent)]
+        inputs.append((owns, forward(picked)))
+        held = inputs[-1][1][len(picked) // 2]
     query = lax.all_to_all(query, "head", split_axis=0, concat_axis=0, tiled=True)
     distances, after = list(range(1, count_head)), ()
     pieces, places = [], []

time: 50.1 us -> 49.8 us (level)
  waiting for transfers between devices: 8.07 us -> 6.17 us
  starting transfers between devices: 28 us -> 29.6 us
    ppermute x18, waiting for transfers between devices: 5.76 us -> 3.62 us  [shifted(): lax.ppermute(array, axis, [(i, (i + distance) % count) for i in range(cou...]
    ppermute x18, starting transfers between devices: 23.9 us -> 25.5 us  [shifted(): lax.ppermute(array, axis, [(i, (i + distance) % count) for i in range(cou...]
  transfers between devices with their start and end apart: 19 -> 19, of which waited for: 5 -> 6; matrix products, arithmetic and copies ran while one was open for 0% -> 0% of each run, Pallas kernels for 17% -> 17%
where the time goes in v3:
time: 49.8 us; the launch traced here: 49.5 us
  starting transfers between devices  29.6 us (59%)
  Pallas kernels  11.9 us (24%)
  waiting for transfers between devices  6.17 us (12%)
  local copies, waits for them, and re-layouts  1.71 us (3%)
    ppermute x18, starting transfers between devices, shifted(): lax.ppermute(array, axis, [(i, (i + distance) % count) for i in range(cou...  25.5 us
    pallas_call x3, Pallas kernels, attend(): pl.pallas_call(functools.partial(attend_kernel, (count_head, count_tm), h...  4.35 us
    all_to_all x1, starting transfers between devices, shards(): lax.all_to_all(query, 'head', split_axis=0, concat_axis=0, tiled=True)  4.12 us
    ppermute x18, waiting for transfers between devices, shifted(): lax.ppermute(array, axis, [(i, (i + distance) % count) for i in range(cou...  3.62 us
    pallas_call x1, Pallas kernels, rotate_pieces(): pl.pallas_call(functools.partial(rotate_kernel, message, sources, count_h...  2.86 us
    pallas_call x1, Pallas kernels, plan(): pl.pallas_call(functools.partial(plan_kernel, messages, count_head, count...  2.76 us
    all_to_all x1, waiting for transfers between devices, shards(): lax.all_to_all(query, 'head', split_axis=0, concat_axis=0, tiled=True)  2.55 us
    unnamed x16, local copies, waits for them, and re-layouts  1.71 us
  transfers between devices with their start and end apart: 19, of which 6 were waited for; matrix products, arithmetic and copies ran while one was open for 0% of the time, Pallas kernels for 17%

profile of v3, /device:TPU:0, one launch (start us, length us, event | category | flops | bytes accessed | tf_op | source)
XLA Modules:
  0.0 49.5 jit_solution(2378950821652454139)
XLA Ops:
  0.0 0.0 copy-start.1
  0.0 0.0 copy-start
  0.0 2.9 %shard_map.55 = (bf16[4,16,768]{2,1,0:T(8,128)(2,1)}, bf16[4,16,768]{2,1,0:T(8,128)(2,1)}, bf16[4,16,768]{2,1,0:T(8,128)(2,1)}, bf16[4,16,768]{2,1,0:T(8,128)(2,1)}, f32[8,128]{1,0:T(8,128)}) custom-call(bf16[4,16,3072]{2,1,0:T(8,128)(2,1)} %refs_1_.3, bf16[4,16,3072]{2,1,0:T(8,128)(2,1)} %refs_2_.1), custom_call_target="tpu_custom_call" | custom-call | tf_op jit(solution)/shard_map/pallas_call | solution.py:114
  2.9 0.0 copy-start.7
  2.9 3.1 %collective-permute-start = (bf16[4,16,768]{2,1,0:T(8,128)(2,1)}, bf16[4,16,768]{2,1,0:T(8,128)(2,1)S(1)}, u32[]{:S(2)}, u32[]{:S(2)}) collective-permute-start(bf16[4,16,768]{2,1,0:T(8,128)(2,1)} %get-tuple-element.34), channel_id=1, source_target_pairs={{0,4},{4,8},{8,12},{12,0},{1,5},{5,9},{9,13},{13,1},{2,6},{6,10},{... | collective-permute-start | bytes 294920 | tf_op jit(solution)/shard_map/ppermute | solution.py:415
  6.0 2.6 %collective-permute-start.1 = (bf16[4,16,768]{2,1,0:T(8,128)(2,1)}, bf16[4,16,768]{2,1,0:T(8,128)(2,1)S(1)}, u32[]{:S(2)}, u32[]{:S(2)}) collective-permute-start(bf16[4,16,768]{2,1,0:T(8,128)(2,1)} %get-tuple-element.35), channel_id=1, source_target_pairs={{0,8},{4,12},{8,0},{12,4},{1,9},{5,13},{9,1},{13,5},{2,10},{6,14},... | collective-permute-start | bytes 294920 | tf_op jit(solution)/shard_map/ppermute | solution.py:415
  8.5 0.0 copy-start.5
  8.5 1.3 %collective-permute-start.2 = (bf16[4,16,768]{2,1,0:T(8,128)(2,1)}, bf16[4,16,768]{2,1,0:T(8,128)(2,1)S(1)}, u32[]{:S(2)}, u32[]{:S(2)}) collective-permute-start(bf16[4,16,768]{2,1,0:T(8,128)(2,1)} %get-tuple-element.36), channel_id=1, source_target_pairs={{0,12},{4,0},{8,4},{12,8},{1,13},{5,1},{9,5},{13,9},{2,14},{6,2},{... | collective-permute-start | bytes 294920 | tf_op jit(solution)/shard_map/ppermute | solution.py:415
  9.9 0.0 copy-done.1
  9.9 0.0 copy-done
  9.9 0.0 copy-done.7
  9.9 0.0 copy-done.5
  9.9 0.0 copy-start.2
  9.9 1.0 %copy-done.2 = bf16[4,16,3072]{2,1,0:T(8,128)(2,1)S(1)} copy-done((bf16[4,16,3072]{2,1,0:T(8,128)(2,1)S(1)}, bf16[4,16,3072]{2,1,0:T(8,128)(2,1)}, u32[]{:S(2)}) %copy-start.2) | copy-done | bytes 393240
  10.9 0.0 copy-start.4
  10.9 0.7 %copy-done.4 = s32[16,32]{1,0:T(8,128)S(1)} copy-done((s32[16,32]{1,0:T(8,128)S(1)}, s32[16,32]{1,0:T(8,128)}, u32[]{:S(2)}) %copy-start.4) | copy-done | bytes 2072
  11.6 0.0 copy-start.3
  11.6 2.8 %shard_map.56 = (s32[8]{0:T(128)S(1)}, f32[4,576]{1,0:T(4,128)S(1)}, bf16[4,4,16,768]{3,2,1,0:T(8,128)(2,1)}, bf16[4,16,768]{2,1,0:T(8,128)(2,1)S(1)}, bf16[4,16...) custom-call(bf16[4,16,3072]{2,1,0:T(8,128)(2,1)S(1)} %copy-done.2, ...), custom_call_target="tpu_custom_call" | custom-call | tf_op jit(solution)/shard_map/pallas_call | solution.py:281
  14.4 0.7 %collective-permute-start.9 = (bf16[4,16,768]{2,1,0:T(8,128)(2,1)S(1)}, bf16[4,16,768]{2,1,0:T(8,128)(2,1)S(1)}, u32[]{:S(2)}, u32[]{:S(2)}) collective-permute-start(bf16[4,16,768]{2,1,0:T(8,128)(2,1)S(1)} %get-tuple-element.46), channel_id=1, source_target_pairs={{0,4},{4,8},{8,12},{12,0},{1,5},{5,9},{9,13},{13,1},{2,6},{6,10},{... | collective-permute-start | bytes 294920 | tf_op jit(solution)/shard_map/ppermute | solution.py:415
  15.1 0.5 %collective-permute-start.10 = (bf16[4,16,768]{2,1,0:T(8,128)(2,1)S(1)}, bf16[4,16,768]{2,1,0:T(8,128)(2,1)S(1)}, u32[]{:S(2)}, u32[]{:S(2)}) collective-permute-start(bf16[4,16,768]{2,1,0:T(8,128)(2,1)S(1)} %get-tuple-element.47), channel_id=1, source_target_pairs={{0,8},{4,12},{8,0},{12,4},{1,9},{5,13},{9,1},{13,5},{2,10},{6,14},... | collective-permute-start | bytes 294920 | tf_op jit(solution)/shard_map/ppermute | solution.py:415
  15.6 0.0 collective-permute-done.refs_1_
  15.6 2.6 %collective-permute-start.11 = (bf16[4,16,768]{2,1,0:T(8,128)(2,1)S(1)}, bf16[4,16,768]{2,1,0:T(8,128)(2,1)S(1)}, u32[]{:S(2)}, u32[]{:S(2)}) collective-permute-start(bf16[4,16,768]{2,1,0:T(8,128)(2,1)S(1)} %get-tuple-element.48), channel_id=1, source_target_pairs={{0,12},{4,0},{8,4},{12,8},{1,13},{5,1},{9,5},{13,9},{2,14},{6,2},{... | collective-permute-start | bytes 294920 | tf_op jit(solution)/shard_map/ppermute | solution.py:415
  18.3 0.0 collective-permute-done.1.refs_2_
  18.3 0.0 collective-permute-done.2.refs_3_
  18.3 0.0 copy-done.3
  18.3 0.6 %shard_map.57 = (bf16[2,4,16,768]{3,2,1,0:T(8,128)(2,1)S(1)}, bf16[1,4,16,768]{3,2,1,0:T(8,128)(2,1)S(1)}, bf16[2,4,16,768]{3,2,1,0:T(8,128)(2,1)S(1)}, bf16[4,4,16,768]{3,2,1,0:T(8,128)(2,1)}) custom-call(s32[8]{0:T(128)S(1)} %get-tuple-element.32.picks_ref, bf16[4,16,768]{2,1,0:T(8,128)(2,1)S(1)} %copy-done.3, ...), custom_call_target="tpu_custom_call", output_to_operand_aliasing={{3}: (5, {})} | custom-call | flops 99999997952 | tf_op jit(solution)/shard_map/pallas_call | solution.py:153
  18.9 1.6 %collective-permute-start.4 = (bf16[1,4,16,768]{3,2,1,0:T(8,128)(2,1)S(1)}, bf16[1,4,16,768]{3,2,1,0:T(8,128)(2,1)S(1)}, u32[]{:S(2)}, u32[]{:S(2)}) collective-permute-start(bf16[1,4,16,768]{3,2,1,0:T(8,128)(2,1)S(1)} %get-tuple-element.40), channel_id=1, source_target_pairs={{0,2},{1,3},{2,0},{3,1},{4,6},{5,7},{6,4},{7,5},{8,10},{9,11},{10,... | collective-permute-start | bytes 294920 | tf_op jit(solution)/shard_map/ppermute | solution.py:415
  20.4 4.1 %all-to-all-start = ((bf16[4,4,16,768]{3,2,1,0:T(8,128)(2,1)}), bf16[4,4,16,768]{3,2,1,0:T(8,128)(2,1)S(1)}, u32[]{:S(2)}, u32[]{:S(2)}) async-start(bf16[4,4,16,768]{3,2,1,0:T(8,128)(2,1)} %get-tuple-element.38), calls=%async_computation | async-start | bytes 786432 | tf_op jit(solution)/shard_map/all_to_all | solution.py:448
  24.5 0.0 collective-permute-start.3
  24.6 0.0 collective-permute-done.9.refs_1_.refs_8_
  24.6 1.7 %collective-permute-start.5 = (bf16[2,4,16,768]{3,2,1,0:T(8,128)(2,1)S(1)}, bf16[2,4,16,768]{3,2,1,0:T(8,128)(2,1)S(1)}, u32[]{:S(2)}, u32[]{:S(2)}) collective-permute-start(bf16[2,4,16,768]{3,2,1,0:T(8,128)(2,1)S(1)} %get-tuple-element.41), channel_id=1, source_target_pairs={{0,3},{1,0},{2,1},{3,2},{4,7},{5,4},{6,5},{7,6},{8,11},{9,8},{10,9... | collective-permute-start | bytes 589832 | tf_op jit(solution)/shard_map/ppermute | solution.py:415
  26.3 0.0 collective-permute-done.10.refs_2_.refs_9_
  26.3 0.0 collective-permute-done.11.refs_3_.refs_10_
  26.3 0.0 collective-permute-done.4.refs_5_.refs_4_
  26.3 0.6 %shard_map.59 = (bf16[2,4,16,768]{3,2,1,0:T(8,128)(2,1)S(1)}, bf16[1,4,16,768]{3,2,1,0:T(8,128)(2,1)S(1)}, bf16[2,4,16,768]{3,2,1,0:T(8,128)(2,1)S(1)}) custom-call(s32[8]{0:T(128)S(1)} %get-tuple-element.32.picks_ref, bf16[4,16,768]{2,1,0:T(8,128)(2,1)S(1)} %get-tuple-element.45.refs_0_.refs_7_, ...), custom_call_target="tpu_custom_call" | custom-call | flops 99999997952 | tf_op jit(solution)/shard_map/pallas_call | solution.py:153
  26.9 0.6 %collective-permute-start.13 = (bf16[1,4,16,768]{3,2,1,0:T(8,128)(2,1)S(1)}, bf16[1,4,16,768]{3,2,1,0:T(8,128)(2,1)S(1)}, u32[]{:S(2)}, u32[]{:S(2)}) collective-permute-start(bf16[1,4,16,768]{3,2,1,0:T(8,128)(2,1)S(1)} %get-tuple-element.50), channel_id=1, source_target_pairs={{0,2},{1,3},{2,0},{3,1},{4,6},{5,7},{6,4},{7,5},{8,10},{9,11},{10,... | collective-permute-start | bytes 294920 | tf_op jit(solution)/shard_map/ppermute | solution.py:415
  27.5 0.0 collective-permute-start.12
  27.5 0.0 copy-start.6
  27.5 1.7 %collective-permute-start.14 = (bf16[2,4,16,768]{3,2,1,0:T(8,128)(2,1)S(1)}, bf16[2,4,16,768]{3,2,1,0:T(8,128)(2,1)S(1)}, u32[]{:S(2)}, u32[]{:S(2)}) collective-permute-start(bf16[2,4,16,768]{3,2,1,0:T(8,128)(2,1)S(1)} %get-tuple-element.51), channel_id=1, source_target_pairs={{0,3},{1,0},{2,1},{3,2},{4,7},{5,4},{6,5},{7,6},{8,11},{9,8},{10,9... | collective-permute-start | bytes 589832 | tf_op jit(solution)/shard_map/ppermute | solution.py:415
  29.3 1.7 %collective-permute-done.3.refs_4_ = bf16[2,4,16,768]{3,2,1,0:T(8,128)(2,1)S(1)} collective-permute-done((bf16[2,4,16,768]{3,2,1,0:T(8,128)(2,1)S(1)}, bf16[2,4,16,768]{3,2,1,0:T(8,128)(2,1)S(1)}, u32[]{:S(2)}, u32[]{:S(2)}) %collective-permute-start.3) | collective-permute-done | bytes 196640 | tf_op jit(solution)/shard_map/ppermute | solution.py:415
  30.9 0.7 %collective-permute-done.5.refs_6_ = bf16[2,4,16,768]{3,2,1,0:T(8,128)(2,1)S(1)} collective-permute-done((bf16[2,4,16,768]{3,2,1,0:T(8,128)(2,1)S(1)}, bf16[2,4,16,768]{3,2,1,0:T(8,128)(2,1)S(1)}, u32[]{:S(2)}, u32[]{:S(2)}) %collective-permute-start.5) | collective-permute-done | bytes 196640 | tf_op jit(solution)/shard_map/ppermute | solution.py:415
  31.7 2.6 %all-to-all-done.query_ref = bf16[4,4,16,768]{3,2,1,0:T(8,128)(2,1)S(1)} async-done(((bf16[4,4,16,768]{3,2,1,0:T(8,128)(2,1)}), bf16[4,4,16,768]{3,2,1,0:T(8,128)(2,1)S(1)}, u32[]{:S(2)}, u32[]{:S(2)}) %all-to-all-start) | async-done | bytes 393248 | tf_op jit(solution)/shard_map/all_to_all | solution.py:448
  34.2 0.0 copy-done.6
  34.2 1.5 %shard_map.58 = (bf16[4,16,384]{2,1,0:T(8,128)(2,1)S(1)}, bf16[4,16,384]{2,1,0:T(8,128)(2,1)S(1)}, bf16[4,16,384]{2,1,0:T(8,128)(2,1)S(1)}) custom-call(s32[16]{0:T(128)S(1)} %copy-done.6, f32[4,576]{1,0:T(4,128)S(1)} %get-tuple-element.31.bias_ref, bf16[4,4,16,768]{3,2,1,0:T(8,128)(2,1)S(1)} %all-to-all-done.query_ref, bf16[4,16,768]{2,1,0:T(8,128)(2,1)S(1)} %copy-done.3, ...), custom_call_target="tpu_custom_call" | custom-call | flops 99999997952 | tf_op jit(solution)/shard_map/pallas_call | solution.py:372
  35.7 0.4 collective-permute-start.7
  36.2 2.6 %collective-permute-start.8 = (bf16[4,16,384]{2,1,0:T(8,128)(2,1)S(1)}, bf16[4,16,384]{2,1,0:T(8,128)(2,1)S(1)}, u32[]{:S(2)}, u32[]{:S(2)}) collective-permute-start(bf16[4,16,384]{2,1,0:T(8,128)(2,1)S(1)} %get-tuple-element.44), channel_id=1, source_target_pairs={{0,4},{4,8},{8,12},{12,0},{1,5},{5,9},{9,13},{13,1},{2,6},{6,10},{... | collective-permute-start | bytes 147464 | tf_op jit(solution)/shard_map/ppermute | solution.py:415
  38.8 0.0 collective-permute-done.13.refs_5_.refs_12_
  38.8 1.2 %collective-permute-start.6 = (bf16[4,16,384]{2,1,0:T(8,128)(2,1)S(1)}, bf16[4,16,384]{2,1,0:T(8,128)(2,1)S(1)}, u32[]{:S(2)}, u32[]{:S(2)}) collective-permute-start(bf16[4,16,384]{2,1,0:T(8,128)(2,1)S(1)} %get-tuple-element.42.refs_7_), channel_id=1, source_target_pairs={{0,12},{4,0},{8,4},{12,8},{1,13},{5,1},{9,5},{13,9},{2,14},{6,2},{... | collective-permute-start | bytes 147464 | tf_op jit(solution)/shard_map/ppermute | solution.py:415
  40.0 0.0 collective-permute-done.12.refs_4_.refs_11_
  40.0 0.0 collective-permute-done.14.refs_6_.refs_13_
  40.0 1.5 %shard_map.60 = (bf16[4,16,384]{2,1,0:T(8,128)(2,1)S(1)}, bf16[4,16,384]{2,1,0:T(8,128)(2,1)S(1)}, bf16[4,16,384]{2,1,0:T(8,128)(2,1)S(1)}) custom-call(s32[16]{0:T(128)S(1)} %copy-done.6, f32[4,576]{1,0:T(4,128)S(1)} %get-tuple-element.31.bias_ref, bf16[4,4,16,768]{3,2,1,0:T(8,128)(2,1)S(1)} %all-to-all-done.query_ref, ...), custom_call_target="tpu_custom_call" | custom-call | tf_op jit(solution)/shard_map/pallas_call | solution.py:372
  41.5 0.8 %collective-permute-start.16 = (bf16[4,16,384]{2,1,0:T(8,128)(2,1)S(1)}, bf16[4,16,384]{2,1,0:T(8,128)(2,1)S(1)}, u32[]{:S(2)}, u32[]{:S(2)}) collective-permute-start(bf16[4,16,384]{2,1,0:T(8,128)(2,1)S(1)} %get-tuple-element.53), channel_id=1, source_target_pairs={{0,8},{4,12},{8,0},{12,4},{1,9},{5,13},{9,1},{13,5},{2,10},{6,14},... | collective-permute-start | bytes 147464 | tf_op jit(solution)/shard_map/ppermute | solution.py:415
  42.3 1.6 %collective-permute-start.17 = (bf16[4,16,384]{2,1,0:T(8,128)(2,1)S(1)}, bf16[4,16,384]{2,1,0:T(8,128)(2,1)S(1)}, u32[]{:S(2)}, u32[]{:S(2)}) collective-permute-start(bf16[4,16,384]{2,1,0:T(8,128)(2,1)S(1)} %get-tuple-element.54), channel_id=1, source_target_pairs={{0,4},{4,8},{8,12},{12,0},{1,5},{5,9},{9,13},{13,1},{2,6},{6,10},{... | collective-permute-start | bytes 147464 | tf_op jit(solution)/shard_map/ppermute | solution.py:415
  43.9 0.0 collective-permute-done.7.refs_1_
  44.0 2.2 %collective-permute-start.15 = (bf16[4,16,384]{2,1,0:T(8,128)(2,1)S(1)}, bf16[4,16,384]{2,1,0:T(8,128)(2,1)S(1)}, u32[]{:S(2)}, u32[]{:S(2)}) collective-permute-start(bf16[4,16,384]{2,1,0:T(8,128)(2,1)S(1)} %get-tuple-element.52.refs_14_), channel_id=1, source_target_pairs={{0,12},{4,0},{8,4},{12,8},{1,13},{5,1},{9,5},{13,9},{2,14},{6,2},{... | collective-permute-start | bytes 147464 | tf_op jit(solution)/shard_map/ppermute | solution.py:415
  46.1 1.4 %shard_map.61.refs_6_ = bf16[4,16,768]{2,1,0:T(8,128)(2,1)S(1)} custom-call(s32[16]{0:T(128)S(1)} %copy-done.6, f32[4,576]{1,0:T(4,128)S(1)} %get-tuple-element.31.bias_ref, bf16[4,4,16,768]{3,2,1,0:T(8,128)(2,1)S(1)} %all-to-all-done.query_ref, bf16[4,16,768]{2,1,0:T(8,128)(2,1)S(1)} %copy-done.3, bf16[4,16,768]{2,1,0:T(8,128)(2,1)S(1)} %collective-permute-done.refs_1_, ...), custom_call_target="tpu_custom_call" | custom-call | tf_op jit(solution)/shard_map/pallas_call | solution.py:372
  47.5 0.0 collective-permute-done.8.refs_2_
  47.5 0.0 collective-permute-done.6.refs_0_
  47.5 0.5 collective-permute-done.16.refs_4_
  48.0 0.4 collective-permute-done.17.refs_5_
  48.4 0.3 collective-permute-done.15.refs_3_
  48.7 0.8 %shard_map.62 = bf16[4,16,3072]{2,1,0:T(8,128)(2,1)} custom-call(bf16[4,16,384]{2,1,0:T(8,128)(2,1)S(1)} %collective-permute-done.6.refs_0_, bf16[4,16,384]{2,1,0:T(8,128)(2,1)S(1)} %collective-permute-done.7.refs_1_, bf16[4,16,384]{2,1,0:T(8,128)(2,1)S(1)} %collective-permute-done.8.refs_2_, bf16[4,16,384]{2,1,0:T(8,128)(2,1)S(1)} %collective-permute-done.15.refs_3_, ...), custom_call_target="tpu_custom_call" | custom-call | tf_op jit(solution)/shard_map/pallas_call | solution.py:403
Async XLA Ops:
  0.0 9.9 %copy-start.1 = (bf16[4,16,3072]{2,1,0:T(8,128)(2,1)S(1)}, bf16[4,16,3072]{2,1,0:T(8,128)(2,1)}, u32[]{:S(2)}) copy-start(bf16[4,16,3072]{2,1,0:T(8,128)(2,1)} %refs_2_.1) | copy-start | bytes 1179652
  0.0 9.9 %copy-start = (bf16[4,16,3072]{2,1,0:T(8,128)(2,1)S(1)}, bf16[4,16,3072]{2,1,0:T(8,128)(2,1)}, u32[]{:S(2)}) copy-start(bf16[4,16,3072]{2,1,0:T(8,128)(2,1)} %refs_1_.3) | copy-start | bytes 1179652
  2.9 7.0 %copy-start.7 = (f32[8,128]{1,0:T(8,128)S(1)}, f32[8,128]{1,0:T(8,128)}, u32[]{:S(2)}) copy-start(f32[8,128]{1,0:T(8,128)} %get-tuple-element.30.refs_5_) | copy-start | bytes 12292
  2.9 12.7 %collective-permute-start = (bf16[4,16,768]{2,1,0:T(8,128)(2,1)}, bf16[4,16,768]{2,1,0:T(8,128)(2,1)S(1)}, u32[]{:S(2)}, u32[]{:S(2)}) collective-permute-start(bf16[4,16,768]{2,1,0:T(8,128)(2,1)} %get-tuple-element.34), channel_id=1, source_target_pairs={{0,4},{4,8},{8,12},{12,0},{1,5},{5,9},{9,13},{13,1},{2,6},{6,10},{... | collective-permute-start | bytes 294920 | tf_op jit(solution)/shard_map/ppermute | solution.py:415
  6.0 12.3 %collective-permute-start.1 = (bf16[4,16,768]{2,1,0:T(8,128)(2,1)}, bf16[4,16,768]{2,1,0:T(8,128)(2,1)S(1)}, u32[]{:S(2)}, u32[]{:S(2)}) collective-permute-start(bf16[4,16,768]{2,1,0:T(8,128)(2,1)} %get-tuple-element.35), channel_id=1, source_target_pairs={{0,8},{4,12},{8,0},{12,4},{1,9},{5,13},{9,1},{13,5},{2,10},{6,14},... | collective-permute-start | bytes 294920 | tf_op jit(solution)/shard_map/ppermute | solution.py:415
  8.5 1.4 %copy-start.5 = (s32[16]{0:T(128)S(1)}, s32[16]{0:T(128)}, u32[]{:S(2)}) copy-start(s32[16]{0:T(128)} %tokens_ref.5) | copy-start | bytes 196
  8.5 9.7 %collective-permute-start.2 = (bf16[4,16,768]{2,1,0:T(8,128)(2,1)}, bf16[4,16,768]{2,1,0:T(8,128)(2,1)S(1)}, u32[]{:S(2)}, u32[]{:S(2)}) collective-permute-start(bf16[4,16,768]{2,1,0:T(8,128)(2,1)} %get-tuple-element.36), channel_id=1, source_target_pairs={{0,12},{4,0},{8,4},{12,8},{1,13},{5,1},{9,5},{13,9},{2,14},{6,2},{... | collective-permute-start | bytes 294920 | tf_op jit(solution)/shard_map/ppermute | solution.py:415
  9.9 1.0 %copy-start.2 = (bf16[4,16,3072]{2,1,0:T(8,128)(2,1)S(1)}, bf16[4,16,3072]{2,1,0:T(8,128)(2,1)}, u32[]{:S(2)}) copy-start(bf16[4,16,3072]{2,1,0:T(8,128)(2,1)} %refs_0_.3) | copy-start | bytes 1179652
  10.9 0.7 %copy-start.4 = (s32[16,32]{1,0:T(8,128)S(1)}, s32[16,32]{1,0:T(8,128)}, u32[]{:S(2)}) copy-start(s32[16,32]{1,0:T(8,128)} %refs_3_.1) | copy-start | bytes 6148
  11.6 6.7 %copy-start.3 = (bf16[4,16,768]{2,1,0:T(8,128)(2,1)S(1)}, bf16[4,16,768]{2,1,0:T(8,128)(2,1)}, u32[]{:S(2)}) copy-start(bf16[4,16,768]{2,1,0:T(8,128)(2,1)} %get-tuple-element.33.refs_0_) | copy-start | bytes 294916
  14.4 10.2 %collective-permute-start.9 = (bf16[4,16,768]{2,1,0:T(8,128)(2,1)S(1)}, bf16[4,16,768]{2,1,0:T(8,128)(2,1)S(1)}, u32[]{:S(2)}, u32[]{:S(2)}) collective-permute-start(bf16[4,16,768]{2,1,0:T(8,128)(2,1)S(1)} %get-tuple-element.46), channel_id=1, source_target_pairs={{0,4},{4,8},{8,12},{12,0},{1,5},{5,9},{9,13},{13,1},{2,6},{6,10},{... | collective-permute-start | bytes 294920 | tf_op jit(solution)/shard_map/ppermute | solution.py:415
  15.1 11.2 %collective-permute-start.10 = (bf16[4,16,768]{2,1,0:T(8,128)(2,1)S(1)}, bf16[4,16,768]{2,1,0:T(8,128)(2,1)S(1)}, u32[]{:S(2)}, u32[]{:S(2)}) collective-permute-start(bf16[4,16,768]{2,1,0:T(8,128)(2,1)S(1)} %get-tuple-element.47), channel_id=1, source_target_pairs={{0,8},{4,12},{8,0},{12,4},{1,9},{5,13},{9,1},{13,5},{2,10},{6,14},... | collective-permute-start | bytes 294920 | tf_op jit(solution)/shard_map/ppermute | solution.py:415
  15.6 10.7 %collective-permute-start.11 = (bf16[4,16,768]{2,1,0:T(8,128)(2,1)S(1)}, bf16[4,16,768]{2,1,0:T(8,128)(2,1)S(1)}, u32[]{:S(2)}, u32[]{:S(2)}) collective-permute-start(bf16[4,16,768]{2,1,0:T(8,128)(2,1)S(1)} %get-tuple-element.48), channel_id=1, source_target_pairs={{0,12},{4,0},{8,4},{12,8},{1,13},{5,1},{9,5},{13,9},{2,14},{6,2},{... | collective-permute-start | bytes 294920 | tf_op jit(solution)/shard_map/ppermute | solution.py:415
  18.9 7.4 %collective-permute-start.4 = (bf16[1,4,16,768]{3,2,1,0:T(8,128)(2,1)S(1)}, bf16[1,4,16,768]{3,2,1,0:T(8,128)(2,1)S(1)}, u32[]{:S(2)}, u32[]{:S(2)}) collective-permute-start(bf16[1,4,16,768]{3,2,1,0:T(8,128)(2,1)S(1)} %get-tuple-element.40), channel_id=1, source_target_pairs={{0,2},{1,3},{2,0},{3,1},{4,6},{5,7},{6,4},{7,5},{8,10},{9,11},{10,... | collective-permute-start | bytes 294920 | tf_op jit(solution)/shard_map/ppermute | solution.py:415
  20.4 13.8 %all-to-all-start = ((bf16[4,4,16,768]{3,2,1,0:T(8,128)(2,1)}), bf16[4,4,16,768]{3,2,1,0:T(8,128)(2,1)S(1)}, u32[]{:S(2)}, u32[]{:S(2)}) async-start(bf16[4,4,16,768]{3,2,1,0:T(8,128)(2,1)} %get-tuple-element.38), calls=%async_computation | async-start | bytes 786432 | tf_op jit(solution)/shard_map/all_to_all | solution.py:448
  24.5 6.4 %collective-permute-start.3 = (bf16[2,4,16,768]{3,2,1,0:T(8,128)(2,1)S(1)}, bf16[2,4,16,768]{3,2,1,0:T(8,128)(2,1)S(1)}, u32[]{:S(2)}, u32[]{:S(2)}) collective-permute-start(bf16[2,4,16,768]{3,2,1,0:T(8,128)(2,1)S(1)} %get-tuple-element.39), channel_id=1, source_target_pairs={{0,1},{1,2},{2,3},{3,0},{4,5},{5,6},{6,7},{7,4},{8,9},{9,10},{10,1... | collective-permute-start | bytes 589832 | tf_op jit(solution)/shard_map/ppermute | solution.py:415
  24.6 7.1 %collective-permute-start.5 = (bf16[2,4,16,768]{3,2,1,0:T(8,128)(2,1)S(1)}, bf16[2,4,16,768]{3,2,1,0:T(8,128)(2,1)S(1)}, u32[]{:S(2)}, u32[]{:S(2)}) collective-permute-start(bf16[2,4,16,768]{3,2,1,0:T(8,128)(2,1)S(1)} %get-tuple-element.41), channel_id=1, source_target_pairs={{0,3},{1,0},{2,1},{3,2},{4,7},{5,4},{6,5},{7,6},{8,11},{9,8},{10,9... | collective-permute-start | bytes 589832 | tf_op jit(solution)/shard_map/ppermute | solution.py:415
  26.9 11.9 %collective-permute-start.13 = (bf16[1,4,16,768]{3,2,1,0:T(8,128)(2,1)S(1)}, bf16[1,4,16,768]{3,2,1,0:T(8,128)(2,1)S(1)}, u32[]{:S(2)}, u32[]{:S(2)}) collective-permute-start(bf16[1,4,16,768]{3,2,1,0:T(8,128)(2,1)S(1)} %get-tuple-element.50), channel_id=1, source_target_pairs={{0,2},{1,3},{2,0},{3,1},{4,6},{5,7},{6,4},{7,5},{8,10},{9,11},{10,... | collective-permute-start | bytes 294920 | tf_op jit(solution)/shard_map/ppermute | solution.py:415
  27.5 12.5 %collective-permute-start.12 = (bf16[2,4,16,768]{3,2,1,0:T(8,128)(2,1)S(1)}, bf16[2,4,16,768]{3,2,1,0:T(8,128)(2,1)S(1)}, u32[]{:S(2)}, u32[]{:S(2)}) collective-permute-start(bf16[2,4,16,768]{3,2,1,0:T(8,128)(2,1)S(1)} %get-tuple-element.49), channel_id=1, source_target_pairs={{0,1},{1,2},{2,3},{3,0},{4,5},{5,6},{6,7},{7,4},{8,9},{9,10},{10,1... | collective-permute-start | bytes 589832 | tf_op jit(solution)/shard_map/ppermute | solution.py:415
  27.5 6.7 %copy-start.6 = (s32[16]{0:T(128)S(1)}, s32[16]{0:T(128)}, u32[]{:S(2)}) copy-start(s32[16]{0:T(128)} %tokens_ref.5) | copy-start | bytes 196
  27.5 12.5 %collective-permute-start.14 = (bf16[2,4,16,768]{3,2,1,0:T(8,128)(2,1)S(1)}, bf16[2,4,16,768]{3,2,1,0:T(8,128)(2,1)S(1)}, u32[]{:S(2)}, u32[]{:S(2)}) collective-permute-start(bf16[2,4,16,768]{3,2,1,0:T(8,128)(2,1)S(1)} %get-tuple-element.51), channel_id=1, source_target_pairs={{0,3},{1,0},{2,1},{3,2},{4,7},{5,4},{6,5},{7,6},{8,11},{9,8},{10,9... | collective-permute-start | bytes 589832 | tf_op jit(solution)/shard_map/ppermute | solution.py:415
  35.7 8.2 %collective-permute-start.7 = (bf16[4,16,384]{2,1,0:T(8,128)(2,1)S(1)}, bf16[4,16,384]{2,1,0:T(8,128)(2,1)S(1)}, u32[]{:S(2)}, u32[]{:S(2)}) collective-permute-start(bf16[4,16,384]{2,1,0:T(8,128)(2,1)S(1)} %get-tuple-element.43), channel_id=1, source_target_pairs={{0,8},{4,12},{8,0},{12,4},{1,9},{5,13},{9,1},{13,5},{2,10},{6,14},... | collective-permute-start | bytes 147464 | tf_op jit(solution)/shard_map/ppermute | solution.py:415
  36.2 11.4 %collective-permute-start.8 = (bf16[4,16,384]{2,1,0:T(8,128)(2,1)S(1)}, bf16[4,16,384]{2,1,0:T(8,128)(2,1)S(1)}, u32[]{:S(2)}, u32[]{:S(2)}) collective-permute-start(bf16[4,16,384]{2,1,0:T(8,128)(2,1)S(1)} %get-tuple-element.44), channel_id=1, source_target_pairs={{0,4},{4,8},{8,12},{12,0},{1,5},{5,9},{9,13},{13,1},{2,6},{6,10},{... | collective-permute-start | bytes 147464 | tf_op jit(solution)/shard_map/ppermute | solution.py:415
  38.8 8.8 %collective-permute-start.6 = (bf16[4,16,384]{2,1,0:T(8,128)(2,1)S(1)}, bf16[4,16,384]{2,1,0:T(8,128)(2,1)S(1)}, u32[]{:S(2)}, u32[]{:S(2)}) collective-permute-start(bf16[4,16,384]{2,1,0:T(8,128)(2,1)S(1)} %get-tuple-element.42.refs_7_), channel_id=1, source_target_pairs={{0,12},{4,0},{8,4},{12,8},{1,13},{5,1},{9,5},{13,9},{2,14},{6,2},{... | collective-permute-start | bytes 147464 | tf_op jit(solution)/shard_map/ppermute | solution.py:415
  41.5 6.5 %collective-permute-start.16 = (bf16[4,16,384]{2,1,0:T(8,128)(2,1)S(1)}, bf16[4,16,384]{2,1,0:T(8,128)(2,1)S(1)}, u32[]{:S(2)}, u32[]{:S(2)}) collective-permute-start(bf16[4,16,384]{2,1,0:T(8,128)(2,1)S(1)} %get-tuple-element.53), channel_id=1, source_target_pairs={{0,8},{4,12},{8,0},{12,4},{1,9},{5,13},{9,1},{13,5},{2,10},{6,14},... | collective-permute-start | bytes 147464 | tf_op jit(solution)/shard_map/ppermute | solution.py:415
  42.3 6.1 %collective-permute-start.17 = (bf16[4,16,384]{2,1,0:T(8,128)(2,1)S(1)}, bf16[4,16,384]{2,1,0:T(8,128)(2,1)S(1)}, u32[]{:S(2)}, u32[]{:S(2)}) collective-permute-start(bf16[4,16,384]{2,1,0:T(8,128)(2,1)S(1)} %get-tuple-element.54), channel_id=1, source_target_pairs={{0,4},{4,8},{8,12},{12,0},{1,5},{5,9},{9,13},{13,1},{2,6},{6,10},{... | collective-permute-start | bytes 147464 | tf_op jit(solution)/shard_map/ppermute | solution.py:415
  44.0 4.8 %collective-permute-start.15 = (bf16[4,16,384]{2,1,0:T(8,128)(2,1)S(1)}, bf16[4,16,384]{2,1,0:T(8,128)(2,1)S(1)}, u32[]{:S(2)}, u32[]{:S(2)}) collective-permute-start(bf16[4,16,384]{2,1,0:T(8,128)(2,1)S(1)} %get-tuple-element.52.refs_14_), channel_id=1, source_target_pairs={{0,12},{4,0},{8,4},{12,8},{1,13},{5,1},{9,5},{13,9},{2,14},{6,2},{... | collective-permute-start | bytes 147464 | tf_op jit(solution)/shard_map/ppermute | solution.py:415

commit v4 on v3

--- a/solution.py
+++ b/solution.py
@@ -444,7 +444,7 @@
         if not inputs:
             *picked, query = picked
         inputs.append((owns, forward(picked)))
-        held = inputs[-1][1][len(picked) // 2]
+        held = inputs[-1][1][0]
     query = lax.all_to_all(query, "head", split_axis=0, concat_axis=0, tiled=True)
     distances, after = list(range(1, count_head)), ()
     pieces, places = [], []

time: 49.8 us -> 53.4 us (1.072)
  waiting for transfers between devices: 6.17 us -> 9.91 us
    all_to_all x1, waiting for transfers between devices: 2.55 us -> 6.91 us  [shards(): lax.all_to_all(query, 'head', split_axis=0, concat_axis=0, tiled=True)]
    all_to_all x1, starting transfers between devices: 4.12 us -> 3.46 us  [shards(): lax.all_to_all(query, 'head', split_axis=0, concat_axis=0, tiled=True)]
    ppermute x18, waiting for transfers between devices: 3.62 us -> 3.01 us  [shifted(): lax.ppermute(array, axis, [(i, (i + distance) % count) for i in range(cou...]
  transfers between devices with their start and end apart: 19 -> 19, of which waited for: 6 -> 5; matrix products, arithmetic and copies ran while one was open for 0% -> 0% of each run, Pallas kernels for 17% -> 14%
where the time goes in v4:
time: 53.4 us; the launch traced here: 53.2 us
  starting transfers between devices  29.4 us (55%)
  Pallas kernels  11.9 us (22%)
  waiting for transfers between devices  9.91 us (19%)
  local copies, waits for them, and re-layouts  1.71 us (3%)
    ppermute x18, starting transfers between devices, shifted(): lax.ppermute(array, axis, [(i, (i + distance) % count) for i in range(cou...  26 us
    all_to_all x1, waiting for transfers between devices, shards(): lax.all_to_all(query, 'head', split_axis=0, concat_axis=0, tiled=True)  6.91 us
    pallas_call x3, Pallas kernels, attend(): pl.pallas_call(functools.partial(attend_kernel, (count_head, count_tm), h...  4.35 us
    all_to_all x1, starting transfers between devices, shards(): lax.all_to_all(query, 'head', split_axis=0, concat_axis=0, tiled=True)  3.46 us
    ppermute x18, waiting for transfers between devices, shifted(): lax.ppermute(array, axis, [(i, (i + distance) % count) for i in range(cou...  3.01 us
    pallas_call x1, Pallas kernels, rotate_pieces(): pl.pallas_call(functools.partial(rotate_kernel, message, sources, count_h...  2.86 us
    pallas_call x1, Pallas kernels, plan(): pl.pallas_call(functools.partial(plan_kernel, messages, count_head, count...  2.76 us
    unnamed x16, local copies, waits for them, and re-layouts  1.71 us
  transfers between devices with their start and end apart: 19, of which 5 were waited for; matrix products, arithmetic and copies ran while one was open for 0% of the time, Pallas kernels for 14%

profile of v4, /device:TPU:0, one launch (start us, length us, event | category | flops | bytes accessed | tf_op | source)
XLA Modules:
  0.0 53.2 jit_solution(4842732236902320129)
XLA Ops:
  0.0 0.0 copy-start.1
  0.0 0.0 copy-start
  0.0 2.9 %shard_map.55 = (bf16[4,16,768]{2,1,0:T(8,128)(2,1)}, bf16[4,16,768]{2,1,0:T(8,128)(2,1)}, bf16[4,16,768]{2,1,0:T(8,128)(2,1)}, bf16[4,16,768]{2,1,0:T(8,128)(2,1)}, f32[8,128]{1,0:T(8,128)}) custom-call(bf16[4,16,3072]{2,1,0:T(8,128)(2,1)} %refs_1_.3, bf16[4,16,3072]{2,1,0:T(8,128)(2,1)} %refs_2_.1), custom_call_target="tpu_custom_call" | custom-call | tf_op jit(solution)/shard_map/pallas_call | solution.py:114
  2.9 0.0 copy-start.7
  2.9 3.1 %collective-permute-start = (bf16[4,16,768]{2,1,0:T(8,128)(2,1)}, bf16[4,16,768]{2,1,0:T(8,128)(2,1)S(1)}, u32[]{:S(2)}, u32[]{:S(2)}) collective-permute-start(bf16[4,16,768]{2,1,0:T(8,128)(2,1)} %get-tuple-element.34), channel_id=1, source_target_pairs={{0,4},{4,8},{8,12},{12,0},{1,5},{5,9},{9,13},{13,1},{2,6},{6,10},{... | collective-permute-start | bytes 294920 | tf_op jit(solution)/shard_map/ppermute | solution.py:415
  6.0 2.6 %collective-permute-start.1 = (bf16[4,16,768]{2,1,0:T(8,128)(2,1)}, bf16[4,16,768]{2,1,0:T(8,128)(2,1)S(1)}, u32[]{:S(2)}, u32[]{:S(2)}) collective-permute-start(bf16[4,16,768]{2,1,0:T(8,128)(2,1)} %get-tuple-element.35), channel_id=1, source_target_pairs={{0,8},{4,12},{8,0},{12,4},{1,9},{5,13},{9,1},{13,5},{2,10},{6,14},... | collective-permute-start | bytes 294920 | tf_op jit(solution)/shard_map/ppermute | solution.py:415
  8.5 0.0 copy-start.5
  8.5 1.3 %collective-permute-start.2 = (bf16[4,16,768]{2,1,0:T(8,128)(2,1)}, bf16[4,16,768]{2,1,0:T(8,128)(2,1)S(1)}, u32[]{:S(2)}, u32[]{:S(2)}) collective-permute-start(bf16[4,16,768]{2,1,0:T(8,128)(2,1)} %get-tuple-element.36), channel_id=1, source_target_pairs={{0,12},{4,0},{8,4},{12,8},{1,13},{5,1},{9,5},{13,9},{2,14},{6,2},{... | collective-permute-start | bytes 294920 | tf_op jit(solution)/shard_map/ppermute | solution.py:415
  9.9 0.0 copy-done.1
  9.9 0.0 copy-done
  9.9 0.0 copy-done.7
  9.9 0.0 copy-done.5
  9.9 0.0 copy-start.2
  9.9 1.0 %copy-done.2 = bf16[4,16,3072]{2,1,0:T(8,128)(2,1)S(1)} copy-done((bf16[4,16,3072]{2,1,0:T(8,128)(2,1)S(1)}, bf16[4,16,3072]{2,1,0:T(8,128)(2,1)}, u32[]{:S(2)}) %copy-start.2) | copy-done | bytes 393240
  10.9 0.0 copy-start.4
  10.9 0.7 %copy-done.4 = s32[16,32]{1,0:T(8,128)S(1)} copy-done((s32[16,32]{1,0:T(8,128)S(1)}, s32[16,32]{1,0:T(8,128)}, u32[]{:S(2)}) %copy-start.4) | copy-done | bytes 2072
  11.6 0.0 copy-start.3
  11.6 2.8 %shard_map.56 = (s32[8]{0:T(128)S(1)}, f32[4,576]{1,0:T(4,128)S(1)}, bf16[4,4,16,768]{3,2,1,0:T(8,128)(2,1)}, bf16[4,16,768]{2,1,0:T(8,128)(2,1)S(1)}, bf16[4,16...) custom-call(bf16[4,16,3072]{2,1,0:T(8,128)(2,1)S(1)} %copy-done.2, ...), custom_call_target="tpu_custom_call" | custom-call | tf_op jit(solution)/shard_map/pallas_call | solution.py:281
  14.4 0.0 collective-permute-done.refs_1_
  14.4 1.0 %collective-permute-done.1.refs_2_ = bf16[4,16,768]{2,1,0:T(8,128)(2,1)S(1)} collective-permute-done((bf16[4,16,768]{2,1,0:T(8,128)(2,1)}, bf16[4,16,768]{2,1,0:T(8,128)(2,1)S(1)}, u32[]{:S(2)}, u32[]{:S(2)}) %collective-permute-start.1) | collective-permute-done | bytes 98336 | tf_op jit(solution)/shard_map/ppermute | solution.py:415
  15.3 0.0 collective-permute-done.2.refs_3_
  15.4 0.0 copy-done.3
  15.4 0.6 %shard_map.57 = (bf16[2,4,16,768]{3,2,1,0:T(8,128)(2,1)S(1)}, bf16[1,4,16,768]{3,2,1,0:T(8,128)(2,1)S(1)}, bf16[2,4,16,768]{3,2,1,0:T(8,128)(2,1)S(1)}, bf16[4,4,16,768]{3,2,1,0:T(8,128)(2,1)}) custom-call(s32[8]{0:T(128)S(1)} %get-tuple-element.32.picks_ref, bf16[4,16,768]{2,1,0:T(8,128)(2,1)S(1)} %copy-done.3, ...), custom_call_target="tpu_custom_call", output_to_operand_aliasing={{3}: (5, {})} | custom-call | flops 99999997952 | tf_op jit(solution)/shard_map/pallas_call | solution.py:153
  16.0 0.1 collective-permute-start.3
  16.0 2.6 %collective-permute-start.9 = (bf16[4,16,768]{2,1,0:T(8,128)(2,1)S(1)}, bf16[4,16,768]{2,1,0:T(8,128)(2,1)S(1)}, u32[]{:S(2)}, u32[]{:S(2)}) collective-permute-start(bf16[4,16,768]{2,1,0:T(8,128)(2,1)S(1)} %get-tuple-element.46), channel_id=1, source_target_pairs={{0,4},{4,8},{8,12},{12,0},{1,5},{5,9},{9,13},{13,1},{2,6},{6,10},{... | collective-permute-start | bytes 294920 | tf_op jit(solution)/shard_map/ppermute | solution.py:415
  18.6 1.6 %collective-permute-start.10 = (bf16[4,16,768]{2,1,0:T(8,128)(2,1)S(1)}, bf16[4,16,768]{2,1,0:T(8,128)(2,1)S(1)}, u32[]{:S(2)}, u32[]{:S(2)}) collective-permute-start(bf16[4,16,768]{2,1,0:T(8,128)(2,1)S(1)} %get-tuple-element.47), channel_id=1, source_target_pairs={{0,8},{4,12},{8,0},{12,4},{1,9},{5,13},{9,1},{13,5},{2,10},{6,14},... | collective-permute-start | bytes 294920 | tf_op jit(solution)/shard_map/ppermute | solution.py:415
  20.3 0.8 %collective-permute-start.11 = (bf16[4,16,768]{2,1,0:T(8,128)(2,1)S(1)}, bf16[4,16,768]{2,1,0:T(8,128)(2,1)S(1)}, u32[]{:S(2)}, u32[]{:S(2)}) collective-permute-start(bf16[4,16,768]{2,1,0:T(8,128)(2,1)S(1)} %get-tuple-element.48), channel_id=1, source_target_pairs={{0,12},{4,0},{8,4},{12,8},{1,13},{5,1},{9,5},{13,9},{2,14},{6,2},{... | collective-permute-start | bytes 294920 | tf_op jit(solution)/shard_map/ppermute | solution.py:415
  21.1 3.5 %all-to-all-start = ((bf16[4,4,16,768]{3,2,1,0:T(8,128)(2,1)}), bf16[4,4,16,768]{3,2,1,0:T(8,128)(2,1)S(1)}, u32[]{:S(2)}, u32[]{:S(2)}) async-start(bf16[4,4,16,768]{3,2,1,0:T(8,128)(2,1)} %get-tuple-element.38), calls=%async_computation | async-start | bytes 786432 | tf_op jit(solution)/shard_map/all_to_all | solution.py:448
  24.5 1.6 %collective-permute-start.4 = (bf16[1,4,16,768]{3,2,1,0:T(8,128)(2,1)S(1)}, bf16[1,4,16,768]{3,2,1,0:T(8,128)(2,1)S(1)}, u32[]{:S(2)}, u32[]{:S(2)}) collective-permute-start(bf16[1,4,16,768]{3,2,1,0:T(8,128)(2,1)S(1)} %get-tuple-element.40), channel_id=1, source_target_pairs={{0,2},{1,3},{2,0},{3,1},{4,6},{5,7},{6,4},{7,5},{8,10},{9,11},{10,... | collective-permute-start | bytes 294920 | tf_op jit(solution)/shard_map/ppermute | solution.py:415
  26.1 0.0 collective-permute-done.9.refs_1_.refs_8_
  26.1 0.8 %collective-permute-start.5 = (bf16[2,4,16,768]{3,2,1,0:T(8,128)(2,1)S(1)}, bf16[2,4,16,768]{3,2,1,0:T(8,128)(2,1)S(1)}, u32[]{:S(2)}, u32[]{:S(2)}) collective-permute-start(bf16[2,4,16,768]{3,2,1,0:T(8,128)(2,1)S(1)} %get-tuple-element.41), channel_id=1, source_target_pairs={{0,3},{1,0},{2,1},{3,2},{4,7},{5,4},{6,5},{7,6},{8,11},{9,8},{10,9... | collective-permute-start | bytes 589832 | tf_op jit(solution)/shard_map/ppermute | solution.py:415
  26.9 1.0 %collective-permute-done.10.refs_2_.refs_9_ = bf16[4,16,768]{2,1,0:T(8,128)(2,1)S(1)} collective-permute-done((bf16[4,16,768]{2,1,0:T(8,128)(2,1)S(1)}, bf16[4,16,768]{2,1,0:T(8,128)(2,1)S(1)}, u32[]{:S(2)}, u32[]{:S(2)}) %collective-permute-start.10) | collective-permute-done | bytes 98336 | tf_op jit(solution)/shard_map/ppermute | solution.py:415
  27.9 0.3 collective-permute-done.11.refs_3_.refs_10_
  28.1 0.0 collective-permute-done.3.refs_4_
  28.2 0.6 %shard_map.59 = (bf16[2,4,16,768]{3,2,1,0:T(8,128)(2,1)S(1)}, bf16[1,4,16,768]{3,2,1,0:T(8,128)(2,1)S(1)}, bf16[2,4,16,768]{3,2,1,0:T(8,128)(2,1)S(1)}) custom-call(s32[8]{0:T(128)S(1)} %get-tuple-element.32.picks_ref, bf16[4,16,768]{2,1,0:T(8,128)(2,1)S(1)} %get-tuple-element.45.refs_0_.refs_7_, ...), custom_call_target="tpu_custom_call" | custom-call | flops 99999997952 | tf_op jit(solution)/shard_map/pallas_call | solution.py:153
  28.7 0.9 %collective-permute-start.13 = (bf16[1,4,16,768]{3,2,1,0:T(8,128)(2,1)S(1)}, bf16[1,4,16,768]{3,2,1,0:T(8,128)(2,1)S(1)}, u32[]{:S(2)}, u32[]{:S(2)}) collective-permute-start(bf16[1,4,16,768]{3,2,1,0:T(8,128)(2,1)S(1)} %get-tuple-element.50), channel_id=1, source_target_pairs={{0,2},{1,3},{2,0},{3,1},{4,6},{5,7},{6,4},{7,5},{8,10},{9,11},{10,... | collective-permute-start | bytes 294920 | tf_op jit(solution)/shard_map/ppermute | solution.py:415
  29.7 0.0 collective-permute-start.12
  29.7 0.0 copy-start.6
  29.7 1.7 %collective-permute-start.14 = (bf16[2,4,16,768]{3,2,1,0:T(8,128)(2,1)S(1)}, bf16[2,4,16,768]{3,2,1,0:T(8,128)(2,1)S(1)}, u32[]{:S(2)}, u32[]{:S(2)}) collective-permute-start(bf16[2,4,16,768]{3,2,1,0:T(8,128)(2,1)S(1)} %get-tuple-element.51), channel_id=1, source_target_pairs={{0,3},{1,0},{2,1},{3,2},{4,7},{5,4},{6,5},{7,6},{8,11},{9,8},{10,9... | collective-permute-start | bytes 589832 | tf_op jit(solution)/shard_map/ppermute | solution.py:415
  31.4 0.0 collective-permute-done.4.refs_5_
  31.4 0.0 collective-permute-done.5.refs_6_
  31.4 6.9 %all-to-all-done.query_ref = bf16[4,4,16,768]{3,2,1,0:T(8,128)(2,1)S(1)} async-done(((bf16[4,4,16,768]{3,2,1,0:T(8,128)(2,1)}), bf16[4,4,16,768]{3,2,1,0:T(8,128)(2,1)S(1)}, u32[]{:S(2)}, u32[]{:S(2)}) %all-to-all-start) | async-done | bytes 393248 | tf_op jit(solution)/shard_map/all_to_all | solution.py:448
  38.3 0.0 copy-done.6
  38.3 1.5 %shard_map.58 = (bf16[4,16,384]{2,1,0:T(8,128)(2,1)S(1)}, bf16[4,16,384]{2,1,0:T(8,128)(2,1)S(1)}, bf16[4,16,384]{2,1,0:T(8,128)(2,1)S(1)}) custom-call(s32[16]{0:T(128)S(1)} %copy-done.6, f32[4,576]{1,0:T(4,128)S(1)} %get-tuple-element.31.bias_ref, bf16[4,4,16,768]{3,2,1,0:T(8,128)(2,1)S(1)} %all-to-all-done.query_ref, bf16[4,16,768]{2,1,0:T(8,128)(2,1)S(1)} %copy-done.3, ...), custom_call_target="tpu_custom_call" | custom-call | flops 99999997952 | tf_op jit(solution)/shard_map/pallas_call | solution.py:372
  39.8 0.1 collective-permute-start.7
  39.9 1.4 %collective-permute-start.8 = (bf16[4,16,384]{2,1,0:T(8,128)(2,1)S(1)}, bf16[4,16,384]{2,1,0:T(8,128)(2,1)S(1)}, u32[]{:S(2)}, u32[]{:S(2)}) collective-permute-start(bf16[4,16,384]{2,1,0:T(8,128)(2,1)S(1)} %get-tuple-element.44), channel_id=1, source_target_pairs={{0,4},{4,8},{8,12},{12,0},{1,5},{5,9},{9,13},{13,1},{2,6},{6,10},{... | collective-permute-start | bytes 147464 | tf_op jit(solution)/shard_map/ppermute | solution.py:415
  41.3 0.0 collective-permute-done.13.refs_5_.refs_12_
  41.3 2.5 %collective-permute-start.6 = (bf16[4,16,384]{2,1,0:T(8,128)(2,1)S(1)}, bf16[4,16,384]{2,1,0:T(8,128)(2,1)S(1)}, u32[]{:S(2)}, u32[]{:S(2)}) collective-permute-start(bf16[4,16,384]{2,1,0:T(8,128)(2,1)S(1)} %get-tuple-element.42.refs_7_), channel_id=1, source_target_pairs={{0,12},{4,0},{8,4},{12,8},{1,13},{5,1},{9,5},{13,9},{2,14},{6,2},{... | collective-permute-start | bytes 147464 | tf_op jit(solution)/shard_map/ppermute | solution.py:415
  43.8 0.0 collective-permute-done.12.refs_4_.refs_11_
  43.8 0.0 collective-permute-done.14.refs_6_.refs_13_
  43.8 1.5 %shard_map.60 = (bf16[4,16,384]{2,1,0:T(8,128)(2,1)S(1)}, bf16[4,16,384]{2,1,0:T(8,128)(2,1)S(1)}, bf16[4,16,384]{2,1,0:T(8,128)(2,1)S(1)}) custom-call(s32[16]{0:T(128)S(1)} %copy-done.6, f32[4,576]{1,0:T(4,128)S(1)} %get-tuple-element.31.bias_ref, bf16[4,4,16,768]{3,2,1,0:T(8,128)(2,1)S(1)} %all-to-all-done.query_ref, ...), custom_call_target="tpu_custom_call" | custom-call | tf_op jit(solution)/shard_map/pallas_call | solution.py:372
  45.3 1.1 %collective-permute-start.16 = (bf16[4,16,384]{2,1,0:T(8,128)(2,1)S(1)}, bf16[4,16,384]{2,1,0:T(8,128)(2,1)S(1)}, u32[]{:S(2)}, u32[]{:S(2)}) collective-permute-start(bf16[4,16,384]{2,1,0:T(8,128)(2,1)S(1)} %get-tuple-element.53), channel_id=1, source_target_pairs={{0,8},{4,12},{8,0},{12,4},{1,9},{5,13},{9,1},{13,5},{2,10},{6,14},... | collective-permute-start | bytes 147464 | tf_op jit(solution)/shard_map/ppermute | solution.py:415
  46.4 0.0 collective-permute-start.17
  46.4 0.0 collective-permute-done.7.refs_1_
  46.4 3.8 %collective-permute-start.15 = (bf16[4,16,384]{2,1,0:T(8,128)(2,1)S(1)}, bf16[4,16,384]{2,1,0:T(8,128)(2,1)S(1)}, u32[]{:S(2)}, u32[]{:S(2)}) collective-permute-start(bf16[4,16,384]{2,1,0:T(8,128)(2,1)S(1)} %get-tuple-element.52.refs_14_), channel_id=1, source_target_pairs={{0,12},{4,0},{8,4},{12,8},{1,13},{5,1},{9,5},{13,9},{2,14},{6,2},{... | collective-permute-start | bytes 147464 | tf_op jit(solution)/shard_map/ppermute | solution.py:415
  50.2 1.4 %shard_map.61.refs_6_ = bf16[4,16,768]{2,1,0:T(8,128)(2,1)S(1)} custom-call(s32[16]{0:T(128)S(1)} %copy-done.6, f32[4,576]{1,0:T(4,128)S(1)} %get-tuple-element.31.bias_ref, bf16[4,4,16,768]{3,2,1,0:T(8,128)(2,1)S(1)} %all-to-all-done.query_ref, bf16[4,16,768]{2,1,0:T(8,128)(2,1)S(1)} %copy-done.3, bf16[4,16,768]{2,1,0:T(8,128)(2,1)S(1)} %collective-permute-done.refs_1_, ...), custom_call_target="tpu_custom_call" | custom-call | tf_op jit(solution)/shard_map/pallas_call | solution.py:372
  51.6 0.0 collective-permute-done.8.refs_2_
  51.6 0.0 collective-permute-done.6.refs_0_
  51.7 0.0 collective-permute-done.16.refs_4_
  51.7 0.7 %collective-permute-done.17.refs_5_ = bf16[4,16,384]{2,1,0:T(8,128)(2,1)S(1)} collective-permute-done((bf16[4,16,384]{2,1,0:T(8,128)(2,1)S(1)}, bf16[4,16,384]{2,1,0:T(8,128)(2,1)S(1)}, u32[]{:S(2)}, u32[]{:S(2)}) %collective-permute-start.17) | collective-permute-done | bytes 49184 | tf_op jit(solution)/shard_map/ppermute | solution.py:415
  52.4 0.0 collective-permute-done.15.refs_3_
  52.4 0.8 %shard_map.62 = bf16[4,16,3072]{2,1,0:T(8,128)(2,1)} custom-call(bf16[4,16,384]{2,1,0:T(8,128)(2,1)S(1)} %collective-permute-done.6.refs_0_, bf16[4,16,384]{2,1,0:T(8,128)(2,1)S(1)} %collective-permute-done.7.refs_1_, bf16[4,16,384]{2,1,0:T(8,128)(2,1)S(1)} %collective-permute-done.8.refs_2_, bf16[4,16,384]{2,1,0:T(8,128)(2,1)S(1)} %collective-permute-done.15.refs_3_, ...), custom_call_target="tpu_custom_call" | custom-call | tf_op jit(solution)/shard_map/pallas_call | solution.py:403
Async XLA Ops:
  0.0 9.9 %copy-start.1 = (bf16[4,16,3072]{2,1,0:T(8,128)(2,1)S(1)}, bf16[4,16,3072]{2,1,0:T(8,128)(2,1)}, u32[]{:S(2)}) copy-start(bf16[4,16,3072]{2,1,0:T(8,128)(2,1)} %refs_2_.1) | copy-start | bytes 1179652
  0.0 9.9 %copy-start = (bf16[4,16,3072]{2,1,0:T(8,128)(2,1)S(1)}, bf16[4,16,3072]{2,1,0:T(8,128)(2,1)}, u32[]{:S(2)}) copy-start(bf16[4,16,3072]{2,1,0:T(8,128)(2,1)} %refs_1_.3) | copy-start | bytes 1179652
  2.9 7.0 %copy-start.7 = (f32[8,128]{1,0:T(8,128)S(1)}, f32[8,128]{1,0:T(8,128)}, u32[]{:S(2)}) copy-start(f32[8,128]{1,0:T(8,128)} %get-tuple-element.30.refs_5_) | copy-start | bytes 12292
  2.9 11.5 %collective-permute-start = (bf16[4,16,768]{2,1,0:T(8,128)(2,1)}, bf16[4,16,768]{2,1,0:T(8,128)(2,1)S(1)}, u32[]{:S(2)}, u32[]{:S(2)}) collective-permute-start(bf16[4,16,768]{2,1,0:T(8,128)(2,1)} %get-tuple-element.34), channel_id=1, source_target_pairs={{0,4},{4,8},{8,12},{12,0},{1,5},{5,9},{9,13},{13,1},{2,6},{6,10},{... | collective-permute-start | bytes 294920 | tf_op jit(solution)/shard_map/ppermute | solution.py:415
  6.0 9.4 %collective-permute-start.1 = (bf16[4,16,768]{2,1,0:T(8,128)(2,1)}, bf16[4,16,768]{2,1,0:T(8,128)(2,1)S(1)}, u32[]{:S(2)}, u32[]{:S(2)}) collective-permute-start(bf16[4,16,768]{2,1,0:T(8,128)(2,1)} %get-tuple-element.35), channel_id=1, source_target_pairs={{0,8},{4,12},{8,0},{12,4},{1,9},{5,13},{9,1},{13,5},{2,10},{6,14},... | collective-permute-start | bytes 294920 | tf_op jit(solution)/shard_map/ppermute | solution.py:415
  8.5 1.4 %copy-start.5 = (s32[16]{0:T(128)S(1)}, s32[16]{0:T(128)}, u32[]{:S(2)}) copy-start(s32[16]{0:T(128)} %tokens_ref.5) | copy-start | bytes 196
  8.5 6.8 %collective-permute-start.2 = (bf16[4,16,768]{2,1,0:T(8,128)(2,1)}, bf16[4,16,768]{2,1,0:T(8,128)(2,1)S(1)}, u32[]{:S(2)}, u32[]{:S(2)}) collective-permute-start(bf16[4,16,768]{2,1,0:T(8,128)(2,1)} %get-tuple-element.36), channel_id=1, source_target_pairs={{0,12},{4,0},{8,4},{12,8},{1,13},{5,1},{9,5},{13,9},{2,14},{6,2},{... | collective-permute-start | bytes 294920 | tf_op jit(solution)/shard_map/ppermute | solution.py:415
  9.9 1.0 %copy-start.2 = (bf16[4,16,3072]{2,1,0:T(8,128)(2,1)S(1)}, bf16[4,16,3072]{2,1,0:T(8,128)(2,1)}, u32[]{:S(2)}) copy-start(bf16[4,16,3072]{2,1,0:T(8,128)(2,1)} %refs_0_.3) | copy-start | bytes 1179652
  10.9 0.7 %copy-start.4 = (s32[16,32]{1,0:T(8,128)S(1)}, s32[16,32]{1,0:T(8,128)}, u32[]{:S(2)}) copy-start(s32[16,32]{1,0:T(8,128)} %refs_3_.1) | copy-start | bytes 6148
  11.6 3.8 %copy-start.3 = (bf16[4,16,768]{2,1,0:T(8,128)(2,1)S(1)}, bf16[4,16,768]{2,1,0:T(8,128)(2,1)}, u32[]{:S(2)}) copy-start(bf16[4,16,768]{2,1,0:T(8,128)(2,1)} %get-tuple-element.33.refs_0_) | copy-start | bytes 294916
  16.0 12.2 %collective-permute-start.3 = (bf16[2,4,16,768]{3,2,1,0:T(8,128)(2,1)S(1)}, bf16[2,4,16,768]{3,2,1,0:T(8,128)(2,1)S(1)}, u32[]{:S(2)}, u32[]{:S(2)}) collective-permute-start(bf16[2,4,16,768]{3,2,1,0:T(8,128)(2,1)S(1)} %get-tuple-element.39), channel_id=1, source_target_pairs={{0,1},{1,2},{2,3},{3,0},{4,5},{5,6},{6,7},{7,4},{8,9},{9,10},{10,1... | collective-permute-start | bytes 589832 | tf_op jit(solution)/shard_map/ppermute | solution.py:415
  16.0 10.1 %collective-permute-start.9 = (bf16[4,16,768]{2,1,0:T(8,128)(2,1)S(1)}, bf16[4,16,768]{2,1,0:T(8,128)(2,1)S(1)}, u32[]{:S(2)}, u32[]{:S(2)}) collective-permute-start(bf16[4,16,768]{2,1,0:T(8,128)(2,1)S(1)} %get-tuple-element.46), channel_id=1, source_target_pairs={{0,4},{4,8},{8,12},{12,0},{1,5},{5,9},{9,13},{13,1},{2,6},{6,10},{... | collective-permute-start | bytes 294920 | tf_op jit(solution)/shard_map/ppermute | solution.py:415
  18.6 9.2 %collective-permute-start.10 = (bf16[4,16,768]{2,1,0:T(8,128)(2,1)S(1)}, bf16[4,16,768]{2,1,0:T(8,128)(2,1)S(1)}, u32[]{:S(2)}, u32[]{:S(2)}) collective-permute-start(bf16[4,16,768]{2,1,0:T(8,128)(2,1)S(1)} %get-tuple-element.47), channel_id=1, source_target_pairs={{0,8},{4,12},{8,0},{12,4},{1,9},{5,13},{9,1},{13,5},{2,10},{6,14},... | collective-permute-start | bytes 294920 | tf_op jit(solution)/shard_map/ppermute | solution.py:415
  20.3 7.9 %collective-permute-start.11 = (bf16[4,16,768]{2,1,0:T(8,128)(2,1)S(1)}, bf16[4,16,768]{2,1,0:T(8,128)(2,1)S(1)}, u32[]{:S(2)}, u32[]{:S(2)}) collective-permute-start(bf16[4,16,768]{2,1,0:T(8,128)(2,1)S(1)} %get-tuple-element.48), channel_id=1, source_target_pairs={{0,12},{4,0},{8,4},{12,8},{1,13},{5,1},{9,5},{13,9},{2,14},{6,2},{... | collective-permute-start | bytes 294920 | tf_op jit(solution)/shard_map/ppermute | solution.py:415
  21.1 17.3 %all-to-all-start = ((bf16[4,4,16,768]{3,2,1,0:T(8,128)(2,1)}), bf16[4,4,16,768]{3,2,1,0:T(8,128)(2,1)S(1)}, u32[]{:S(2)}, u32[]{:S(2)}) async-start(bf16[4,4,16,768]{3,2,1,0:T(8,128)(2,1)} %get-tuple-element.38), calls=%async_computation | async-start | bytes 786432 | tf_op jit(solution)/shard_map/all_to_all | solution.py:448
  24.5 6.9 %collective-permute-start.4 = (bf16[1,4,16,768]{3,2,1,0:T(8,128)(2,1)S(1)}, bf16[1,4,16,768]{3,2,1,0:T(8,128)(2,1)S(1)}, u32[]{:S(2)}, u32[]{:S(2)}) collective-permute-start(bf16[1,4,16,768]{3,2,1,0:T(8,128)(2,1)S(1)} %get-tuple-element.40), channel_id=1, source_target_pairs={{0,2},{1,3},{2,0},{3,1},{4,6},{5,7},{6,4},{7,5},{8,10},{9,11},{10,... | collective-permute-start | bytes 294920 | tf_op jit(solution)/shard_map/ppermute | solution.py:415
  26.1 5.3 %collective-permute-start.5 = (bf16[2,4,16,768]{3,2,1,0:T(8,128)(2,1)S(1)}, bf16[2,4,16,768]{3,2,1,0:T(8,128)(2,1)S(1)}, u32[]{:S(2)}, u32[]{:S(2)}) collective-permute-start(bf16[2,4,16,768]{3,2,1,0:T(8,128)(2,1)S(1)} %get-tuple-element.41), channel_id=1, source_target_pairs={{0,3},{1,0},{2,1},{3,2},{4,7},{5,4},{6,5},{7,6},{8,11},{9,8},{10,9... | collective-permute-start | bytes 589832 | tf_op jit(solution)/shard_map/ppermute | solution.py:415
  28.7 12.5 %collective-permute-start.13 = (bf16[1,4,16,768]{3,2,1,0:T(8,128)(2,1)S(1)}, bf16[1,4,16,768]{3,2,1,0:T(8,128)(2,1)S(1)}, u32[]{:S(2)}, u32[]{:S(2)}) collective-permute-start(bf16[1,4,16,768]{3,2,1,0:T(8,128)(2,1)S(1)} %get-tuple-element.50), channel_id=1, source_target_pairs={{0,2},{1,3},{2,0},{3,1},{4,6},{5,7},{6,4},{7,5},{8,10},{9,11},{10,... | collective-permute-start | bytes 294920 | tf_op jit(solution)/shard_map/ppermute | solution.py:415
  29.7 14.1 %collective-permute-start.12 = (bf16[2,4,16,768]{3,2,1,0:T(8,128)(2,1)S(1)}, bf16[2,4,16,768]{3,2,1,0:T(8,128)(2,1)S(1)}, u32[]{:S(2)}, u32[]{:S(2)}) collective-permute-start(bf16[2,4,16,768]{3,2,1,0:T(8,128)(2,1)S(1)} %get-tuple-element.49), channel_id=1, source_target_pairs={{0,1},{1,2},{2,3},{3,0},{4,5},{5,6},{6,7},{7,4},{8,9},{9,10},{10,1... | collective-permute-start | bytes 589832 | tf_op jit(solution)/shard_map/ppermute | solution.py:415
  29.7 8.7 %copy-start.6 = (s32[16]{0:T(128)S(1)}, s32[16]{0:T(128)}, u32[]{:S(2)}) copy-start(s32[16]{0:T(128)} %tokens_ref.5) | copy-start | bytes 196
  29.7 14.1 %collective-permute-start.14 = (bf16[2,4,16,768]{3,2,1,0:T(8,128)(2,1)S(1)}, bf16[2,4,16,768]{3,2,1,0:T(8,128)(2,1)S(1)}, u32[]{:S(2)}, u32[]{:S(2)}) collective-permute-start(bf16[2,4,16,768]{3,2,1,0:T(8,128)(2,1)S(1)} %get-tuple-element.51), channel_id=1, source_target_pairs={{0,3},{1,0},{2,1},{3,2},{4,7},{5,4},{6,5},{7,6},{8,11},{9,8},{10,9... | collective-permute-start | bytes 589832 | tf_op jit(solution)/shard_map/ppermute | solution.py:415
  39.8 6.6 %collective-permute-start.7 = (bf16[4,16,384]{2,1,0:T(8,128)(2,1)S(1)}, bf16[4,16,384]{2,1,0:T(8,128)(2,1)S(1)}, u32[]{:S(2)}, u32[]{:S(2)}) collective-permute-start(bf16[4,16,384]{2,1,0:T(8,128)(2,1)S(1)} %get-tuple-element.43), channel_id=1, source_target_pairs={{0,8},{4,12},{8,0},{12,4},{1,9},{5,13},{9,1},{13,5},{2,10},{6,14},... | collective-permute-start | bytes 147464 | tf_op jit(solution)/shard_map/ppermute | solution.py:415
  39.9 11.7 %collective-permute-start.8 = (bf16[4,16,384]{2,1,0:T(8,128)(2,1)S(1)}, bf16[4,16,384]{2,1,0:T(8,128)(2,1)S(1)}, u32[]{:S(2)}, u32[]{:S(2)}) collective-permute-start(bf16[4,16,384]{2,1,0:T(8,128)(2,1)S(1)} %get-tuple-element.44), channel_id=1, source_target_pairs={{0,4},{4,8},{8,12},{12,0},{1,5},{5,9},{9,13},{13,1},{2,6},{6,10},{... | collective-permute-start | bytes 147464 | tf_op jit(solution)/shard_map/ppermute | solution.py:415
  41.3 10.4 %collective-permute-start.6 = (bf16[4,16,384]{2,1,0:T(8,128)(2,1)S(1)}, bf16[4,16,384]{2,1,0:T(8,128)(2,1)S(1)}, u32[]{:S(2)}, u32[]{:S(2)}) collective-permute-start(bf16[4,16,384]{2,1,0:T(8,128)(2,1)S(1)} %get-tuple-element.42.refs_7_), channel_id=1, source_target_pairs={{0,12},{4,0},{8,4},{12,8},{1,13},{5,1},{9,5},{13,9},{2,14},{6,2},{... | collective-permute-start | bytes 147464 | tf_op jit(solution)/shard_map/ppermute | solution.py:415
  45.3 6.4 %collective-permute-start.16 = (bf16[4,16,384]{2,1,0:T(8,128)(2,1)S(1)}, bf16[4,16,384]{2,1,0:T(8,128)(2,1)S(1)}, u32[]{:S(2)}, u32[]{:S(2)}) collective-permute-start(bf16[4,16,384]{2,1,0:T(8,128)(2,1)S(1)} %get-tuple-element.53), channel_id=1, source_target_pairs={{0,8},{4,12},{8,0},{12,4},{1,9},{5,13},{9,1},{13,5},{2,10},{6,14},... | collective-permute-start | bytes 147464 | tf_op jit(solution)/shard_map/ppermute | solution.py:415
  46.4 5.9 %collective-permute-start.17 = (bf16[4,16,384]{2,1,0:T(8,128)(2,1)S(1)}, bf16[4,16,384]{2,1,0:T(8,128)(2,1)S(1)}, u32[]{:S(2)}, u32[]{:S(2)}) collective-permute-start(bf16[4,16,384]{2,1,0:T(8,128)(2,1)S(1)} %get-tuple-element.54), channel_id=1, source_target_pairs={{0,4},{4,8},{8,12},{12,0},{1,5},{5,9},{9,13},{13,1},{2,6},{6,10},{... | collective-permute-start | bytes 147464 | tf_op jit(solution)/shard_map/ppermute | solution.py:415
  46.4 5.9 %collective-permute-start.15 = (bf16[4,16,384]{2,1,0:T(8,128)(2,1)S(1)}, bf16[4,16,384]{2,1,0:T(8,128)(2,1)S(1)}, u32[]{:S(2)}, u32[]{:S(2)}) collective-permute-start(bf16[4,16,384]{2,1,0:T(8,128)(2,1)S(1)} %get-tuple-element.52.refs_14_), channel_id=1, source_target_pairs={{0,12},{4,0},{8,4},{12,8},{1,13},{5,1},{9,5},{13,9},{2,14},{6,2},{... | collective-permute-start | bytes 147464 | tf_op jit(solution)/shard_map/ppermute | solution.py:415
